TPU v7x, 32 devices: a whole 2x2x4 slice. The times are simulated.
32 devices in a mesh: dp: 16 (over z, y, core), mp: 2 (over x).
Axes of the slice: x: 2, y: 2, z: 4, core: 2. Of those that a mesh axis runs over, the one named last changes fastest.
Arguments:
- inputs: bfloat16 [65536, 1024], P(('dp', 'mp')), may hold values from -6 to 6
- skip_in: bfloat16 [65536, 1024], P(('dp', 'mp')), may hold values from -6 to 6
- cotangent: bfloat16 [65536, 1024], P(('dp', 'mp')), may hold values from -6 to 6
- lengths: int32 [16, 8], P('dp'), may hold values from 1 to 3840, as said below
- w_concat: bfloat16 [2048, 1024], replicated, may hold values from -0.125 to 0.125
- b_concat: float32 [1024], replicated, may hold values from -2 to 2
- gain_attn: float32 [1024], replicated, may hold values from 0.5 to 1.5
- w_query: bfloat16 [1024, 1024], P(None, 'mp'), may hold values from -0.1875 to 0.1875
- w_key: bfloat16 [1024, 1024], P(None, 'mp'), may hold values from -0.1875 to 0.1875
- w_value: bfloat16 [1024, 1024], P(None, 'mp'), may hold values from -0.1875 to 0.1875
- w_out: bfloat16 [1024, 1024], P('mp'), may hold values from -4 to 4
- b_out: float32 [1024], replicated, may hold values from -2 to 2
- gain_ffn: float32 [1024], replicated, may hold values from 0.5 to 1.5
- w_up: bfloat16 [1024, 4096], P(None, 'mp'), may hold values from -0.1875 to 0.1875
- b_up: bfloat16 [4096], P('mp'), may hold values from -3 to 3
- w_down: bfloat16 [4096, 1024], P('mp'), may hold values from -0.09375 to 0.09375
- b_down: float32 [1024], replicated, may hold values from -2 to 2
Outputs:
- output: float32 [65536, 1024], P(('dp', 'mp'))
- grad_inputs: float32 [65536, 1024], P(('dp', 'mp'))
- grad_skip: float32 [65536, 1024], P(('dp', 'mp'))
- grad_w_concat: float32 [2048, 1024], replicated
- grad_b_concat: float32 [1024], replicated
- grad_gain_attn: float32 [1024], replicated
- grad_w_query: float32 [1024, 1024], P(None, 'mp')
- grad_w_key: float32 [1024, 1024], P(None, 'mp')
- grad_w_value: float32 [1024, 1024], P(None, 'mp')
- grad_w_out: float32 [1024, 1024], P('mp')
- grad_b_out: float32 [1024], replicated
- grad_gain_ffn: float32 [1024], replicated
- grad_w_up: float32 [1024, 4096], P(None, 'mp')
- grad_b_up: float32 [4096], P('mp')
- grad_w_down: float32 [4096, 1024], P('mp')
- grad_b_down: float32 [1024], replicated
Inputs may be any that keep to these rules, and one draw needn't show every extreme that they name: `lengths`: row g holds group g's utterances, laid end to end from the group's first row; they sum to at most 4096, each is 1 or more, and the first is at least 3712 long.
All inputs are finite; a program needn't handle non-finite values.
Results may differ from a plain program's by a relative error of at most 0.02.
Values may be sent and summed in bfloat16 or wider, within the bound.
A program may use at most 576 MiB of HBM per device.

v0:
```python
import jax
import jax.numpy as jnp
from jax import lax
from jax.sharding import PartitionSpec as P

HEAD_DIM = 64


EPS = 1e-06


def layout(lengths_row, count):
    ends = jnp.cumsum(lengths_row)
    starts = ends - lengths_row
    places = jnp.arange(count, dtype=jnp.int32)
    seg = jnp.sum((places[:, None] >= ends[None, :]).astype(jnp.int32), axis=1)
    owner = seg[:, None] == jnp.arange(lengths_row.shape[0], dtype=jnp.int32)[None, :]
    start_of = jnp.sum(jnp.where(owner, starts[None, :], 0), axis=1)
    pos = (places - start_of).astype(jnp.float32)
    valid = (places < ends[-1]).astype(jnp.float32)
    return (seg, pos, valid)


def tables(pos):
    half = HEAD_DIM // 2
    freq = jnp.exp(-jnp.log(10000.0) * jnp.arange(half, dtype=jnp.float32) * 2.0 / HEAD_DIM)
    angle = pos[:, None] * freq[None, :]
    return (jnp.cos(angle), jnp.sin(angle))


def rotate(x, cosine, sine, back):
    count = x.shape[0]
    shaped = x.reshape(count, -1, HEAD_DIM)
    half = HEAD_DIM // 2
    first, second = (shaped[..., :half], shaped[..., half:])
    cc, ss = (cosine[:, None, :], sine[:, None, :])
    if back:
        joined = [first * cc + second * ss, second * cc - first * ss]
    else:
        joined = [first * cc - second * ss, second * cc + first * ss]
    return jnp.concatenate(joined, -1).reshape(count, -1)


def dot_tn(left, right):
    return lax.dot_general(
        left, right, (((0,), (0,)), ((), ())), preferred_element_type=jnp.float32
    )


def dot_nt(left, right):
    return lax.dot_general(
        left, right, (((1,), (1,)), ((), ())), preferred_element_type=jnp.float32
    )


def gelu_exact(v):
    return jax.nn.gelu(v, approximate=False)


def norm_back(grad, stream, scale, gain):
    tilted = grad * gain
    grad_gain = jnp.sum(grad * stream * scale, axis=0)
    grad_stream = scale * tilted - stream * scale**3 * jnp.mean(
        tilted * stream, axis=-1, keepdims=True
    )
    return (grad_stream, grad_gain)


def masked_scores(qblock, sblock, keys, seg_all):
    scores = jnp.einsum("qhd,khd->hqk", qblock, keys, preferred_element_type=jnp.float32) * 0.125
    allowed = sblock[:, None] == seg_all[None, :]
    return jnp.where(allowed[None], scores, -1e30)


def attend_forward(query, keys, values, seg_all, heads):
    count = query.shape[0]
    block = min(512, count)
    nblocks = count // block
    qh = query.reshape(nblocks, block, heads, HEAD_DIM)
    kh = keys.reshape(count, heads, HEAD_DIM)
    vh = values.reshape(count, heads, HEAD_DIM)
    segs = seg_all.reshape(nblocks, block)

    def one_block(items):
        qblock, sblock = items
        scores = masked_scores(qblock, sblock, kh, seg_all)
        top = jnp.max(scores, axis=-1, keepdims=True)
        expo = jnp.exp(scores - top)
        total = jnp.sum(expo, axis=-1, keepdims=True)
        probs = (expo / total).astype(jnp.bfloat16)
        mixed = jnp.einsum("hqk,khd->qhd", probs, vh, preferred_element_type=jnp.float32)
        return (mixed.astype(jnp.bfloat16), (top + jnp.log(total))[..., 0])

    mixed, logsum = lax.map(one_block, (qh, segs))
    return (mixed.reshape(count, heads * HEAD_DIM), logsum)


def attend_backward(query, keys, values, grad_mixed, logsum, seg_all, heads):
    count = query.shape[0]
    block = min(512, count)
    nblocks = count // block
    qh = query.reshape(nblocks, block, heads, HEAD_DIM)
    gh = grad_mixed.reshape(nblocks, block, heads, HEAD_DIM)
    kh = keys.reshape(count, heads, HEAD_DIM)
    vh = values.reshape(count, heads, HEAD_DIM)
    segs = seg_all.reshape(nblocks, block)

    def one_block(carry, items):
        grad_keys, grad_values = carry
        qblock, sblock, gblock, lblock = items
        scores = masked_scores(qblock, sblock, kh, seg_all)
        probs = jnp.exp(scores - lblock[..., None])
        grad_values = grad_values + jnp.einsum(
            "hqk,qhd->khd", probs.astype(jnp.bfloat16), gblock, preferred_element_type=jnp.float32
        )
        grad_probs = jnp.einsum("qhd,khd->hqk", gblock, vh, preferred_element_type=jnp.float32)
        centre = jnp.sum(probs * grad_probs, axis=-1, keepdims=True)
        grad_scores = (probs * (grad_probs - centre)).astype(jnp.bfloat16)
        grad_query = (
            jnp.einsum("hqk,khd->qhd", grad_scores, kh, preferred_element_type=jnp.float32) * 0.125
        )
        grad_keys = (
            grad_keys
            + jnp.einsum("hqk,qhd->khd", grad_scores, qblock, preferred_element_type=jnp.float32)
            * 0.125
        )
        return ((grad_keys, grad_values), grad_query)

    zeros = jnp.zeros((count, heads, HEAD_DIM), jnp.float32)
    (grad_keys, grad_values), grad_query = lax.scan(
        one_block, (zeros, zeros), (qh, segs, gh, logsum)
    )
    width = heads * HEAD_DIM
    return (
        grad_query.reshape(count, width),
        grad_keys.reshape(count, width),
        grad_values.reshape(count, width),
    )


def body(
    inputs,
    skip_in,
    cotangent,
    lengths,
    w_concat,
    b_concat,
    gain_attn,
    w_query,
    w_key,
    w_value,
    w_out,
    b_out,
    gain_ffn,
    w_up,
    b_up,
    w_down,
    b_down,
):
    parts = lax.axis_size("mp")
    rank = lax.axis_index("mp")
    rows = inputs.shape[0]
    group = rows * parts
    heads = w_query.shape[1] // HEAD_DIM
    seg_all, pos_all, valid_all = layout(lengths[0], group)
    valid_here = lax.dynamic_slice_in_dim(valid_all, rank * rows, rows, 0)[:, None]
    cosine, sine = tables(pos_all)
    joined = jnp.concatenate([inputs, skip_in], axis=1)
    h0 = jnp.dot(joined, w_concat, preferred_element_type=jnp.float32) + b_concat
    scale_one = lax.rsqrt(jnp.mean(h0 * h0, axis=-1, keepdims=True) + EPS)
    n1 = (h0 * scale_one * gain_attn).astype(jnp.bfloat16)
    n1_all = lax.all_gather(n1, "mp", axis=0, tiled=True)
    query = rotate(
        jnp.dot(n1_all, w_query, preferred_element_type=jnp.float32), cosine, sine, False
    ).astype(jnp.bfloat16)
    keys = rotate(
        jnp.dot(n1_all, w_key, preferred_element_type=jnp.float32), cosine, sine, False
    ).astype(jnp.bfloat16)
    values = jnp.dot(n1_all, w_value, preferred_element_type=jnp.float32).astype(jnp.bfloat16)
    mixed, logsum = attend_forward(query, keys, values, seg_all, heads)
    attn_sum = lax.psum_scatter(
        jnp.dot(mixed, w_out, preferred_element_type=jnp.float32).astype(jnp.bfloat16),
        "mp",
        scatter_dimension=0,
        tiled=True,
    ).astype(jnp.float32)
    h1 = h0 + attn_sum + b_out
    scale_two = lax.rsqrt(jnp.mean(h1 * h1, axis=-1, keepdims=True) + EPS)
    n2 = (h1 * scale_two * gain_ffn).astype(jnp.bfloat16)
    grad_out_rows = cotangent.astype(jnp.float32) * valid_here
    grad_b_down = jnp.sum(grad_out_rows, axis=0)
    grad_out_low = grad_out_rows.astype(jnp.bfloat16)
    n2_all = lax.all_gather(n2, "mp", axis=0, tiled=True)
    upper = jnp.dot(n2_all, w_up, preferred_element_type=jnp.float32) + b_up.astype(jnp.float32)
    hidden = gelu_exact(upper).astype(jnp.bfloat16)
    branch = lax.psum_scatter(
        jnp.dot(hidden, w_down, preferred_element_type=jnp.float32).astype(jnp.bfloat16),
        "mp",
        scatter_dimension=0,
        tiled=True,
    ).astype(jnp.float32)
    grad_out_all = lax.all_gather(grad_out_low, "mp", axis=0, tiled=True)
    grad_w_down = dot_tn(hidden, grad_out_all)
    _, pull = jax.vjp(gelu_exact, upper)
    grad_upper = pull(dot_nt(grad_out_all, w_down))[0].astype(jnp.bfloat16)
    grad_w_up = dot_tn(n2_all, grad_upper)
    grad_b_up = jnp.sum(grad_upper.astype(jnp.float32), axis=0)
    grad_n2 = lax.psum_scatter(
        dot_nt(grad_upper, w_up).astype(jnp.bfloat16), "mp", scatter_dimension=0, tiled=True
    ).astype(jnp.float32)
    output = valid_here * (h1 + branch + b_down)
    grad_h1, grad_gain_ffn = norm_back(grad_n2, h1, scale_two, gain_ffn)
    grad_h1 = grad_h1 + grad_out_rows
    grad_b_out = jnp.sum(grad_h1, axis=0)
    grad_h1_all = lax.all_gather(grad_h1.astype(jnp.bfloat16), "mp", axis=0, tiled=True)
    grad_w_out = dot_tn(mixed, grad_h1_all)
    grad_mixed = dot_nt(grad_h1_all, w_out).astype(jnp.bfloat16)
    grad_query, grad_keys, grad_values = attend_backward(
        query, keys, values, grad_mixed, logsum, seg_all, heads
    )
    grad_qp = rotate(grad_query, cosine, sine, True).astype(jnp.bfloat16)
    grad_kp = rotate(grad_keys, cosine, sine, True).astype(jnp.bfloat16)
    grad_vp = grad_values.astype(jnp.bfloat16)
    grad_w_query = dot_tn(n1_all, grad_qp)
    grad_w_key = dot_tn(n1_all, grad_kp)
    grad_w_value = dot_tn(n1_all, grad_vp)
    total = dot_nt(grad_qp, w_query)
    total = total + dot_nt(grad_kp, w_key)
    grad_n1 = lax.psum_scatter(
        (total + dot_nt(grad_vp, w_value)).astype(jnp.bfloat16),
        "mp",
        scatter_dimension=0,
        tiled=True,
    ).astype(jnp.float32)
    grad_h0, grad_gain_attn = norm_back(grad_n1, h0, scale_one, gain_attn)
    grad_h0_low = (grad_h0 + grad_h1).astype(jnp.bfloat16)
    grad_w_concat = dot_tn(joined, grad_h0_low)
    grad_b_concat = jnp.sum(grad_h0_low.astype(jnp.float32), axis=0)
    grad_joined = dot_nt(grad_h0_low, w_concat)
    width = inputs.shape[1]
    split = (
        lax.psum(grad_w_query.astype(jnp.bfloat16), "dp").astype(jnp.float32),
        lax.psum(grad_w_key.astype(jnp.bfloat16), "dp").astype(jnp.float32),
        lax.psum(grad_w_value.astype(jnp.bfloat16), "dp").astype(jnp.float32),
        lax.psum(grad_w_out.astype(jnp.bfloat16), "dp").astype(jnp.float32),
        lax.psum(grad_w_up.astype(jnp.bfloat16), "dp").astype(jnp.float32),
        lax.psum(grad_b_up.astype(jnp.bfloat16), "dp").astype(jnp.float32),
        lax.psum(grad_w_down.astype(jnp.bfloat16), "dp").astype(jnp.float32),
    )
    shared = lax.psum(
        (grad_w_concat, grad_b_concat, grad_gain_attn, grad_b_out, grad_gain_ffn, grad_b_down),
        ("dp", "mp"),
    )
    return (
        output,
        grad_joined[:, :width],
        grad_joined[:, width:],
        shared[0],
        shared[1],
        shared[2],
        split[0],
        split[1],
        split[2],
        split[3],
        shared[3],
        shared[4],
        split[4],
        split[5],
        split[6],
        shared[5],
    )


def solution(mesh):
    placed = (
        P(("dp", "mp"), None),
        P(("dp", "mp"), None),
        P(("dp", "mp"), None),
        P("dp", None),
        P(),
        P(),
        P(),
        P(None, "mp"),
        P(None, "mp"),
        P(None, "mp"),
        P("mp", None),
        P(),
        P(),
        P(None, "mp"),
        P("mp"),
        P("mp", None),
        P(),
    )
    return jax.shard_map(
        body,
        mesh=mesh,
        in_specs=placed,
        out_specs=(
            P(("dp", "mp"), None),
            P(("dp", "mp"), None),
            P(("dp", "mp"), None),
            P(),
            P(),
            P(),
            P(None, "mp"),
            P(None, "mp"),
            P(None, "mp"),
            P("mp", None),
            P(),
            P(),
            P(None, "mp"),
            P("mp"),
            P("mp", None),
            P(),
        ),
        check_vma=False,
    )
```

profile of v0, /device:TPU:0, one launch (start us, length us, event | category | flops | bytes accessed | tf_op | source)
XLA Modules:
  0.0 3942.7 jit_solution(4838027299111747648)
XLA Ops:
  32.6 101.6 %all-gather.5.cloned.1.call-done = bf16[4096,1024]{1,0:T(8,128)(2,1)} async-done(((bf16[2048,1024]{1,0:T(8,128)(2,1)}), bf16[4096,1024]{1,0:T(8,128)(2,1)}) %all-gather.5.cloned.1.call-update) | async-done | bytes 8388624 | tf_op jit(solution)/shard_map/all_gather | solution.py:172
  166.1 643.8 %while.27 = (s32[]{:T(128)}, bf16[8,512,8,64]{1,3,2,0:T(8,128)(2,1)}, f32[8,8,512]{2,1,0:T(8,128)}, s32[8,512]{1,0:T(8,128)}, s32[4096]{0:T(1024)}, /*index=5*/b...) while((s32[]{:T(128)}, ...), condition=%wide.region_7.8_spmd, body=%wide.region_4.7_spmd.sunk | while | flops 4498649088 | bytes 219306096 | solution.py:94
  825.7 99.3 %reduce-scatter.5.cloned.1.call-done = bf16[2048,1024]{1,0:T(8,128)(2,1)} async-done(((bf16[4096,1024]{1,0:T(8,128)(2,1)}), bf16[2048,1024]{1,0:T(8,128)(2,1)}) %reduce-scatter.5.cloned.1.call-update) | async-done | bytes 4194320 | tf_op jit(solution)/shard_map/reduce_scatter | solution.py:181
  943.5 97.2 %all-gather.7.cloned.1.call-done = bf16[4096,1024]{1,0:T(8,128)(2,1)} async-done(((bf16[2048,1024]{1,0:T(8,128)(2,1)}), bf16[4096,1024]{1,0:T(8,128)(2,1)}) %all-gather.7.cloned.1.call-update) | async-done | bytes 8388624 | tf_op jit(solution)/shard_map/all_gather | solution.py:193
  1040.7 93.9 %multiply_convert_fusion.1 = (bf16[4096,2048]{1,0:T(8,128)(2,1)}, f32[4096,2048]{1,0:T(8,128)}, f32[4096,2048]{1,0:T(8,128)}) fusion(f32[2048]{0:T(1024)S(1)} %convert_element_type.159, bf16[4096,1024]{1,0:T(8,128)(2,1)} %all-gather.7.cloned.1.call-done, bf16[1024,2048]{1,0:T(8,128)(2,1)} %param.34), kind=kOutput, calls=%fused_computation.46 | convolution fusion | flops 17733517312 | bytes 96477184 | tf_op jit(solution)/shard_map/dot_general | solution.py:194
  1146.8 39.6 %fusion.60 = (bf16[2048]{0:T(1024)(128)(2,1)}, bf16[4096,2048]{1,0:T(8,128)(2,1)}) fusion(f32[4096,2048]{1,0:T(8,128)} %get-tuple-element.274, bf16[4096,1024]{1,0:T(8,128)(2,1)} %all-gather.9.cloned.1.call-done, bf16[2048,1024]{1,0:T(8,128)(2,1)} %param.36, f32[4096,2048]{1,0:T(8,128)} %get-tuple-element.305, f32[2048]{0:T(1024)S(1)} %convert_element_type.159), kind=kOutput, calls=%fused_computation.136 | convolution fusion | flops 17314084864 | bytes 96481280 | tf_op jit(solution)/shard_map/dot_general | solution.py:51
  1233.7 75.6 %reduce-scatter.9.cloned.1.call-done = bf16[2048,1024]{1,0:T(8,128)(2,1)} async-done(((bf16[4096,1024]{1,0:T(8,128)(2,1)}), bf16[2048,1024]{1,0:T(8,128)(2,1)}) %reduce-scatter.9.cloned.1.call-update) | async-done | bytes 4194320 | tf_op jit(solution)/shard_map/reduce_scatter | solution.py:208
  1315.9 95.4 %reduce-scatter.7.cloned.1.call-done = bf16[2048,1024]{1,0:T(8,128)(2,1)} async-done(((bf16[4096,1024]{1,0:T(8,128)(2,1)}), bf16[2048,1024]{1,0:T(8,128)(2,1)}) %reduce-scatter.7.cloned.1.call-update) | async-done | bytes 4194320 | tf_op jit(solution)/shard_map/reduce_scatter | solution.py:196
  1430.7 104.1 %all-gather.11.cloned.1.call-done = bf16[4096,1024]{1,0:T(8,128)(2,1)} async-done(((bf16[2048,1024]{1,0:T(8,128)(2,1)}), bf16[4096,1024]{1,0:T(8,128)(2,1)}) %all-gather.11.cloned.1.call-update) | async-done | bytes 8388624 | tf_op jit(solution)/shard_map/all_gather | solution.py:215
  1565.3 1774.5 %while.28 = (s32[]{:T(128)}, f32[4096,8,64]{0,2,1:T(8,128)}, f32[4096,8,64]{0,2,1:T(8,128)}, f32[8,512,8,64]{1,0,3,2:T(8,128)}, bf16[8,512,8,64]{1,3,2,0:T(8,128...) while((s32[]{:T(128)}, f32[4096,8,64]{0,2,1:T(8,128)}, ...), condition=%wide.region_15.16_spmd.clone, body=%wide.region_13.15_spmd.clone.sunk | while | flops 10901254144 | bytes 561092736 | solution.py:130
  1595.3 49.2 %multiply_reduce_fusion.4 = (f32[8,512]{1,0:T(8,128)S(1)}, f32[8,512,4096]{2,1,0:T(8,128)}) fusion(f32[8,512,4096]{2,1,0:T(8,128)} %fusion.147, f32[8,512]{1,0:T(8,128)S(1)} %dynamic-slice_bitcast_fusion.2, bf16[4096,8,64]{0,2,1:T(8,128)(2,1)} %get-tuple-element.494, bf16[8,512,8,64]{1,3,2,0:T(8,128)(2,1)} %get-tuple-element.491, s32[]{:T(128)S(6)} %copy.84, ...), kind=kOutput, calls=%fused_computation.19.clone.2 | convolution fusion | flops 2231365632 | bytes 141066240 | tf_op jit(solution)/shard_map/while/body/eval_jaxpr/qhd,khd->hqk/dot_general | solution.py:70
  1644.5 52.9 %multiply_convert_fusion.5 = bf16[8,512,4096]{2,1,0:T(8,128)(2,1)} fusion(f32[8,512,4096]{2,1,0:T(8,128)} %get-tuple-element.432, f32[8,512,4096]{2,1,0:T(8,128)} %fusion.147, f32[8,512]{1,0:T(8,128)S(1)} %get-tuple-element.433), kind=kLoop, calls=%fused_computation.18.clone.1 | loop fusion | flops 50331648 | bytes 167788544 | tf_op jit(solution)/shard_map/while/body/eval_jaxpr/convert_element_type | solution.py:118
  1812.8 49.2 %multiply_reduce_fusion.4 = (f32[8,512]{1,0:T(8,128)S(1)}, f32[8,512,4096]{2,1,0:T(8,128)}) fusion(f32[8,512,4096]{2,1,0:T(8,128)} %fusion.147, f32[8,512]{1,0:T(8,128)S(1)} %dynamic-slice_bitcast_fusion.2, bf16[4096,8,64]{0,2,1:T(8,128)(2,1)} %get-tuple-element.494, bf16[8,512,8,64]{1,3,2,0:T(8,128)(2,1)} %get-tuple-element.491, s32[]{:T(128)S(6)} %copy.84, ...), kind=kOutput, calls=%fused_computation.19.clone.2 | convolution fusion | flops 2231365632 | bytes 141066240 | tf_op jit(solution)/shard_map/while/body/eval_jaxpr/qhd,khd->hqk/dot_general | solution.py:70
  1862.0 52.9 %multiply_convert_fusion.5 = bf16[8,512,4096]{2,1,0:T(8,128)(2,1)} fusion(f32[8,512,4096]{2,1,0:T(8,128)} %get-tuple-element.432, f32[8,512,4096]{2,1,0:T(8,128)} %fusion.147, f32[8,512]{1,0:T(8,128)S(1)} %get-tuple-element.433), kind=kLoop, calls=%fused_computation.18.clone.1 | loop fusion | flops 50331648 | bytes 167788544 | tf_op jit(solution)/shard_map/while/body/eval_jaxpr/convert_element_type | solution.py:118
  2035.2 49.2 %multiply_reduce_fusion.4 = (f32[8,512]{1,0:T(8,128)S(1)}, f32[8,512,4096]{2,1,0:T(8,128)}) fusion(f32[8,512,4096]{2,1,0:T(8,128)} %fusion.147, f32[8,512]{1,0:T(8,128)S(1)} %dynamic-slice_bitcast_fusion.2, bf16[4096,8,64]{0,2,1:T(8,128)(2,1)} %get-tuple-element.494, bf16[8,512,8,64]{1,3,2,0:T(8,128)(2,1)} %get-tuple-element.491, s32[]{:T(128)S(6)} %copy.84, ...), kind=kOutput, calls=%fused_computation.19.clone.2 | convolution fusion | flops 2231365632 | bytes 141066240 | tf_op jit(solution)/shard_map/while/body/eval_jaxpr/qhd,khd->hqk/dot_general | solution.py:70
  2084.4 52.9 %multiply_convert_fusion.5 = bf16[8,512,4096]{2,1,0:T(8,128)(2,1)} fusion(f32[8,512,4096]{2,1,0:T(8,128)} %get-tuple-element.432, f32[8,512,4096]{2,1,0:T(8,128)} %fusion.147, f32[8,512]{1,0:T(8,128)S(1)} %get-tuple-element.433), kind=kLoop, calls=%fused_computation.18.clone.1 | loop fusion | flops 50331648 | bytes 167788544 | tf_op jit(solution)/shard_map/while/body/eval_jaxpr/convert_element_type | solution.py:118
  2257.5 49.2 %multiply_reduce_fusion.4 = (f32[8,512]{1,0:T(8,128)S(1)}, f32[8,512,4096]{2,1,0:T(8,128)}) fusion(f32[8,512,4096]{2,1,0:T(8,128)} %fusion.147, f32[8,512]{1,0:T(8,128)S(1)} %dynamic-slice_bitcast_fusion.2, bf16[4096,8,64]{0,2,1:T(8,128)(2,1)} %get-tuple-element.494, bf16[8,512,8,64]{1,3,2,0:T(8,128)(2,1)} %get-tuple-element.491, s32[]{:T(128)S(6)} %copy.84, ...), kind=kOutput, calls=%fused_computation.19.clone.2 | convolution fusion | flops 2231365632 | bytes 141066240 | tf_op jit(solution)/shard_map/while/body/eval_jaxpr/qhd,khd->hqk/dot_general | solution.py:70
  2306.7 52.9 %multiply_convert_fusion.5 = bf16[8,512,4096]{2,1,0:T(8,128)(2,1)} fusion(f32[8,512,4096]{2,1,0:T(8,128)} %get-tuple-element.432, f32[8,512,4096]{2,1,0:T(8,128)} %fusion.147, f32[8,512]{1,0:T(8,128)S(1)} %get-tuple-element.433), kind=kLoop, calls=%fused_computation.18.clone.1 | loop fusion | flops 50331648 | bytes 167788544 | tf_op jit(solution)/shard_map/while/body/eval_jaxpr/convert_element_type | solution.py:118
  2479.8 49.2 %multiply_reduce_fusion.4 = (f32[8,512]{1,0:T(8,128)S(1)}, f32[8,512,4096]{2,1,0:T(8,128)}) fusion(f32[8,512,4096]{2,1,0:T(8,128)} %fusion.147, f32[8,512]{1,0:T(8,128)S(1)} %dynamic-slice_bitcast_fusion.2, bf16[4096,8,64]{0,2,1:T(8,128)(2,1)} %get-tuple-element.494, bf16[8,512,8,64]{1,3,2,0:T(8,128)(2,1)} %get-tuple-element.491, s32[]{:T(128)S(6)} %copy.84, ...), kind=kOutput, calls=%fused_computation.19.clone.2 | convolution fusion | flops 2231365632 | bytes 141066240 | tf_op jit(solution)/shard_map/while/body/eval_jaxpr/qhd,khd->hqk/dot_general | solution.py:70
  2529.1 52.9 %multiply_convert_fusion.5 = bf16[8,512,4096]{2,1,0:T(8,128)(2,1)} fusion(f32[8,512,4096]{2,1,0:T(8,128)} %get-tuple-element.432, f32[8,512,4096]{2,1,0:T(8,128)} %fusion.147, f32[8,512]{1,0:T(8,128)S(1)} %get-tuple-element.433), kind=kLoop, calls=%fused_computation.18.clone.1 | loop fusion | flops 50331648 | bytes 167788544 | tf_op jit(solution)/shard_map/while/body/eval_jaxpr/convert_element_type | solution.py:118
  2702.2 49.2 %multiply_reduce_fusion.4 = (f32[8,512]{1,0:T(8,128)S(1)}, f32[8,512,4096]{2,1,0:T(8,128)}) fusion(f32[8,512,4096]{2,1,0:T(8,128)} %fusion.147, f32[8,512]{1,0:T(8,128)S(1)} %dynamic-slice_bitcast_fusion.2, bf16[4096,8,64]{0,2,1:T(8,128)(2,1)} %get-tuple-element.494, bf16[8,512,8,64]{1,3,2,0:T(8,128)(2,1)} %get-tuple-element.491, s32[]{:T(128)S(6)} %copy.84, ...), kind=kOutput, calls=%fused_computation.19.clone.2 | convolution fusion | flops 2231365632 | bytes 141066240 | tf_op jit(solution)/shard_map/while/body/eval_jaxpr/qhd,khd->hqk/dot_general | solution.py:70
  2751.4 52.9 %multiply_convert_fusion.5 = bf16[8,512,4096]{2,1,0:T(8,128)(2,1)} fusion(f32[8,512,4096]{2,1,0:T(8,128)} %get-tuple-element.432, f32[8,512,4096]{2,1,0:T(8,128)} %fusion.147, f32[8,512]{1,0:T(8,128)S(1)} %get-tuple-element.433), kind=kLoop, calls=%fused_computation.18.clone.1 | loop fusion | flops 50331648 | bytes 167788544 | tf_op jit(solution)/shard_map/while/body/eval_jaxpr/convert_element_type | solution.py:118
  2924.5 49.2 %multiply_reduce_fusion.4 = (f32[8,512]{1,0:T(8,128)S(1)}, f32[8,512,4096]{2,1,0:T(8,128)}) fusion(f32[8,512,4096]{2,1,0:T(8,128)} %fusion.147, f32[8,512]{1,0:T(8,128)S(1)} %dynamic-slice_bitcast_fusion.2, bf16[4096,8,64]{0,2,1:T(8,128)(2,1)} %get-tuple-element.494, bf16[8,512,8,64]{1,3,2,0:T(8,128)(2,1)} %get-tuple-element.491, s32[]{:T(128)S(6)} %copy.84, ...), kind=kOutput, calls=%fused_computation.19.clone.2 | convolution fusion | flops 2231365632 | bytes 141066240 | tf_op jit(solution)/shard_map/while/body/eval_jaxpr/qhd,khd->hqk/dot_general | solution.py:70
  2973.7 52.9 %multiply_convert_fusion.5 = bf16[8,512,4096]{2,1,0:T(8,128)(2,1)} fusion(f32[8,512,4096]{2,1,0:T(8,128)} %get-tuple-element.432, f32[8,512,4096]{2,1,0:T(8,128)} %fusion.147, f32[8,512]{1,0:T(8,128)S(1)} %get-tuple-element.433), kind=kLoop, calls=%fused_computation.18.clone.1 | loop fusion | flops 50331648 | bytes 167788544 | tf_op jit(solution)/shard_map/while/body/eval_jaxpr/convert_element_type | solution.py:118
  3026.7 28.1 bitcast_add_fusion.5
  3146.9 49.2 %multiply_reduce_fusion.4 = (f32[8,512]{1,0:T(8,128)S(1)}, f32[8,512,4096]{2,1,0:T(8,128)}) fusion(f32[8,512,4096]{2,1,0:T(8,128)} %fusion.147, f32[8,512]{1,0:T(8,128)S(1)} %dynamic-slice_bitcast_fusion.2, bf16[4096,8,64]{0,2,1:T(8,128)(2,1)} %get-tuple-element.494, bf16[8,512,8,64]{1,3,2,0:T(8,128)(2,1)} %get-tuple-element.491, s32[]{:T(128)S(6)} %copy.84, ...), kind=kOutput, calls=%fused_computation.19.clone.2 | convolution fusion | flops 2231365632 | bytes 141066240 | tf_op jit(solution)/shard_map/while/body/eval_jaxpr/qhd,khd->hqk/dot_general | solution.py:70
  3196.1 52.9 %multiply_convert_fusion.5 = bf16[8,512,4096]{2,1,0:T(8,128)(2,1)} fusion(f32[8,512,4096]{2,1,0:T(8,128)} %get-tuple-element.432, f32[8,512,4096]{2,1,0:T(8,128)} %fusion.147, f32[8,512]{1,0:T(8,128)S(1)} %get-tuple-element.433), kind=kLoop, calls=%fused_computation.18.clone.1 | loop fusion | flops 50331648 | bytes 167788544 | tf_op jit(solution)/shard_map/while/body/eval_jaxpr/convert_element_type | solution.py:118
  3469.6 28.4 reduce-scatter.11.cloned.1.call-done
  3526.0 34.5 psum.101
  3561.1 180.2 %all-reduce.7.cloned.1.call-done = (bf16[1024,512]{1,0:T(8,128)(2,1)}, bf16[1024,512]{1,0:T(8,128)(2,1)}, bf16[1024,512]{1,0:T(8,128)(2,1)}, bf16[512,1024]{1,0:...) async-done(((bf16[1024,512]{1,0:T(8,128)(2,1)}, bf16[1024,512]{1,0:T(8,128)(2,1)}, bf16[1024,512]{1,0:T(8,128)(2,1)}, bf16[512,1024]{1,0:T(8,128)(2,1)}, ...) | async-done | bytes 12582928 | tf_op jit(solution)/shard_map/psum | solution.py:242
  3760.4 42.6 %all-reduce = (f32[1024]{0:T(1024)}, f32[1024]{0:T(1024)}, f32[1024]{0:T(1024)}, f32[1024]{0:T(1024)}, f32[1024]{0:T(1024)}) all-reduce(f32[1024]{0:T(1024)S(1)} %get-tuple-element.271, f32[1024]{0:T(1024)S(1)} %get-tuple-element.216, f32[1024]{0:T(1024)S(1)} %copy-done.42, ...), channel_id=1, replica_groups=mesh['dp'=16,'mp'=2] {'dp','mp'}, use_global_device_ids=true, to_apply=%region_20.21 | all-reduce | flops 5120 | bytes 40960 | tf_op jit(solution)/shard_map/psum | solution.py:250
  3822.1 105.0 %all-reduce.5.cloned.1.call-done = f32[2048,1024]{1,0:T(8,128)} async-done(((f32[2048,1024]{1,0:T(8,128)}), f32[2048,1024]{1,0:T(8,128)}) %all-reduce.5.cloned.1.call-update) | async-done | bytes 8388624 | tf_op jit(solution)/shard_map/psum | solution.py:250
  (339 shorter events, 1983.5 us)
Async XLA Ops:
  7.2 811.6 %copy-start = (bf16[512,1024]{1,0:T(8,128)(2,1)S(1)}, bf16[512,1024]{1,0:T(8,128)(2,1)}, u32[]{:S(2)}) copy-start(bf16[512,1024]{1,0:T(8,128)(2,1)} %param.31) | copy-start | bytes 3145732
  7.2 127.0 %all-gather.5.cloned.1.call-start = ((), (), s32[]{:S(2)}) async-start(), calls=%async_computation.4 | async-start | bytes 12582912 | tf_op jit(solution)/shard_map/all_gather | solution.py:172
  12.0 12.8 copy-start.37
  27.4 897.7 %reduce-scatter.5.cloned.1.call-start = ((), (), s32[]{:S(2)}) async-start(), calls=%async_computation.5 | async-start | bytes 12582912 | tf_op jit(solution)/shard_map/reduce_scatter | solution.py:181
  27.9 106.4 %copy-start.48 = (s32[8,1]{0,1:T(1,128)}, s32[8,1]{0,1:T(1,128)S(1)}, u32[]{:S(2)}) copy-start(s32[8,1]{0,1:T(1,128)S(1)} %reduce-window.4) | copy-start | bytes 100
  32.6 116.7 %copy-start.8 = (f32[4096,32]{0,1:T(8,128)}, f32[4096,32]{0,1:T(8,128)S(1)}, u32[]{:S(2)}) copy-start(f32[4096,32]{0,1:T(8,128)S(1)} %get-tuple-element.297) | copy-start | bytes 1572868
  32.6 116.7 %copy-start.10 = (f32[4096,32]{0,1:T(8,128)}, f32[4096,32]{0,1:T(8,128)S(1)}, u32[]{:S(2)}) copy-start(f32[4096,32]{0,1:T(8,128)S(1)} %get-tuple-element.298) | copy-start | bytes 1572868
  825.6 99.4 %copy-start.33 = (f32[1024]{0:T(1024)S(1)}, f32[1024]{0:T(1024)}, u32[]{:S(2)}) copy-start(f32[1024]{0:T(1024)} %param.26) | copy-start | bytes 12292
  825.6 99.4 %copy-start.44 = (f32[1024]{0:T(1024)S(1)}, f32[1024]{0:T(1024)}, u32[]{:S(2)}) copy-start(f32[1024]{0:T(1024)} %param.32) | copy-start | bytes 12292
  825.7 108.4 %copy-start.35 = (f32[1024]{0:T(1024)S(1)}, f32[1024]{0:T(1024)}, u32[]{:S(2)}) copy-start(f32[1024]{0:T(1024)} %param.33) | copy-start | bytes 12292
  825.7 215.0 %all-gather.7.cloned.1.call-start = ((), (), s32[]{:S(2)}) async-start(), calls=%async_computation.6 | async-start | bytes 12582912 | tf_op jit(solution)/shard_map/all_gather | solution.py:193
  936.5 210.3 %all-gather.9.cloned.1.call-start = ((), (), s32[]{:S(2)}) async-start(), calls=%async_computation.8 | async-start | bytes 12582912 | tf_op jit(solution)/shard_map/all_gather | solution.py:202
  943.4 365.9 %reduce-scatter.9.cloned.1.call-start = ((), (), s32[]{:S(2)}) async-start(), calls=%async_computation.9 | async-start | bytes 12582912 | tf_op jit(solution)/shard_map/reduce_scatter | solution.py:208
  1209.9 201.4 %reduce-scatter.7.cloned.1.call-start = ((), (), s32[]{:S(2)}) async-start(), calls=%async_computation.7 | async-start | bytes 12582912 | tf_op jit(solution)/shard_map/reduce_scatter | solution.py:196
  1233.6 75.7 %copy-start.29 = (f32[2048]{0:T(1024)S(1)}, f32[2048]{0:T(1024)}, u32[]{:S(2)}) copy-start(f32[2048]{0:T(1024)} %copy-done.28) | copy-start | bytes 24580
  1233.6 75.7 %copy-start.36 = (f32[1024]{0:T(1024)S(1)}, f32[1024]{0:T(1024)}, u32[]{:S(2)}) copy-start(f32[1024]{0:T(1024)} %param.33) | copy-start | bytes 12292
  1233.6 177.7 %copy-start.31 = (f32[2048]{0:T(1024)S(1)}, f32[2048]{0:T(1024)}, u32[]{:S(2)}) copy-start(f32[2048]{0:T(1024)} %copy-done.30) | copy-start | bytes 24580
  1233.6 177.7 %copy-start.40 = (f32[2048]{0:T(1024)S(1)}, f32[2048]{0:T(1024)}, u32[]{:S(2)}) copy-start(f32[2048]{0:T(1024)} %get-tuple-element.301) | copy-start | bytes 24580
  1233.6 177.7 %copy-start.45 = (f32[1024]{0:T(1024)S(1)}, f32[1024]{0:T(1024)}, u32[]{:S(2)}) copy-start(f32[1024]{0:T(1024)} %param.37) | copy-start | bytes 12292
  1233.6 301.2 %all-gather.11.cloned.1.call-start = ((), (), s32[]{:S(2)}) async-start(), calls=%async_computation.10 | async-start | bytes 12582912 | tf_op jit(solution)/shard_map/all_gather | solution.py:215
  1430.7 2067.3 %reduce-scatter.11.cloned.1.call-start = ((), (), s32[]{:S(2)}) async-start(), calls=%async_computation.11 | async-start | bytes 12582912 | tf_op jit(solution)/shard_map/reduce_scatter | solution.py:229
  3398.5 342.7 %all-reduce.7.cloned.1.call-start = ((), (), s32[]{:S(2)}) async-start(), calls=%async_computation.13 | async-start | bytes 25165824 | tf_op jit(solution)/shard_map/psum | solution.py:242
  3398.6 48.5 %slice-start.4 = ((s8[8388608]{0:T(1024)(128)(4,1)}), s8[4194304]{0:T(1024)(128)(4,1)S(1)}, s32[]{:S(2)}) async-start(s8[8388608]{0:T(1024)(128)(4,1)} %bitcast.178), calls=%async_computation.18 | async-start | bytes 8388608
  3422.6 24.6 copy-start.20
  3422.6 24.6 slice-start.5
  3452.7 11.2 slice-start.6
  3469.5 28.5 copy-start.27
  3469.5 28.5 copy-start.34
  3469.5 28.5 copy-start.38
  3469.5 34.7 copy-start.39
  3469.5 457.6 %all-reduce.5.cloned.1.call-start = ((), (), s32[]{:S(2)}) async-start(), calls=%async_computation.12 | async-start | bytes 16777216 | tf_op jit(solution)/shard_map/psum | solution.py:250
  3498.0 16.2 slice-start
  (40 other events, 207.5 us)
Sparse Core Ops, SparseCore 0:
  27.5 106.6 all-gather.4
  825.8 99.2 reduce-scatter.4
  936.6 103.9 all-gather.6
  1042.7 103.9 all-gather.8
  1210.1 99.2 reduce-scatter.8
  1312.0 99.2 reduce-scatter.6
  1430.8 104.0 all-gather.10
  3398.7 99.2 reduce-scatter.10
  3504.2 237.0 all-reduce.6
  3747.4 179.6 all-reduce.4
where the time goes:
time: 3960 us; the launch traced here: 3940 us
  matrix products  1940 us (49%)
  waiting for transfers between devices  899 us (23%)
  other arithmetic  731 us (18%)
  local copies, waits for them, and re-layouts  280 us (7%)
  blocking collectives  77.1 us (2%)
    dot_general x16, matrix products, masked_scores(): jnp.einsum('qhd,khd->hqk', qblock, keys, preferred_element_type=jnp.float32)  613 us
    convert_element_type x8, other arithmetic, one_block(): grad_scores = (probs * (grad_probs - centre)).astype(jnp.bfloat16)  423 us
    dot_general x8, matrix products, one_block(): jnp.einsum('hqk,khd->qhd', probs, vh, preferred_element_type=jnp.float32)  223 us
    dot_general x8, matrix products, one_block(): jnp.einsum('hqk,qhd->khd', probs.astype(jnp.bfloat16), gblock, preferred_...  223 us
    dot_general x8, matrix products, one_block(): jnp.einsum('qhd,khd->hqk', gblock, vh, preferred_element_type=jnp.float32)  209 us
    dynamic_update_slice x16, local copies, waits for them, and re-layouts, attend_backward(): lax.scan(one_block, (zeros, zeros), (qh, segs, gh, logsum))  183 us
    psum x1, waiting for transfers between devices, body(): lax.psum(grad_w_query.astype(jnp.bfloat16), 'dp').astype(jnp.float32)  180 us
    dot_general x8, matrix products, one_block(): jnp.einsum('hqk,qhd->khd', grad_scores, qblock, preferred_element_type=jn...  178 us
  transfers between devices with their start and end apart: 10, of which 10 were waited for; matrix products, arithmetic and copies ran while one was open for 7% of the time, Pallas kernels for 0%

commit v1 on v0

v1 whole, which is shorter than its diff:
```python
import functools

import jax
import jax.numpy as jnp
from jax import lax
from jax.experimental import pallas as pl
from jax.experimental.pallas import tpu as pltpu
from jax.sharding import Mesh
from jax.sharding import PartitionSpec as P

HEAD_DIM = 64
HALF = HEAD_DIM // 2
EPS = 1e-06
FIRST_LEAST = 3712
FIRST_MOST = 3840
SEGS = 16
LOG2E = 1.4426950408889634
LN2 = 0.6931471805599453
VMEM = 60 * 2**20

BF = jnp.bfloat16
F32 = jnp.float32


def dot(left, right, dims=((1,), (0,))):
    return lax.dot_general(left, right, (dims, ((), ())), preferred_element_type=F32)


def dot_tn(left, right):
    return dot(left, right, ((0,), (0,)))


def dot_nt(left, right):
    return dot(left, right, ((1,), (1,)))


def layout(lengths_row, count):
    ends = jnp.cumsum(lengths_row)
    starts = ends - lengths_row
    places = jnp.arange(count, dtype=jnp.int32)
    seg = jnp.sum((places[:, None] >= ends[None, :]).astype(jnp.int32), axis=1)
    owner = seg[:, None] == jnp.arange(lengths_row.shape[0], dtype=jnp.int32)[None, :]
    start_of = jnp.sum(jnp.where(owner, starts[None, :], 0), axis=1)
    pos = (places - start_of).astype(F32)
    valid = (places < ends[-1]).astype(F32)
    return (ends.astype(jnp.int32), pos, valid)


def tables(pos):
    freq = jnp.exp(-jnp.log(10000.0) * jnp.arange(HALF, dtype=F32) * 2.0 / HEAD_DIM)
    angle = freq[:, None] * pos[None, :]
    return (jnp.cos(angle), jnp.sin(angle))


def norm_back(grad, stream, scale, gain):
    tilted = grad * gain
    grad_gain = jnp.sum(grad * stream * scale, axis=0)
    grad_stream = scale * tilted - stream * scale**3 * jnp.mean(
        tilted * stream, axis=-1, keepdims=True
    )
    return (grad_stream, grad_gain)


def params():
    return pltpu.CompilerParams(vmem_limit_bytes=VMEM)


def cost(flops, moved):
    return pl.CostEstimate(flops=flops // 8, bytes_accessed=moved // 8, transcendentals=0)


def project_kernel(x_ref, w_ref, cos_ref, sin_ref, q_ref, k_ref, v_ref):
    x = x_ref[...]
    c, s = cos_ref[...], sin_ref[...]
    width = q_ref.shape[0]
    for out, first, factor in ((q_ref, 0, 0.125 * LOG2E), (k_ref, width, 1.0)):
        t = dot_nt(w_ref[first : first + width, :], x)
        for h in range(0, width, HEAD_DIM):
            a, b = t[h : h + HALF], t[h + HALF : h + HEAD_DIM]
            out[h : h + HALF, :] = ((a * c - b * s) * factor).astype(BF)
            out[h + HALF : h + HEAD_DIM, :] = ((b * c + a * s) * factor).astype(BF)
    v_ref[...] = dot_nt(w_ref[2 * width :, :], x).astype(BF)


def project(x, w, cosine, sine):
    count, depth = x.shape
    width = w.shape[0] // 3
    block = min(512, count)
    table = pl.BlockSpec((HALF, block), lambda i: (0, i))
    out = pl.BlockSpec((width, block), lambda i: (0, i))
    return pl.pallas_call(
        project_kernel,
        grid=(count // block,),
        in_specs=[
            pl.BlockSpec((block, depth), lambda i: (i, 0)),
            pl.BlockSpec(w.shape, lambda i: (0, 0)),
            table,
            table,
        ],
        out_specs=[out] * 3,
        out_shape=[jax.ShapeDtypeStruct((width, count), BF)] * 3,
        compiler_params=params(),
        name="project",
    )(x, w, cosine, sine)


def segments(ends_ref, first, count):
    pos = lax.broadcasted_iota(jnp.int32, (1, count), 1) + first
    seg = jnp.zeros((1, count), jnp.int32)
    for i in range(ends_ref.shape[0]):
        seg = seg + (pos >= ends_ref[i]).astype(jnp.int32)
    return lax.broadcasted_iota(jnp.int32, (SEGS, 1), 0) == seg


def zeros(rows, count):
    return jnp.zeros((rows, count), F32)


def key_pieces(count):
    if count == 4096:
        main = [(k0, 384) for k0 in range(0, FIRST_MOST, 384)]
        whole = [(k0, 1024) for k0 in range(0, count, 1024)]
        return [
            (0, 2048, main),
            (2048, 1536, main),
            (3584, 256, whole),
            (FIRST_MOST, 256, [(FIRST_LEAST, count - FIRST_LEAST)]),
        ]
    step = min(512, count)
    every = [(k0, step) for k0 in range(0, count, step)]
    return [(q0, step, every) for q0 in range(0, count, step)]


def attend_kernel(cut, ends_ref, part_ref, q_ref, k_ref, v_ref, o_ref, l_ref, kaug, qaug, vaug):
    count = k_ref.shape[1]
    here = q_ref.shape[1]
    part = part_ref[0]
    same = segments(ends_ref, 0, count)
    kaug[...] = (
        jnp.concatenate([k_ref[...].astype(F32), jnp.where(same, 0.0, -1e30), zeros(48, count)], 0)
        .T.astype(BF)
    )
    mine = segments(ends_ref, part * here, here)
    qaug[...] = jnp.concatenate(
        [q_ref[...].astype(F32), jnp.where(mine, 1.0, 0.0), zeros(48, here)], 0
    ).astype(BF)
    first = lax.broadcasted_iota(jnp.int32, (SEGS, count), 0) == 0
    vaug[...] = jnp.concatenate([v_ref[...].astype(F32), jnp.where(first, 1.0, 0.0)], 0).astype(BF)

    def block(q0, width, pieces):
        queries = qaug[:, q0 : q0 + width]
        top = jnp.full((1, width), -jnp.inf, F32)
        acc = jnp.zeros((HEAD_DIM + SEGS, width), F32)
        for k0, n in pieces:
            scores = dot(kaug[k0 : k0 + n, :], queries)
            higher = jnp.maximum(top, jnp.max(scores, axis=0, keepdims=True))
            probs = jnp.exp2(scores - higher).astype(BF)
            acc = acc * jnp.exp2(top - higher) + dot(vaug[:, k0 : k0 + n], probs)
            top = higher
        total = acc[HEAD_DIM : HEAD_DIM + 1]
        o_ref[:, q0 : q0 + width] = (acc[:HEAD_DIM] / total).astype(BF)
        l_ref[0, :, q0 : q0 + width] = top + jnp.log2(total)

    pieces = key_pieces(count)
    for p in range(cut):
        low, high = p * here, (p + 1) * here

        @pl.when(part == p)
        def _():
            for q0, width, keys in pieces:
                if low <= q0 < high:
                    block(q0 - low, width, keys)


def attend(ends, part, query, keys, values, cut):
    rows, count = query.shape
    heads = rows // HEAD_DIM
    here = count // cut
    whole = pl.BlockSpec((HEAD_DIM, count), lambda h, e, p: (h, 0))
    return pl.pallas_call(
        functools.partial(attend_kernel, cut),
        grid_spec=pltpu.PrefetchScalarGridSpec(
            num_scalar_prefetch=2,
            grid=(heads,),
            in_specs=[
                pl.BlockSpec((HEAD_DIM, here), lambda h, e, p: (h, p[0])),
                whole,
                whole,
            ],
            out_specs=[
                pl.BlockSpec((HEAD_DIM, here), lambda h, e, p: (h, 0)),
                pl.BlockSpec((1, 1, here), lambda h, e, p: (h, 0, 0)),
            ],
            scratch_shapes=[
                pltpu.VMEM((count, 128), BF),
                pltpu.VMEM((128, here), BF),
                pltpu.VMEM((HEAD_DIM + SEGS, count), BF),
            ],
        ),
        out_shape=[
            jax.ShapeDtypeStruct((rows, here), BF),
            jax.ShapeDtypeStruct((heads, 1, here), F32),
        ],
        compiler_params=params(),
        name="attend",
        cost_estimate=cost(4 * rows * here * count, 8 * rows * count),
    )(ends, part, query, keys, values)


def local_segments(ends_ref, part, count):
    return segments(ends_ref, part * count, count)


def spans(first, last, step):
    return [(k0, min(step, last - k0)) for k0 in range(first, last, step)]


def regions(query_part, key_parts, half):
    edge, start = FIRST_MOST - half, FIRST_LEAST - half

    def keys(first, last, p):
        return [(p, k0, n) for k0, n in spans(first, last, 1024)]

    if query_part == 0:
        found = []
        for p in key_parts:
            found += keys(0, half, 0) if p == 0 else keys(0, edge, 1)
        return [(0, half, found)]
    low = edge - 256
    if list(key_parts) == [0]:
        return [(0, edge, keys(0, half, 0)), (edge, half - edge, [])]
    main, mixed, last = [], [], []
    for p in key_parts:
        if p == 0:
            main += keys(0, half, 0)
            mixed += keys(0, half, 0)
        else:
            main += keys(0, edge, 1)
            mixed += keys(0, half, 1)
            last += [(1, start, half - start)]
    return [(0, low, main), (low, 256, mixed), (edge, half - edge, last)]


def half_kernel(query_far, key_sides, given, last, ends_ref, part_ref, *refs):
    refs = list(refs)
    q_ref = refs.pop(0)
    kv = {side: (refs.pop(0), refs.pop(0)) for side in key_sides}
    acc_in, top_in = (refs.pop(0), refs.pop(0)) if given else (None, None)
    out_ref, top_ref = refs.pop(0), refs.pop(0)
    qaug = refs.pop(0)
    kaug = {side: refs.pop(0) for side in key_sides}
    vaug = {side: refs.pop(0) for side in key_sides}
    half = q_ref.shape[1]
    rank = part_ref[0]

    @pl.when(pl.program_id(0) == 0)
    def _():
        for side in key_sides:
            same = local_segments(ends_ref, rank if side == 0 else 1 - rank, half)
            blank = zeros(HEAD_DIM, half)
            kaug[side][...] = (
                jnp.concatenate([blank, jnp.where(same, 0.0, -1e30), zeros(48, half)], 0)
                .T.astype(BF)
            )
            first = lax.broadcasted_iota(jnp.int32, (SEGS, half), 0) == 0
            vaug[side][HEAD_DIM:, :] = jnp.where(first, 1.0, 0.0).astype(BF)
        mine = local_segments(ends_ref, 1 - rank if query_far else rank, half)
        qaug[HEAD_DIM:, :] = jnp.concatenate(
            [jnp.where(mine, 1.0, 0.0), zeros(48, half)], 0
        ).astype(BF)

    for side in key_sides:
        kaug[side][:, :HEAD_DIM] = kv[side][0][...].T
        vaug[side][:HEAD_DIM, :] = kv[side][1][...]
    qaug[:HEAD_DIM, :] = q_ref[...]

    for here in range(2):
        query_part = 1 - here if query_far else here
        part_of = {side: here if side == 0 else 1 - here for side in key_sides}
        side_of = {p: side for side, p in part_of.items()}

        @pl.when(rank == here)
        def _():
            for q0, width, pieces in regions(query_part, list(side_of), half):
                there = slice(q0, q0 + width)
                queries = qaug[:, there]
                if given:
                    top, acc = top_in[0, :, there], acc_in[0, :, there]
                else:
                    top = jnp.full((1, width), -jnp.inf, F32)
                    acc = jnp.zeros((HEAD_DIM + SEGS, width), F32)
                for p, k0, n in pieces:
                    side = side_of[p]
                    scores = dot(kaug[side][k0 : k0 + n, :], queries)
                    higher = jnp.maximum(top, jnp.max(scores, axis=0, keepdims=True))
                    probs = jnp.exp2(scores - higher).astype(BF)
                    acc = acc * jnp.exp2(top - higher) + dot(vaug[side][:, k0 : k0 + n], probs)
                    top = higher
                if last:
                    total = acc[HEAD_DIM : HEAD_DIM + 1]
                    out_ref[:, there] = (acc[:HEAD_DIM] / total).astype(BF)
                    top_ref[0, :, there] = top + jnp.log2(total)
                else:
                    out_ref[0, :, there] = acc
                    top_ref[0, :, there] = top


def attend_half(name, ends, rank, query, query_far, keys, carry=None, last=True):
    rows, half = query.shape
    heads = rows // HEAD_DIM
    sides = sorted(keys)
    head = pl.BlockSpec((HEAD_DIM, half), lambda h, e, r: (h, 0))
    tall = pl.BlockSpec((1, HEAD_DIM + SEGS, half), lambda h, e, r: (h, 0, 0))
    line = pl.BlockSpec((1, 1, half), lambda h, e, r: (h, 0, 0))
    operands = [query]
    for side in sides:
        operands += list(keys[side])
    specs = [head] * len(operands)
    if carry is not None:
        operands += list(carry)
        specs += [tall, line]
    return pl.pallas_call(
        functools.partial(half_kernel, query_far, sides, carry is not None, last),
        grid_spec=pltpu.PrefetchScalarGridSpec(
            num_scalar_prefetch=2,
            grid=(heads,),
            in_specs=specs,
            out_specs=[head if last else tall, line],
            scratch_shapes=[pltpu.VMEM((128, half), BF)]
            + [pltpu.VMEM((half, 128), BF)] * len(sides)
            + [pltpu.VMEM((HEAD_DIM + SEGS, half), BF)] * len(sides),
        ),
        out_shape=[
            jax.ShapeDtypeStruct((rows, half), BF)
            if last
            else jax.ShapeDtypeStruct((heads, HEAD_DIM + SEGS, half), F32),
            jax.ShapeDtypeStruct((heads, 1, half), F32),
        ],
        compiler_params=params(),
        name=name,
        cost_estimate=cost(16 * rows * half * half * len(sides), 8 * rows * half),
    )(ends, rank, *operands)


def split3(x):
    a = x.astype(BF).astype(F32)
    b = (x - a).astype(BF).astype(F32)
    row = lax.broadcasted_iota(jnp.int32, (SEGS, 1), 0)
    return jnp.where(row == 0, a, jnp.where(row == 1, b, jnp.where(row == 2, x - a - b, 0.0)))


def attend_back_kernel(
    ends_ref, q_ref, k_ref, v_ref, g_ref, o_ref, l_ref, cos_ref, sin_ref, d_ref,
    kaug, vaug, qaug, gaug, pair, dq,
):
    count = k_ref.shape[1]
    same = segments(ends_ref, 0, count)
    row = lax.broadcasted_iota(jnp.int32, (SEGS, count), 0)
    shift = jnp.where(row < 3, 1.0, 0.0)
    g = g_ref[...].astype(F32)
    q = q_ref[...].astype(F32)
    delta = jnp.sum(g * o_ref[...].astype(F32), axis=0, keepdims=True)
    kaug[...] = (
        jnp.concatenate(
            [k_ref[...].astype(F32), jnp.where(same, 0.0, -1e30), shift, zeros(32, count)], 0
        )
        .T.astype(BF)
    )
    vaug[...] = (
        jnp.concatenate([v_ref[...].astype(F32), shift, zeros(48, count)], 0).T.astype(BF)
    )
    qaug[...] = jnp.concatenate(
        [q, jnp.where(same, 1.0, 0.0), split3(-l_ref[0]), zeros(32, count)], 0
    ).astype(BF)
    gaug[...] = jnp.concatenate([g, split3(-delta), zeros(48, count)], 0).astype(BF)
    pair[...] = jnp.concatenate([q, g], 0).T.astype(BF)
    dq[...] = jnp.zeros_like(dq)

    def turn(grad, c, s, factor):
        a, b = grad[:HALF], grad[HALF:]
        return (
            jnp.concatenate([a * c + b * s, b * c - a * s], 0) * factor
        ).astype(BF)

    def chunk(k0, n, queries):
        where = pl.ds(k0, n)
        kb, vb, kt = kaug[where, :], vaug[where, :], k_ref[:, where]
        dk = jnp.zeros((n, HEAD_DIM), F32)
        dv = jnp.zeros((n, HEAD_DIM), F32)
        for q0, width in queries:
            there = slice(q0, q0 + width)
            probs = jnp.exp2(dot(kb, qaug[:, there]))
            tilt = (probs * dot(vb, gaug[:, there])).astype(BF)
            dv = dv + dot(probs.astype(BF), pair[there, HEAD_DIM:])
            dk = dk + dot(tilt, pair[there, :HEAD_DIM])
            dq[:, there] += dot(kt, tilt)
        c, s = cos_ref[:, where], sin_ref[:, where]
        d_ref[1, 0, :, where] = turn(dk.T, c, s, LN2)
        d_ref[2, 0, :, where] = dv.T.astype(BF)

    if count == 4096:
        main = [(q0, 1920) for q0 in range(0, FIRST_MOST, 1920)]

        def step(i, carry):
            chunk(pl.multiple_of(i * 512, 512), 512, main)
            return carry

        lax.fori_loop(0, 7, step, 0)
        chunk(3584, 256, [(q0, 1024) for q0 in range(0, count, 1024)])
        chunk(FIRST_MOST, count - FIRST_MOST, [(3584, 512)])
    else:
        size = min(512, count)

        def step(i, carry):
            chunk(pl.multiple_of(i * size, size), size, [(q, size) for q in range(0, count, size)])
            return carry

        lax.fori_loop(0, count // size, step, 0)
    d_ref[0, 0] = turn(dq[...], cos_ref[...], sin_ref[...], 0.125)


def attend_back(ends, query, keys, values, grad, mixed, logsum, cosine, sine):
    rows, count = query.shape
    heads = rows // HEAD_DIM
    whole = pl.BlockSpec((HEAD_DIM, count), lambda h, e: (h, 0))
    table = pl.BlockSpec((HALF, count), lambda h, e: (0, 0))
    out = pl.pallas_call(
        attend_back_kernel,
        grid_spec=pltpu.PrefetchScalarGridSpec(
            num_scalar_prefetch=1,
            grid=(heads,),
            in_specs=[whole] * 5
            + [pl.BlockSpec((1, 1, count), lambda h, e: (h, 0, 0)), table, table],
            out_specs=pl.BlockSpec((3, 1, HEAD_DIM, count), lambda h, e: (0, h, 0, 0)),
            scratch_shapes=[
                pltpu.VMEM((count, 128), BF),
                pltpu.VMEM((count, 128), BF),
                pltpu.VMEM((128, count), BF),
                pltpu.VMEM((128, count), BF),
                pltpu.VMEM((count, 128), BF),
                pltpu.VMEM((HEAD_DIM, count), F32),
            ],
        ),
        out_shape=jax.ShapeDtypeStruct((3, heads, HEAD_DIM, count), BF),
        compiler_params=params(),
        name="attend_back",
        cost_estimate=cost(10 * rows * count * count, 16 * rows * count),
    )(ends, query, keys, values, grad, mixed, logsum, cosine, sine)
    return out.reshape(3 * rows, count)


def turn_back(grad, c, s, factor):
    a, b = grad[:HALF], grad[HALF:]
    return (jnp.concatenate([a * c + b * s, b * c - a * s], 0) * factor).astype(BF)


def back_chunks(key_part, query_parts, half):
    edge = FIRST_MOST - half
    low = edge - 256
    found = []
    if key_part == 0:
        queries = []
        for p in query_parts:
            queries += [(p, 0, half if p == 0 else edge)]
        return [(0, half, 512, queries)]
    main = [(p, 0, half if p == 0 else edge) for p in query_parts]
    found.append((0, low, 512, main))
    found.append((low, 256, 256, [(p, 0, half) for p in query_parts]))
    if 1 in query_parts:
        found.append((edge, half - edge, 256, [(1, low, half - low)]))
    return found


def half_back_kernel(near_only, ends_ref, part_ref, *refs):
    refs = list(refs)
    sides = (0,) if near_only else (0, 1)
    given = {side: [refs.pop(0) for _ in range(8)] for side in sides}
    if near_only:
        partial_ref = refs.pop(0)
        while len(refs) > 1 + 7:
            refs.pop(0)
        out_ref = refs.pop(0)
    else:
        while len(refs) > 2 + 7:
            refs.pop(0)
        out_ref, partial_ref = refs.pop(0), refs.pop(0)
    kaug, vaug, qaug, gaug, pair, dq, sums = refs
    rank = part_ref[0]
    half = given[0][0].shape[1]

    @pl.when(pl.program_id(0) == 0)
    def _():
        row = lax.broadcasted_iota(jnp.int32, (SEGS, half), 0)
        shift = jnp.where(row < 3, 1.0, 0.0)
        blank = zeros(HEAD_DIM, half)
        for side in sides:
            there = slice(side * half, side * half + half)
            same = local_segments(ends_ref, rank if side == 0 else 1 - rank, half)
            kaug[there, :] = (
                jnp.concatenate([blank, jnp.where(same, 0.0, -1e30), shift, zeros(32, half)], 0)
                .T.astype(BF)
            )
            vaug[there, :] = jnp.concatenate([blank, shift, zeros(48, half)], 0).T.astype(BF)
            qaug[HEAD_DIM:, there] = jnp.concatenate(
                [jnp.where(same, 1.0, 0.0), zeros(48, half)], 0
            ).astype(BF)
            gaug[HEAD_DIM:, there] = blank.astype(BF)

    for side in sides:
        q_ref, k_ref, v_ref, g_ref, o_ref, l_ref = given[side][:6]
        there = slice(side * half, side * half + half)
        g = g_ref[...]
        q = q_ref[...]
        delta = jnp.sum(g.astype(F32) * o_ref[...].astype(F32), axis=0, keepdims=True)
        kaug[there, :HEAD_DIM] = k_ref[...].T
        vaug[there, :HEAD_DIM] = v_ref[...].T
        qaug[:HEAD_DIM, there] = q
        qaug[HEAD_DIM + SEGS : HEAD_DIM + 2 * SEGS, there] = split3(-l_ref[0]).astype(BF)
        gaug[:HEAD_DIM, there] = g
        gaug[HEAD_DIM : HEAD_DIM + SEGS, there] = split3(-delta).astype(BF)
        pair[there, :] = jnp.concatenate([q, g], 0).T
    if near_only:
        dq[...] = partial_ref[0, 0]
        sums[...] = partial_ref[1:, 0]
    else:
        dq[...] = jnp.zeros_like(dq)
        sums[...] = jnp.zeros_like(sums)

    def chunk(side, k0, n, queries):
        where = pl.ds(side * half + k0, n)
        kb, vb, kt = kaug[where, :], vaug[where, :], given[side][1][:, pl.ds(k0, n)]
        dk = jnp.zeros((n, HEAD_DIM), F32)
        dv = jnp.zeros((n, HEAD_DIM), F32)
        for q0, width in queries:
            there = slice(q0, q0 + width)
            probs = jnp.exp2(dot(kb, qaug[:, there]))
            tilt = (probs * dot(vb, gaug[:, there])).astype(BF)
            dv = dv + dot(probs.astype(BF), pair[there, HEAD_DIM:])
            dk = dk + dot(tilt, pair[there, :HEAD_DIM])
            dq[:, there] += dot(kt, tilt)
        if side == 0 and not near_only:
            sums[0, :, pl.ds(k0, n)] = dk.T
            sums[1, :, pl.ds(k0, n)] = dv.T
            return
        dk, dv = dk.T, dv.T
        if near_only:
            dk = dk + sums[0, :, pl.ds(k0, n)]
            dv = dv + sums[1, :, pl.ds(k0, n)]
        c, s = given[side][6][:, pl.ds(k0, n)], given[side][7][:, pl.ds(k0, n)]
        out_ref[1, 0, :, pl.ds(k0, n)] = turn_back(dk, c, s, LN2)
        out_ref[2, 0, :, pl.ds(k0, n)] = dv.astype(BF)

    for here in range(2):

        @pl.when(rank == here)
        def _():
            side_of = {here: 0, 1 - here: 1}
            for key_part, side in side_of.items():
                if near_only and side == 1:
                    continue
                if near_only:
                    query_parts = [here]
                else:
                    query_parts = [0, 1] if side == 1 else [1 - here]
                for k0, total, n, queries in back_chunks(key_part, query_parts, half):
                    spread = [(side_of[p] * half + q0, width) for p, q0, width in queries]
                    if total == n:
                        chunk(side, k0, n, spread)
                        continue

                    def step(i, carry):
                        chunk(side, pl.multiple_of(k0 + i * n, n), n, spread)
                        return carry

                    lax.fori_loop(0, total // n, step, 0)

    if near_only:
        c, s = given[0][6][...], given[0][7][...]
        out_ref[0, 0] = turn_back(dq[...], c, s, 0.125)
    else:
        c, s = given[1][6][...], given[1][7][...]
        out_ref[0, 0] = turn_back(dq[:, half:], c, s, 0.125)
        partial_ref[0, 0] = dq[:, :half]
        partial_ref[1:, 0] = sums[...]


def half_back(name, ends, rank, sides, first, count, partial=None, written=(), after=None):
    rows, half = sides[0][0].shape
    heads = rows // HEAD_DIM
    near_only = partial is not None
    head = pl.BlockSpec((HEAD_DIM, half), lambda h, e, r: (h + first, 0))
    line = pl.BlockSpec((1, 1, half), lambda h, e, r: (h + first, 0, 0))
    table = pl.BlockSpec((HALF, half), lambda h, e, r: (0, 0))
    block = pl.BlockSpec((3, 1, HEAD_DIM, half), lambda h, e, r: (0, h + first, 0, 0))
    anywhere = pl.BlockSpec(memory_space=pl.ANY)
    operands, specs = [], []
    for side in sides:
        operands += list(side)
        specs += [head] * 5 + [line, table, table]
    result = jax.ShapeDtypeStruct((3, heads, HEAD_DIM, half), BF)
    if near_only:
        operands.append(partial)
        specs.append(block)
    aliases = {2 + len(operands) + i: i for i in range(len(written))}
    operands += list(written)
    specs += [anywhere] * len(written)
    if after is not None:
        operands.append(after)
        specs.append(anywhere)
    out_specs = [block] if near_only else [block, block]
    out_shape = [result, jax.ShapeDtypeStruct(result.shape, F32)][: len(out_specs)]
    wide = half * len(sides)
    return pl.pallas_call(
        functools.partial(half_back_kernel, near_only),
        grid_spec=pltpu.PrefetchScalarGridSpec(
            num_scalar_prefetch=2,
            grid=(count,),
            in_specs=specs,
            out_specs=out_specs,
            scratch_shapes=[
                pltpu.VMEM((wide, 128), BF),
                pltpu.VMEM((wide, 128), BF),
                pltpu.VMEM((128, wide), BF),
                pltpu.VMEM((128, wide), BF),
                pltpu.VMEM((wide, 128), BF),
                pltpu.VMEM((HEAD_DIM, wide), F32),
                pltpu.VMEM((2, HEAD_DIM, half), F32),
            ],
        ),
        out_shape=out_shape,
        input_output_aliases=aliases,
        compiler_params=params(),
        name=name,
        cost_estimate=cost(40 * count * HEAD_DIM * half * half * (1 if near_only else 3), 40 * count * HEAD_DIM * half),
    )(ends, rank, *operands)


def ffn_kernel(step, given, src_ref, dst_ref, n_ref, g_ref, up_ref, bias_ref, down_ref, *refs):
    branch_in, dn_in = refs[:2] if given else (None, None)
    branch_ref, dn_ref, dw_ref, dbias_ref, branch, dn, sems = refs[3 if given else 0 :]

    rows, depth = n_ref.shape
    steps = [(i, slice(r0, r0 + step)) for i, r0 in enumerate(range(0, rows, step))]
    opening = (pl.program_id(0) == 0) & (pl.program_id(1) == 0)
    closing = (pl.program_id(0) == pl.num_programs(0) - 1) & (
        pl.program_id(1) == pl.num_programs(1) - 1
    )

    def moves(i, part, out):
        if out:
            pairs = ((branch, branch_ref), (dn, dn_ref))
        else:
            pairs = ((branch_in, branch), (dn_in, dn))
        return [
            pltpu.make_async_copy(src.at[part, :], dst.at[part, :], sems.at[j, i])
            for j, (src, dst) in enumerate(pairs)
        ]

    @pl.when(opening)
    def _():
        if given:
            for i, part in steps:
                for move in moves(i, part, False):
                    move.start()
        else:
            branch[...] = jnp.zeros_like(branch)
            dn[...] = jnp.zeros_like(dn)

    up = up_ref[...].reshape(depth, -1)
    down, bias = down_ref[0, 0], bias_ref[0].astype(F32)
    width = up.shape[1]
    dup = jnp.zeros((width, depth), F32)
    ddown = jnp.zeros((width, depth), F32)
    dbias = jnp.zeros((1, width), F32)
    for i, part in steps:
        x, y = n_ref[part, :], g_ref[part, :]
        u = dot(x, up) + bias
        dz = dot_nt(y, down)
        normal = 0.5 * (1.0 + lax.erf(u * 0.7071067811865476))
        density = jnp.exp(-0.5 * u * u) * 0.3989422804014327
        z = (u * normal).astype(BF)
        du = (dz * (normal + u * density)).astype(BF)
        if given:

            @pl.when(opening)
            def _():
                for move in moves(i, part, False):
                    move.wait()

        branch[part, :] += dot(z, down)
        dn[part, :] += dot_nt(du, up)

        @pl.when(closing)
        def _():
            for move in moves(i, part, True):
                move.start()

        ddown = ddown + dot_tn(z, y)
        dup = dup + dot_tn(du, x)
        dbias = dbias + jnp.sum(du.astype(F32), axis=0, keepdims=True)
    dw_ref[0, 0, :width, :] = dup.astype(BF)
    dw_ref[0, 0, width:, :] = ddown.astype(BF)
    dbias_ref[0] = dbias

    @pl.when(closing)
    def _():
        for i, part in steps:
            for move in moves(i, part, True):
                move.wait()


def ffn_block(hidden):
    return min(512, hidden // 2)


def ffn(name, n2, grad, up, bias, down, extra, parts, src, dst, before=None):
    rows, depth = n2.shape
    hidden = up.shape[3]
    block = ffn_block(hidden)
    per = hidden // 2 // block
    step = min(512, rows)
    once = pl.BlockSpec(
        (rows, depth), lambda p, i, f, t: (0, 0), pipeline_mode=pl.Buffered(1)
    )
    anywhere = pl.BlockSpec(memory_space=pl.ANY)
    operands = [n2, grad, up, bias, down] + ([] if before is None else list(before))
    return pl.pallas_call(
        functools.partial(ffn_kernel, step, before is not None),
        grid_spec=pltpu.PrefetchScalarGridSpec(
            num_scalar_prefetch=2,
            grid=(src.shape[0], 2 * per),
            in_specs=[
                once,
                once,
                pl.BlockSpec((2, 1, depth // 2, block), lambda p, i, f, t: (0, f[p], 0, i)),
                pl.BlockSpec((1, 1, block), lambda p, i, f, t: (f[p], 0, i)),
                pl.BlockSpec(
                    (1, 1, block, depth), lambda p, i, f, t: (i // per, f[p], i % per, 0)
                ),
            ]
            + ([] if before is None else [anywhere] * 3),
            out_specs=[anywhere] * 2
            + [
                pl.BlockSpec(
                    (1, 1, 2 * block, depth), lambda p, i, f, t: (i // per, t[p], i % per, 0)
                ),
                pl.BlockSpec((1, 1, block), lambda p, i, f, t: (p, 0, i)),
            ],
            scratch_shapes=[pltpu.VMEM((rows, depth), F32)] * 2
            + [pltpu.SemaphoreType.DMA((2, rows // step))],
        ),
        out_shape=[jax.ShapeDtypeStruct((rows, depth), F32)] * 2
        + [
            jax.ShapeDtypeStruct((2, parts, hidden + extra, depth), BF),
            jax.ShapeDtypeStruct((src.shape[0], 1, hidden), F32),
        ],
        input_output_aliases={} if before is None else {9: 2},
        compiler_params=params(),
        name=name,
        cost_estimate=cost(12 * rows * depth * hidden * src.shape[0], 8 * depth * hidden * src.shape[0]),
    )(src, dst, *operands)


def out_back_kernel(mixed_ref, grad_ref, sums_ref, after_ref, out_ref):
    out_ref[0, 0] = dot(mixed_ref[...], grad_ref[...]).astype(BF)


def out_back(mixed_rows, grad, sums, extra, after):
    heads, rows = mixed_rows.shape
    _, parts, total, depth = sums.shape
    return pl.pallas_call(
        out_back_kernel,
        grid=(parts, 2),
        in_specs=[
            pl.BlockSpec((extra, rows), lambda p, c: (2 * p + c, 0)),
            pl.BlockSpec((rows, depth), lambda p, c: (0, 0)),
            pl.BlockSpec(memory_space=pl.ANY),
            pl.BlockSpec(memory_space=pl.ANY),
        ],
        out_specs=pl.BlockSpec((1, 1, extra, depth), lambda p, c: (c, p, total // extra - 1, 0)),
        out_shape=jax.ShapeDtypeStruct(sums.shape, BF),
        input_output_aliases={2: 0},
        compiler_params=params(),
        name="out_back",
        cost_estimate=cost(2 * rows * depth * heads, 2 * heads * depth),
    )(mixed_rows, grad, sums, after)


def project_back_kernel(*refs):
    out_ref = refs[-1]
    pairs = refs[:-2]
    total = dot(pairs[1][...], pairs[0][...])
    for i in range(2, len(pairs), 2):
        total = total + dot(pairs[i + 1][...], pairs[i][...])
    out_ref[...] = total.T.astype(BF)


def project_back(pairs, after):
    total = pairs[0][1].shape[0]
    depth = pairs[0][0].shape[1]
    block = total // 3
    specs, operands = [], []
    for x, grad in pairs:
        specs += [
            pl.BlockSpec(x.shape, lambda i: (0, 0)),
            pl.BlockSpec((block, x.shape[0]), lambda i: (i, 0)),
        ]
        operands += [x, grad]
    return pl.pallas_call(
        project_back_kernel,
        grid=(3,),
        in_specs=specs + [pl.BlockSpec(memory_space=pl.ANY)],
        out_specs=pl.BlockSpec((depth, block), lambda i: (0, i)),
        out_shape=jax.ShapeDtypeStruct((depth, total), BF),
        compiler_params=params(),
        name="project_back",
        cost_estimate=cost(4 * pairs[0][0].shape[0] * depth * total, 8 * depth * total),
    )(*operands, after)


MESH = pl.DeviceIdType.MESH


def sum_all_kernel(
    big_ref, small_ref, after_ref, out_ref, small_out_ref,
    buf, done, core_in, x_in, y_in, z_in, small, small_in, small_z, local, send, recv, small_send, small_recv,
):
    o, c, m = lax.axis_index("dpo"), lax.axis_index("core"), lax.axis_index("mp")
    y, z = lax.rem(o, 2), lax.div(o, 2)
    zs = 4
    half = buf.shape[0] // 2
    quarter, eighth, last = half // 2, half // 4, half // 16
    sibling = (o, 1 - c, m)
    across = (o, c, 1 - m)
    beside = (z * 2 + 1 - y, c, m)

    def along(j):
        return (j * 2 + y, c, m)

    load = pltpu.make_async_copy(big_ref, buf, local.at[0])
    load.start()
    barrier = pltpu.get_barrier_semaphore()
    others = [lax.rem(z + d, zs) for d in range(1, zs)]
    for device in [sibling, across, beside] + [along(j) for j in others]:
        pl.semaphore_signal(barrier, inc=1, device_id=device, device_id_type=MESH)
    pl.semaphore_wait(barrier, 6)
    small[0] = small_ref[...]
    load.wait()

    def copy(src, dst, i, device, sems=(send, recv)):
        return pltpu.make_async_remote_copy(
            src_ref=src, dst_ref=dst, send_sem=sems[0].at[i], recv_sem=sems[1].at[i],
            device_id=device, device_id_type=MESH,
        )

    def rows(first, n, of=buf):
        return of.at[pl.ds(pl.multiple_of(first, last), n)]

    def back(first, n, i, device):
        return copy(rows(first, n, done), rows(first, n, done), i, device)

    def add(first, n, arrived):
        step = min(128, n)

        def one(i, carry):
            there = pl.ds(pl.multiple_of(first + i * step, last), step)
            here = pl.ds(pl.multiple_of(i * step, step), step)
            buf[there, :] = (
                buf[there, :].astype(F32) + arrived[here, :].astype(F32)
            ).astype(BF)
            return carry

        lax.fori_loop(0, n // step, one, 0)

    started = []

    def go(*args, **kwargs):
        one = copy(*args, **kwargs)
        one.start()
        started.append(one)
        return one

    tiny = (small_send, small_recv)
    mine = c * half
    theirs = (1 - c) * half
    core_a = go(rows(theirs + (1 - m) * quarter, quarter), core_in.at[0], 0, sibling)
    core_b = go(rows(theirs + m * quarter, quarter), core_in.at[1], 1, sibling)
    tiny_core = go(small.at[0], small_in.at[0], 0, sibling, sems=tiny)
    base_far, base = mine + (1 - m) * quarter, mine + m * quarter
    core_a.wait_recv()
    add(base_far, quarter, core_in.at[0])
    x_a = go(rows(base_far + (1 - y) * eighth, eighth), x_in.at[0], 2, across)
    x_b = go(rows(base_far + y * eighth, eighth), x_in.at[1], 3, across)
    tiny_core.wait_recv()
    small[1] = small[0] + small_in[0]
    tiny_x = go(small.at[1], small_in.at[1], 1, across, sems=tiny)
    core_b.wait_recv()
    add(base, quarter, core_in.at[1])
    far_y, near_y = base + (1 - y) * eighth, base + y * eighth
    x_a.wait_recv()
    add(far_y, eighth, x_in.at[0])
    y_a = go(rows(far_y, eighth), y_in, 4, beside)
    tiny_x.wait_recv()
    small[2] = small[1] + small_in[1]
    tiny_y = go(small.at[2], small_in.at[2], 2, beside, sems=tiny)
    x_b.wait_recv()
    add(near_y, eighth, x_in.at[1])
    y_a.wait_recv()
    add(near_y, eighth, y_in)
    for d in range(1, zs):
        j = lax.rem(z + d, zs)
        there = copy(rows(near_y + j * last, last), z_in.at[z], 5 + z, along(j))
        there.start()
        started.append(there)
    tiny_y.wait_recv()
    small_z[z] = small[2] + small_in[2]
    for d in range(1, zs):
        j = lax.rem(z + d, zs)
        there = copy(small_z.at[z], small_z.at[z], 3 + z, along(j), sems=tiny)
        there.start()
        started.append(there)
    own = near_y + z * last
    total = buf[pl.ds(pl.multiple_of(own, last), last), :].astype(F32)
    for d in range(1, zs):
        j = lax.rem(z + d, zs)
        copy(rows(own, last), z_in.at[j], 5 + j, along(j)).wait_recv()
        total = total + z_in[j].astype(F32)
    done[pl.ds(pl.multiple_of(own, last), last), :] = total.astype(BF)

    def hand(first, n, i, device):
        one = back(first, n, i, device)
        one.start()
        started.append(one)
        return one

    for d in range(1, zs):
        hand(own, last, 9 + z, along(lax.rem(z + d, zs)))
    for d in range(1, zs):
        j = lax.rem(z + d, zs)
        back(near_y + j * last, last, 9 + j, along(j)).wait_recv()
    y_back = hand(near_y, eighth, 13, beside)
    x_back = hand(near_y, eighth, 14, across)
    core_back = hand(near_y, eighth, 15, sibling)
    y_back.wait_recv()
    x_more = hand(far_y, eighth, 16, across)
    core_more = hand(far_y, eighth, 17, sibling)
    x_back.wait_recv()
    core_x = hand(base_far + y * eighth, eighth, 18, sibling)
    x_more.wait_recv()
    core_y = hand(base_far + (1 - y) * eighth, eighth, 19, sibling)
    for d in range(1, zs):
        j = lax.rem(z + d, zs)
        copy(small_z.at[j], small_z.at[j], 3 + j, along(j), sems=tiny).wait_recv()
    small_out_ref[...] = (small_z[0] + small_z[1]) + (small_z[2] + small_z[3])
    for one in (core_back, core_more, core_x, core_y):
        one.wait_recv()
    for one in started:
        one.wait_send()
    store = pltpu.make_async_copy(done, out_ref, local.at[1])
    store.start()
    store.wait()


def sum_all(big, small, after):
    rows, width = big.shape
    quarter, eighth, last = rows // 4, rows // 8, rows // 32
    anywhere = pl.BlockSpec(memory_space=pl.ANY)
    whole = pl.BlockSpec(memory_space=pltpu.VMEM)
    dma = pltpu.SemaphoreType.DMA
    return pl.pallas_call(
        sum_all_kernel,
        in_specs=[anywhere, whole, anywhere],
        out_specs=[anywhere, whole],
        out_shape=[
            jax.ShapeDtypeStruct(big.shape, BF),
            jax.ShapeDtypeStruct(small.shape, F32),
        ],
        scratch_shapes=[
            pltpu.VMEM((rows, width), BF),
            pltpu.VMEM((rows, width), BF),
            pltpu.VMEM((2, quarter, width), BF),
            pltpu.VMEM((2, eighth, width), BF),
            pltpu.VMEM((eighth, width), BF),
            pltpu.VMEM((4, last, width), BF),
            pltpu.VMEM((3,) + small.shape, F32),
            pltpu.VMEM((3,) + small.shape, F32),
            pltpu.VMEM((4,) + small.shape, F32),
            dma((2,)),
            dma((20,)),
            dma((20,)),
            dma((7,)),
            dma((7,)),
        ],
        compiler_params=pltpu.CompilerParams(
            collective_id=0, has_side_effects=True, vmem_limit_bytes=VMEM
        ),
        name="sum_all",
        cost_estimate=cost(rows * width, 8 * rows * width),
    )(big, small, after)


def join_back_kernel(grad_ref, w_ref, first_ref, second_ref):
    grad = grad_ref[...]
    width = first_ref.shape[1]
    first_ref[...] = dot_nt(grad, w_ref[:width, :])
    second_ref[...] = dot_nt(grad, w_ref[width:, :])


def join_back(grad, w):
    rows, depth = grad.shape
    width = w.shape[0] // 2
    block = min(256, rows)
    out = pl.BlockSpec((block, width), lambda i: (i, 0))
    return pl.pallas_call(
        join_back_kernel,
        grid=(rows // block,),
        in_specs=[
            pl.BlockSpec((block, depth), lambda i: (i, 0)),
            pl.BlockSpec(w.shape, lambda i: (0, 0)),
        ],
        out_specs=[out, out],
        out_shape=[jax.ShapeDtypeStruct((rows, width), F32)] * 2,
        compiler_params=params(),
        name="join_back",
        cost_estimate=cost(rows * depth * width, 8 * rows * width),
    )(grad, w)


def unpack_kernel(core_ref, own_ref, sibling_ref, up_ref, down_ref):
    mine = core_ref[0] == pl.program_id(0)
    width = down_ref.shape[0]
    block = jnp.where(mine, own_ref[...].astype(F32), sibling_ref[...].astype(F32))
    up_ref[...] = block[:width].T
    down_ref[...] = block[width:]


def unpack(core, own, sibling, hidden):
    depth = own.shape[1]
    block = ffn_block(hidden)
    per = hidden // 2 // block
    piece = pl.BlockSpec((2 * block, depth), lambda c, i, k: (i, 0))
    return pl.pallas_call(
        unpack_kernel,
        grid_spec=pltpu.PrefetchScalarGridSpec(
            num_scalar_prefetch=1,
            grid=(2, per),
            in_specs=[piece, piece],
            out_specs=[
                pl.BlockSpec((depth, block), lambda c, i, k: (0, c * per + i)),
                pl.BlockSpec((block, depth), lambda c, i, k: (c * per + i, 0)),
            ],
        ),
        out_shape=[
            jax.ShapeDtypeStruct((depth, hidden), F32),
            jax.ShapeDtypeStruct((hidden, depth), F32),
        ],
        compiler_params=params(),
        name="unpack",
        cost_estimate=cost(depth * hidden, 12 * depth * hidden),
    )(core, own, sibling)


def body(
    inputs, skip_in, cotangent, lengths, w_concat, b_concat, gain_attn, w_query, w_key, w_value,
    w_out, b_out, gain_ffn, w_up, b_up, w_down, b_down,
):
    parts = lax.axis_size("mp")
    rank = lax.axis_index("mp")
    core = lax.axis_index("core")
    dp = ("dpo", "core")
    rows, width = inputs.shape
    group = rows * parts
    paired = parts == 2 and group == 4096
    ends, pos_all, valid_all = layout(lengths[0], group)
    valid_here = lax.dynamic_slice_in_dim(valid_all, rank * rows, rows, 0)[:, None]
    each, hidden = w_out.shape[0], b_up.shape[0]
    extra = each // 2
    index = rank.reshape(1)
    other = 1 - index
    zero = jnp.zeros((1,), jnp.int32)

    def across(x):
        return lax.ppermute(x, "mp", [(0, 1), (1, 0)])

    def piece(x, i, size, axis=0):
        return lax.dynamic_slice_in_dim(x, i * size, size, axis)

    def order(near, far, axis):
        return jnp.where(
            rank == 0, jnp.concatenate([near, far], axis), jnp.concatenate([far, near], axis)
        )

    joined = jnp.concatenate([inputs, skip_in], axis=1)
    h0 = dot(joined, w_concat) + b_concat
    scale_one = lax.rsqrt(jnp.mean(h0 * h0, axis=-1, keepdims=True) + EPS)
    n1 = (h0 * scale_one * gain_attn).astype(BF)
    n1_far = across(n1) if paired else lax.all_gather(n1, "mp", axis=0, tiled=True)
    def gather(w):
        half = w.shape[0] // 2
        return lax.all_gather(piece(w, core, half), ("core", "mp"), axis=0).reshape(
            2, parts, half, w.shape[1]
        )

    w_qkv = jnp.concatenate([w_query, w_key, w_value], axis=1)
    w_turned = w_qkv.T
    if paired:
        bias_far = across(b_up)
        out_far = across(w_out)
        tables_near = tables(piece(pos_all, rank, rows))
        q_near, k_near, v_near = project(n1, w_turned, *tables_near)
        start = attend_half(
            "near_near", ends, index, q_near, False, {0: (k_near, v_near)}, last=False
        )
        n1_far, start, w_up_late, w_down_late = lax.optimization_barrier(
            (n1_far, start, w_up, w_down)
        )
        up_all = gather(w_up_late)
        down_all = gather(w_down_late)
        tables_far = tables(piece(pos_all, 1 - rank, rows))
        q_far, k_far, v_far = project(n1_far, w_turned, *tables_far)
        mixed_far, log_far = attend_half(
            "far_all", ends, index, q_far, True, {0: (k_near, v_near), 1: (k_far, v_far)}
        )
        mixed_in = across(mixed_far)
        mixed_near, log_near = attend_half(
            "near_far", ends, index, q_near, False, {1: (k_far, v_far)}, carry=start
        )
        mixed_rows = order(mixed_near, mixed_in, 0)
        attended = dot_tn(mixed_near, w_out) + dot_tn(mixed_in, out_far)
    else:
        bias_all = lax.all_gather(b_up, "mp", axis=0).reshape(parts, 1, -1)
        w_out_all = lax.all_gather(w_out, "mp", axis=0, tiled=True)
        up_all = gather(w_up)
        down_all = gather(w_down)
        cosine, sine = tables(pos_all)
        query, keys, values = project(n1_far, w_turned, cosine, sine)
        mixed, logsum = attend(ends, zero, query, keys, values, 1)
        mixed_rows = lax.all_to_all(mixed, "mp", 1, 0, tiled=True)
        attended = dot_tn(mixed_rows, w_out_all)
    h1 = h0 + attended + b_out
    scale_two = lax.rsqrt(jnp.mean(h1 * h1, axis=-1, keepdims=True) + EPS)
    n2 = (h1 * scale_two * gain_ffn).astype(BF)
    grad_rows = cotangent.astype(F32) * valid_here
    grad_low = grad_rows.astype(BF)
    if paired:
        branch, grad_n2, sums, bias_near = ffn(
            "ffn_near", n2, grad_low, w_up.reshape(2, 1, width // 2, hidden),
            b_up.reshape(1, 1, hidden), w_down.reshape(2, 1, hidden // 2, width),
            extra, parts, zero, index,
        )
        both = jnp.stack([bias_far, bias_far]).reshape(2, 1, hidden)
        branch, grad_n2, sums, grad_bias = ffn(
            "ffn_far", n2, grad_low, up_all, both, down_all, extra, parts, other, other,
            before=(branch, grad_n2, sums),
        )
        grad_bias = order(bias_near, grad_bias, 0)
    else:
        every = jnp.arange(parts, dtype=jnp.int32)
        branch, grad_n2, sums, grad_bias = ffn(
            "ffn", n2, grad_low, up_all, bias_all, down_all, extra, parts, every, every
        )
    output = valid_here * (h1 + branch + b_down)
    grad_h1, grad_gain_ffn = norm_back(grad_n2, h1, scale_two, gain_ffn)
    grad_h1 = grad_h1 + grad_rows
    grad_h1_low = grad_h1.astype(BF)
    if paired:
        grad_far = across(dot_nt(out_far, grad_h1_low).astype(BF))
        grad_near = dot_nt(w_out, grad_h1_low).astype(BF)
        landed = grad_far
    else:
        landed = grad_mixed = lax.all_to_all(
            dot_nt(w_out_all, grad_h1_low).astype(BF), "mp", 0, 1, tiled=True
        )
    sums = out_back(mixed_rows, grad_h1_low, sums, extra, landed)
    small = [jnp.sum(grad_rows, 0), grad_gain_ffn, jnp.sum(grad_h1, 0)]
    part = lax.psum_scatter(
        sums.reshape((2 * parts,) + sums.shape[2:]), ("core", "mp"), scatter_dimension=0, tiled=True
    )[0]
    summed = lax.psum(part, "dpo")

    if paired:
        near = (q_near, k_near, v_near, grad_near, mixed_near, log_near) + tables_near
        far = (q_far, k_far, v_far, grad_far, mixed_far, log_far) + tables_far
        heads = each // HEAD_DIM
        calls = 4
        step = heads // calls
        written = ()
        for i in range(calls):
            written = half_back(
                f"back_far{i}", ends, index, (near, far), i * step, step, written=written,
                after=part if i == calls // 2 else None,
            )
        back_far, partial = written
        back_far = back_far.reshape(3 * each, rows)
        sent = across(dot(back_far, w_qkv, ((0,), (1,))).astype(BF))
        written = ()
        for i in range(2):
            written = half_back(
                f"back_near{i}", ends, index, (near,), i * heads // 2, heads // 2,
                partial=partial, written=written, after=summed if i else None,
            )
        back_near = written[0].reshape(3 * each, rows)
        grad_n1 = dot(back_near, w_qkv, ((0,), (1,))) + sent.astype(F32)
        pairs = [(n1, back_near), (n1_far, back_far)]
    else:
        back = attend_back(ends, query, keys, values, grad_mixed, mixed, logsum, cosine, sine)
        grad_n1 = dot(back, w_qkv, ((0,), (1,))).astype(BF)
        grad_n1 = lax.psum_scatter(grad_n1, "mp", scatter_dimension=0, tiled=True).astype(F32)
        pairs = [(n1_far, back)]
    turned = project_back(pairs, summed)
    grad_qkv = lax.psum(turned, dp).astype(F32)
    sibling = lax.ppermute(summed, "core", [(0, 1), (1, 0)])
    grad_up, grad_down = unpack(core.reshape(1), summed, sibling, hidden)
    own_out, sibling_out = summed[hidden:].astype(F32), sibling[hidden:].astype(F32)
    grad_out = jnp.where(
        core == 0,
        jnp.concatenate([own_out, sibling_out]),
        jnp.concatenate([sibling_out, own_out]),
    )

    grad_h0, grad_gain_attn = norm_back(grad_n1, h0, scale_one, gain_attn)
    grad_h0_low = (grad_h0 + grad_h1).astype(BF)
    grad_w_concat = dot_tn(joined, grad_h0_low).astype(BF)
    small = small + [jnp.sum(grad_h0_low.astype(F32), axis=0), grad_gain_attn]
    small = jnp.concatenate(small + [grad_bias.reshape(-1)]).reshape(-1, width)
    small = jnp.pad(small, ((0, -small.shape[0] % 8), (0, 0)))
    if paired and lax.axis_size("dpo") == 8:
        tail, small = sum_all(grad_w_concat, small, turned)
    else:
        tail, small = lax.psum((grad_w_concat, small), dp + ("mp",))
    grad_inputs, grad_skip = join_back(grad_h0_low, w_concat)
    wide = w_query.shape[1]
    return (
        output,
        grad_inputs,
        grad_skip,
        tail.astype(F32),
        small[3],
        small[4],
        grad_qkv[:, :wide],
        grad_qkv[:, wide : 2 * wide],
        grad_qkv[:, 2 * wide :],
        grad_out,
        small[2],
        small[1],
        grad_up,
        piece(small[5 : 5 + parts * hidden // width].reshape(-1), rank, hidden),
        grad_down,
        small[0],
    )


def solution(mesh):
    dp, mp = mesh.shape["dp"], mesh.shape["mp"]
    mesh = Mesh(mesh.devices.reshape(dp // 2, 2, mp), ("dpo", "core", "mp"))
    rows = P(("dpo", "core", "mp"), None)
    columns = P(None, "mp")
    upright = P("mp", None)
    return jax.shard_map(
        body,
        mesh=mesh,
        in_specs=(
            rows, rows, rows, P(("dpo", "core"), None), P(), P(), P(), columns, columns, columns,
            upright, P(), P(), columns, P("mp"), upright, P(),
        ),
        out_specs=(
            rows, rows, rows, P(), P(), P(), columns, columns, columns,
            upright, P(), P(), columns, P("mp"), upright, P(),
        ),
        check_vma=False,
    )
```

time: 3960 us -> 1320 us (0.33)
  matrix products: 1940 us -> 72.4 us
  Pallas kernels: 0 us -> 833 us
  other arithmetic: 731 us -> 61.7 us
  waiting for transfers between devices: 899 us -> 284 us
  local copies, waits for them, and re-layouts: 280 us -> 31.3 us
  blocking collectives: 77.1 us -> 0 us
    dot_general x77 -> x8, matrix products: 1940 us -> 72.4 us  [dot(): lax.dot_general(left, right, (dims, ((), ())), preferred_element_type=F32)]
    pallas_call x0 -> x18, Pallas kernels: none -> 833 us  [the longest x6 369 us: half_back(): pl.pallas_call(functools.partial(half_back_kernel, near_only), grid_spec=...]
    convert_element_type x23 -> x9, other arithmetic: 463 us -> 20.7 us  [the longest x1 6.67 us: body(): tail.astype(F32)]
    all_gather x4 -> x2, waiting for transfers between devices: 315 us -> 0.04 us  [gather(): lax.all_gather(piece(w, core, half), ('core', 'mp'), axis=0)]
    reduce_scatter x4 -> x1, waiting for transfers between devices: 299 us -> 0.02 us  [body(): lax.psum_scatter(sums.reshape((2 * parts,) + sums.shape[2:]), ('core', 'm...]
    dynamic_update_slice x16 -> x0, local copies, waits for them, and re-layouts: 183 us -> none  [attend_backward(): lax.scan(one_block, (zeros, zeros), (qh, segs, gh, logsum))]
    reduce_sum x11 -> x2, other arithmetic: 200 us -> 20.8 us  [the longest x1 12.1 us: body(): small = [jnp.sum(grad_rows, 0), grad_gain_ffn, jnp.sum(grad_h1, 0)]]
    psum x2, waiting for transfers between devices: 285 us -> 134 us  [the longest x1 86.3 us: body(): grad_qkv = lax.psum(turned, dp).astype(F32)]
  transfers between devices with their start and end apart: 10 -> 12, of which waited for: 10 -> 5; matrix products, arithmetic and copies ran while one was open for 7% -> 7% of each run, Pallas kernels for 0% -> 51%
where the time goes in v1:
time: 1320 us
  Pallas kernels  833 us (63%)
  waiting for transfers between devices  284 us (22%)
  matrix products  72.4 us (5%)
  other arithmetic  61.7 us (5%)
  local copies, waits for them, and re-layouts  31.3 us (2%)
  starting transfers between devices  20.2 us (2%)
  between operations  14.7 us (1%)
    pallas_call x6, Pallas kernels, half_back(): pl.pallas_call(functools.partial(half_back_kernel, near_only), grid_spec=...  369 us
    pallas_call x3, Pallas kernels, attend_half(): pl.pallas_call(functools.partial(half_kernel, query_far, sides, carry is...  172 us
    ppermute x6, waiting for transfers between devices, across(): return lax.ppermute(x, 'mp', [(0, 1), (1, 0)])  148 us
    pallas_call x2, Pallas kernels, ffn(): pl.pallas_call(functools.partial(ffn_kernel, step, before is not None), g...  126 us
    pallas_call x1, Pallas kernels, sum_all(): pl.pallas_call(sum_all_kernel, in_specs=[anywhere, whole, anywhere], out_...  88.1 us
    psum x1, waiting for transfers between devices, body(): grad_qkv = lax.psum(turned, dp).astype(F32)  86.3 us
    dot_general x8, matrix products, dot(): lax.dot_general(left, right, (dims, ((), ())), preferred_element_type=F32)  72.4 us
    psum x1, waiting for transfers between devices, body(): summed = lax.psum(part, 'dpo')  48.2 us
  transfers between devices with their start and end apart: 12, of which 5 were waited for; matrix products, arithmetic and copies ran while one was open for 7% of the time, Pallas kernels for 51%

profile of v1, /device:TPU:0, one launch (start us, length us, event | category | flops | bytes accessed | tf_op | source)
XLA Modules:
  0.0 1316.7 jit_solution(8492188367183189007)
XLA Ops:
  12.0 9.3 multiply_reduce_fusion.5
  37.1 11.3 project.2
  48.4 44.0 %near_near.1 = (f32[8,80,2048]{2,1,0:T(8,128)}, f32[8,1,2048]{2,1,0:T(1,128)}) custom-call(s32[8]{0:T(128)} %bitcast.66, s32[1]{0:T(128)} %bitcast.3.part_ref.dst_ref, bf16[512,2048]{1,0:T(8,128)(2,1)} %get-tuple-element.55.refs_0_, bf16[512,2048]{1,0:T(8,128)(2,1)} %get-tuple-element.56.refs_1_, bf16[512,2048]{1,0:T(8,128)(2,1)} %get-tuple-element.57.refs_2_), custom_call_target="tpu_custom_call" | custom-call | flops 4294967296 | bytes 1048576 | tf_op jit(solution)/shard_map/near_near/pallas_call | solution.py:322
  92.4 27.5 %collective-permute-done.x_ref.refs_2_ = bf16[2048,1024]{1,0:T(8,128)(2,1)} collective-permute-done((bf16[2048,1024]{1,0:T(8,128)(2,1)}, bf16[2048,1024]{1,0:T(8,128)(2,1)}, u32[]{:S(2)}, u32[]{:S(2)}) %collective-permute-start) | collective-permute-done | bytes 4194336 | tf_op jit(solution)/shard_map/ppermute | solution.py:1083
  126.3 11.3 project.3
  137.6 83.9 %far_all.1 = (bf16[512,2048]{1,0:T(8,128)(2,1)}, f32[8,1,2048]{2,1,0:T(1,128)}) custom-call(s32[8]{0:T(128)} %bitcast.67, s32[1]{0:T(128)} %bitcast.3.part_ref.dst_ref, bf16[512,2048]{1,0:T(8,128)(2,1)} %get-tuple-element.66.refs_0_.refs_8_, bf16[512,2048]{1,0:T(8,128)(2,1)} %get-tuple-element.56.refs_1_, bf16[512,2048]{1,0:T(8,128)(2,1)} %get-tuple-element.57.refs_2_, ...), custom_call_target="tpu_custom_call" | custom-call | flops 8589934592 | bytes 1048576 | tf_op jit(solution)/shard_map/far_all/pallas_call | solution.py:322
  230.6 78.6 %collective-permute-done.3 = bf16[2048]{0:T(1024)(128)(2,1)S(1)} collective-permute-done((bf16[2048]{0:T(1024)(128)(2,1)S(1)}, bf16[2048]{0:T(1024)(128)(2,1)S(1)}, u32[]{:S(2)}, u32[]{:S(2)}) %collective-permute-start.3) | collective-permute-done | bytes 4128 | tf_op jit(solution)/shard_map/ppermute | solution.py:1083
  309.9 44.5 %near_far.1 = (bf16[512,2048]{1,0:T(8,128)(2,1)}, f32[8,1,2048]{2,1,0:T(1,128)}) custom-call(s32[8]{0:T(128)} %bitcast.68, s32[1]{0:T(128)} %bitcast.3.part_ref.dst_ref, bf16[512,2048]{1,0:T(8,128)(2,1)} %get-tuple-element.55.refs_0_, bf16[512,2048]{1,0:T(8,128)(2,1)} %get-tuple-element.61.refs_1_.refs_3_.refs_9_, ...), custom_call_target="tpu_custom_call" | custom-call | flops 4294967296 | bytes 1048576 | tf_op jit(solution)/shard_map/near_far/pallas_call | solution.py:322
  358.7 7.8 multiply_reduce_fusion.4
  371.1 63.1 %ffn_near.1 = (f32[2048,1024]{1,0:T(8,128)}, f32[2048,1024]{1,0:T(8,128)}, bf16[2,2,2304,1024]{3,2,1,0:T(8,128)(2,1)}, f32[1,1,2048]{2,1,0:T(1,128)}) custom-call(s32[1]{0:T(128)} %constant.42.clone.1.src_ref, s32[1]{0:T(128)} %bitcast.3.part_ref.dst_ref, bf16[2048,1024]{1,0:T(8,128)(2,1)} %multiply_convert_fusion.n_ref, bf16[2048,1024]{1,0:T(8,128)(2,1)} %fusion.1.g_ref, ...), custom_call_target="tpu_custom_call" | custom-call | flops 6442450944 | bytes 2097152 | tf_op jit(solution)/shard_map/ffn_near/pallas_call | solution.py:727
  434.3 63.2 %ffn_far.1 = (f32[2048,1024]{1,0:T(8,128)}, f32[2048,1024]{1,0:T(8,128)}, bf16[2,2,2304,1024]{3,2,1,0:T(8,128)(2,1)}, f32[1,1,2048]{2,1,0:T(1,128)}) custom-call(s32[1]{0:T(128)S(6)} %sub.22.src_ref.dst_ref, s32[1]{0:T(128)S(6)} %sub.22.src_ref.dst_ref, bf16[2048,1024]{1,0:T(8,128)(2,1)} %multiply_convert_fusion.n_ref, ...), custom_call_target="tpu_custom_call", output_to_operand_aliasing={{2}: (9, {})} | custom-call | flops 6442450944 | bytes 2097152 | tf_op jit(solution)/shard_map/ffn_far/pallas_call | solution.py:727
  497.6 7.9 multiply_reduce_fusion.1
  506.9 12.1 fusion.7
  531.7 41.9 %collective-permute-done.4.refs_11_.after_ref = bf16[512,2048]{1,0:T(8,128)(2,1)} collective-permute-done((bf16[512,2048]{1,0:T(8,128)(2,1)}, bf16[512,2048]{1,0:T(8,128)(2,1)}, u32[]{:S(2)}, u32[]{:S(2)}) %collective-permute-start.4) | collective-permute-done | bytes 2097184 | tf_op jit(solution)/shard_map/ppermute | solution.py:1083
  573.5 8.5 out_back.1
  589.2 62.8 %back_far0.1 = (bf16[3,8,64,2048]{3,2,1,0:T(8,128)(2,1)}, f32[3,8,64,2048]{3,2,1,0:T(8,128)}) custom-call(s32[8]{0:T(128)} %bitcast.69, s32[1]{0:T(128)} %bitcast.3.part_ref.dst_ref, bf16[512,2048]{1,0:T(8,128)(2,1)} %get-tuple-element.55.refs_0_, bf16[512,2048]{1,0:T(8,128)(2,1)} %get-tuple-element.56.refs_1_, bf16[512,2048]{1,0:T(8,128)(2,1)} %get-tuple-element.57.refs_2_, ...), custom_call_target="tpu_custom_call" | custom-call | flops 8053063680 | bytes 1310720 | tf_op jit(solution)/shard_map/back_far0/pallas_call | solution.py:613
  652.0 73.8 %back_far1.1 = (bf16[3,8,64,2048]{3,2,1,0:T(8,128)(2,1)}, f32[3,8,64,2048]{3,2,1,0:T(8,128)}) custom-call(s32[8]{0:T(128)} %bitcast.70, s32[1]{0:T(128)} %bitcast.3.part_ref.dst_ref, bf16[512,2048]{1,0:T(8,128)(2,1)} %get-tuple-element.55.refs_0_, bf16[512,2048]{1,0:T(8,128)(2,1)} %get-tuple-element.56.refs_1_, ...), custom_call_target="tpu_custom_call", output_to_operand_aliasing={{0}: (18, {}), {1}: (19, {})} | custom-call | flops 8053063680 | bytes 1310720 | tf_op jit(solution)/shard_map/back_far1/pallas_call | solution.py:613
  725.9 73.4 %back_far2.1 = (bf16[3,8,64,2048]{3,2,1,0:T(8,128)(2,1)}, f32[3,8,64,2048]{3,2,1,0:T(8,128)}) custom-call(s32[8]{0:T(128)} %bitcast.71, s32[1]{0:T(128)} %bitcast.3.part_ref.dst_ref, bf16[512,2048]{1,0:T(8,128)(2,1)} %get-tuple-element.55.refs_0_, bf16[512,2048]{1,0:T(8,128)(2,1)} %get-tuple-element.56.refs_1_, ...), custom_call_target="tpu_custom_call", output_to_operand_aliasing={{0}: (18, {}), {1}: (19, {})} | custom-call | flops 8053063680 | bytes 1310720 | tf_op jit(solution)/shard_map/back_far2/pallas_call | solution.py:613
  800.0 61.7 %back_far3.1 = (bf16[3,8,64,2048]{3,2,1,0:T(8,128)(2,1)}, f32[3,8,64,2048]{3,2,1,0:T(8,128)}) custom-call(s32[8]{0:T(128)} %bitcast.72, s32[1]{0:T(128)} %bitcast.3.part_ref.dst_ref, bf16[512,2048]{1,0:T(8,128)(2,1)} %get-tuple-element.55.refs_0_, bf16[512,2048]{1,0:T(8,128)(2,1)} %get-tuple-element.56.refs_1_, ...), custom_call_target="tpu_custom_call", output_to_operand_aliasing={{0}: (18, {}), {1}: (19, {})} | custom-call | flops 8053063680 | bytes 1310720 | tf_op jit(solution)/shard_map/back_far3/pallas_call | solution.py:613
  861.7 11.2 convolution_convert_fusion
  872.9 14.4 %collective-permute-start.5 = (bf16[2048,1024]{1,0:T(8,128)(2,1)}, bf16[2048,1024]{1,0:T(8,128)(2,1)}, u32[]{:S(2)}, u32[]{:S(2)}) collective-permute-start(bf16[2048,1024]{1,0:T(8,128)(2,1)} %convolution_convert_fusion), channel_id=1, source_target_pairs={{0,1},{1,0},{2,3},{3,2},{4,5},{5,4},{6,7},{7,6},{8,9},{9,8},{10,11... | collective-permute-start | bytes 12582920 | tf_op jit(solution)/shard_map/ppermute | solution.py:1083
  887.4 48.7 %back_near0.1.refs_9_ = bf16[3,8,64,2048]{3,2,1,0:T(8,128)(2,1)} custom-call(s32[8]{0:T(128)} %bitcast.73, s32[1]{0:T(128)} %bitcast.3.part_ref.dst_ref, bf16[512,2048]{1,0:T(8,128)(2,1)} %get-tuple-element.55.refs_0_, bf16[512,2048]{1,0:T(8,128)(2,1)} %get-tuple-element.56.refs_1_, bf16[512,2048]{1,0:T(8,128)(2,1)} %get-tuple-element.57.refs_2_, ...), custom_call_target="tpu_custom_call" | custom-call | flops 5368709120 | bytes 2621440 | tf_op jit(solution)/shard_map/back_near0/pallas_call | solution.py:613
  936.1 48.2 %all-reduce.4.cloned.1.call-done.refs_10_.refs_4_.own_ref = bf16[2304,1024]{1,0:T(8,128)(2,1)} async-done(((bf16[2304,1024]{1,0:T(8,128)(2,1)}), bf16[2304,1024]{1,0:T(8,128)(2,1)}) %all-reduce.4.cloned.1.call-update) | async-done | bytes 4718608 | tf_op jit(solution)/shard_map/psum | solution.py:1179
  984.3 48.9 %back_near1.1 = bf16[3,8,64,2048]{3,2,1,0:T(8,128)(2,1)} custom-call(s32[8]{0:T(128)} %bitcast.74, s32[1]{0:T(128)} %bitcast.3.part_ref.dst_ref, bf16[512,2048]{1,0:T(8,128)(2,1)} %get-tuple-element.55.refs_0_, bf16[512,2048]{1,0:T(8,128)(2,1)} %get-tuple-element.56.refs_1_, ...), custom_call_target="tpu_custom_call", output_to_operand_aliasing={{}: (11, {})} | custom-call | flops 5368709120 | bytes 2621440 | tf_op jit(solution)/shard_map/back_near1/pallas_call | solution.py:613
  1033.3 16.3 %multiply_reduce_fusion = (f32[1024]{0:T(1024)S(1)}, f32[2048]{0:T(1024)S(1)}, f32[2048,1024]{1,0:T(8,128)S(1)}) fusion(f32[2048,1024]{1,0:T(8,128)} %copy-done.2, f32[2048]{0:T(1024)S(1)} %copy-done.20, f32[1024]{0:T(1024)S(1)} %copy-done.22, f32[1024]{0:T(1024)S(1)} %copy-done.28, bf16[2048,1024]{1,0:T(8,128)(2,1)} %collective-permute-done.5, ...), kind=kOutput, calls=%fused_computation | convolution fusion | flops 6470759424 | bytes 30437376 | tf_op jit(solution)/shard_map/dot_general | solution.py:26
  1049.6 8.7 convert_reduce_fusion
  1058.4 19.4 %project_back.1.after_ref = bf16[1024,1536]{1,0:T(8,128)(2,1)} custom-call(bf16[2048,1024]{1,0:T(8,128)(2,1)} %multiply_convert_fusion.1.x_ref.refs_0_, bf16[1536,2048]{1,0:T(8,128)(2,1)} %bitcast.56, bf16[2048,1024]{1,0:T(8,128)(2,1)} %collective-permute-done.x_ref.refs_2_, bf16[1536,2048]{1,0:T(8,128)(2,1)} %bitcast.54, ...), custom_call_target="tpu_custom_call" | custom-call | flops 1610612736 | bytes 1572864 | tf_op jit(solution)/shard_map/project_back/pallas_call | solution.py:809
  1077.8 14.0 %convolution_convert_fusion.1.big_ref = bf16[2048,1024]{1,0:T(8,128)(2,1)} fusion(bf16[2048,2048]{1,0:T(8,128)(2,1)} %copy-done.16, bf16[2048,1024]{1,0:T(8,128)(2,1)} %get-tuple-element.99.grad_ref), kind=kOutput, calls=%fused_computation.19 | convolution fusion | flops 8592031744 | bytes 16777216 | tf_op jit(solution)/shard_map/dot_general | solution.py:26
  1092.4 88.1 %sum_all.1 = (bf16[2048,1024]{1,0:T(8,128)(2,1)}, f32[16,1024]{1,0:T(8,128)}) custom-call(bf16[2048,1024]{1,0:T(8,128)(2,1)} %convolution_convert_fusion.1.big_ref, f32[16,1024]{1,0:T(8,128)} %pad.4.small_ref, bf16[1024,1536]{1,0:T(8,128)(2,1)} %project_back.1.after_ref), custom_call_target="tpu_custom_call" | custom-call | flops 262144 | bytes 2097152 | tf_op jit(solution)/shard_map/sum_all/pallas_call | solution.py:970
  1188.4 14.3 %join_back.1 = (f32[2048,1024]{1,0:T(8,128)}, f32[2048,1024]{1,0:T(8,128)}) custom-call(bf16[2048,1024]{1,0:T(8,128)(2,1)} %get-tuple-element.99.grad_ref, bf16[2048,1024]{1,0:T(8,128)(2,1)} %w_ref.1), custom_call_target="tpu_custom_call" | custom-call | flops 268435456 | bytes 2097152 | tf_op jit(solution)/shard_map/join_back/pallas_call | solution.py:1014
  1204.5 86.3 %all-reduce.6.cloned.1.call-done = bf16[1024,1536]{1,0:T(8,128)(2,1)} async-done(((bf16[1024,1536]{1,0:T(8,128)(2,1)}), bf16[1024,1536]{1,0:T(8,128)(2,1)}) %all-reduce.6.cloned.1.call-update) | async-done | bytes 3145744 | tf_op jit(solution)/shard_map/psum | solution.py:1211
  1298.3 11.6 unpack.1
  (147 shorter events, 85.2 us)
Async XLA Ops:
  7.2 427.1 %all-gather.5.cloned.1.call-start = ((), (), s32[]{:S(2)}) async-start(), calls=%async_computation.4 | async-start | bytes 10485760 | tf_op jit(solution)/shard_map/all_gather | solution.py:1100
  11.9 9.3 copy-start.16
  11.9 10.0 copy-start.27
  21.9 7.8 copy-start.18
  26.1 93.8 %collective-permute-start = (bf16[2048,1024]{1,0:T(8,128)(2,1)}, bf16[2048,1024]{1,0:T(8,128)(2,1)}, u32[]{:S(2)}, u32[]{:S(2)}) collective-permute-start(bf16[2048,1024]{1,0:T(8,128)(2,1)} %multiply_convert_fusion.1.x_ref.refs_0_), channel_id=1, source_target_pairs={{0,1},{1,0},{2,3},{3,2},{4,5},{5,4},{6,7},{7,6},{8,9},{9,8},{10,11... | collective-permute-start | bytes 12582920 | tf_op jit(solution)/shard_map/ppermute | solution.py:1083
  29.8 18.6 %copy-start.10 = (bf16[1024,512]{0,1:T(8,128)(2,1)}, bf16[1024,512]{0,1:T(8,128)(2,1)S(1)}, u32[]{:S(2)}) copy-start(bf16[1024,512]{0,1:T(8,128)(2,1)S(1)} %copy.53) | copy-start | bytes 3145732
  30.3 18.1 %copy-start.12 = (bf16[1024,512]{0,1:T(8,128)(2,1)}, bf16[1024,512]{0,1:T(8,128)(2,1)S(1)}, u32[]{:S(2)}) copy-start(bf16[1024,512]{0,1:T(8,128)(2,1)S(1)} %copy.54) | copy-start | bytes 3145732
  32.2 16.2 %copy-start.14 = (bf16[1024,512]{0,1:T(8,128)(2,1)}, bf16[1024,512]{0,1:T(8,128)(2,1)S(1)}, u32[]{:S(2)}) copy-start(bf16[1024,512]{0,1:T(8,128)(2,1)S(1)} %copy.55) | copy-start | bytes 3145732
  123.1 311.2 %all-gather.7.cloned.1.call-start = ((), (), s32[]{:S(2)}) async-start(), calls=%async_computation.5 | async-start | bytes 10485760 | tf_op jit(solution)/shard_map/all_gather | solution.py:1100
  126.3 599.7 %reduce-scatter.2.cloned.1.call-start = ((), (), s32[]{:S(2)}) async-start(), calls=%async_computation.1 | async-start | bytes 23592960 | tf_op jit(solution)/shard_map/reduce_scatter | solution.py:1176
  137.6 86.0 %copy-start.33 = (bf16[2048]{0:T(1024)(128)(2,1)S(1)}, bf16[2048]{0:T(1024)(128)(2,1)}, u32[]{:S(2)}) copy-start(bf16[2048]{0:T(1024)(128)(2,1)} %param.31) | copy-start | bytes 12292
  137.6 86.1 %copy-start.26 = (s32[8,1]{0,1:T(1,128)S(1)}, s32[8,1]{0,1:T(1,128)}, u32[]{:S(2)}) copy-start(s32[8,1]{0,1:T(1,128)} %copy-done.25) | copy-start | bytes 100
  221.6 137.1 %collective-permute-start.1 = (bf16[512,2048]{1,0:T(8,128)(2,1)}, bf16[512,2048]{1,0:T(8,128)(2,1)S(1)}, u32[]{:S(2)}, u32[]{:S(2)}) collective-permute-start(bf16[512,2048]{1,0:T(8,128)(2,1)} %get-tuple-element.67.refs_12_), channel_id=1, source_target_pairs={{0,1},{1,0},{2,3},{3,2},{4,5},{5,4},{6,7},{7,6},{8,9},{9,8},{10,11... | collective-permute-start | bytes 6291464 | tf_op jit(solution)/shard_map/ppermute | solution.py:1083
  221.7 137.0 %collective-permute-start.2 = (bf16[512,1024]{1,0:T(8,128)(2,1)}, bf16[512,1024]{1,0:T(8,128)(2,1)S(1)}, u32[]{:S(2)}, u32[]{:S(2)}) collective-permute-start(bf16[512,1024]{1,0:T(8,128)(2,1)} %param.27), channel_id=1, source_target_pairs={{0,1},{1,0},{2,3},{3,2},{4,5},{5,4},{6,7},{7,6},{8,9},{9,8},{10,11... | collective-permute-start | bytes 3145736 | tf_op jit(solution)/shard_map/ppermute | solution.py:1083
  223.7 85.5 %collective-permute-start.3 = (bf16[2048]{0:T(1024)(128)(2,1)S(1)}, bf16[2048]{0:T(1024)(128)(2,1)S(1)}, u32[]{:S(2)}, u32[]{:S(2)}) collective-permute-start(bf16[2048]{0:T(1024)(128)(2,1)S(1)} %copy-done.33), channel_id=1, source_target_pairs={{0,1},{1,0},{2,3},{3,2},{4,5},{5,4},{6,7},{7,6},{8,9},{9,8},{10,11... | collective-permute-start | bytes 12296 | tf_op jit(solution)/shard_map/ppermute | solution.py:1083
  358.6 7.9 copy-start.21
  497.5 8.2 copy-start.1
  497.5 9.4 copy-start.6
  497.5 9.4 copy-start.32
  526.1 47.4 %collective-permute-start.4 = (bf16[512,2048]{1,0:T(8,128)(2,1)}, bf16[512,2048]{1,0:T(8,128)(2,1)}, u32[]{:S(2)}, u32[]{:S(2)}) collective-permute-start(bf16[512,2048]{1,0:T(8,128)(2,1)} %fusion.3), channel_id=1, source_target_pairs={{0,1},{1,0},{2,3},{3,2},{4,5},{5,4},{6,7},{7,6},{8,9},{9,8},{10,11... | collective-permute-start | bytes 6291464 | tf_op jit(solution)/shard_map/ppermute | solution.py:1083
  799.3 185.0 %all-reduce.4.cloned.1.call-start = ((), (), s32[]{:S(2)}) async-start(), calls=%async_computation.2 | async-start | bytes 9437184 | tf_op jit(solution)/shard_map/psum | solution.py:1179
  799.9 61.7 %copy-start.11 = (bf16[1024,512]{0,1:T(8,128)(2,1)S(1)}, bf16[1024,512]{0,1:T(8,128)(2,1)}, u32[]{:S(2)}) copy-start(bf16[1024,512]{0,1:T(8,128)(2,1)} %copy-done.10) | copy-start | bytes 3145732
  799.9 61.7 %copy-start.13 = (bf16[1024,512]{0,1:T(8,128)(2,1)S(1)}, bf16[1024,512]{0,1:T(8,128)(2,1)}, u32[]{:S(2)}) copy-start(bf16[1024,512]{0,1:T(8,128)(2,1)} %copy-done.12) | copy-start | bytes 3145732
  799.9 61.7 %copy-start.15 = (bf16[1024,512]{0,1:T(8,128)(2,1)S(1)}, bf16[1024,512]{0,1:T(8,128)(2,1)}, u32[]{:S(2)}) copy-start(bf16[1024,512]{0,1:T(8,128)(2,1)} %copy-done.14) | copy-start | bytes 3145732
  861.7 25.7 %copy-start.29 = (f32[1,1,2048]{2,1,0:T(1,128)S(1)}, f32[1,1,2048]{2,1,0:T(1,128)}, u32[]{:S(2)}) copy-start(f32[1,1,2048]{2,1,0:T(1,128)} %get-tuple-element.88) | copy-start | bytes 24580
  861.7 25.6 %copy-start.30 = (f32[1,1,2048]{2,1,0:T(1,128)S(1)}, f32[1,1,2048]{2,1,0:T(1,128)}, u32[]{:S(2)}) copy-start(f32[1,1,2048]{2,1,0:T(1,128)} %get-tuple-element.89) | copy-start | bytes 24580
  872.9 160.3 %collective-permute-start.5 = (bf16[2048,1024]{1,0:T(8,128)(2,1)}, bf16[2048,1024]{1,0:T(8,128)(2,1)}, u32[]{:S(2)}, u32[]{:S(2)}) collective-permute-start(bf16[2048,1024]{1,0:T(8,128)(2,1)} %convolution_convert_fusion), channel_id=1, source_target_pairs={{0,1},{1,0},{2,3},{3,2},{4,5},{5,4},{6,7},{7,6},{8,9},{9,8},{10,11... | collective-permute-start | bytes 12582920 | tf_op jit(solution)/shard_map/ppermute | solution.py:1083
  936.1 97.1 %copy-start.20 = (f32[2048]{0:T(1024)S(1)}, f32[2048]{0:T(1024)}, u32[]{:S(2)}) copy-start(f32[2048]{0:T(1024)} %copy-done.19) | copy-start | bytes 24580
  936.1 97.1 %copy-start.28 = (f32[1024]{0:T(1024)S(1)}, f32[1024]{0:T(1024)}, u32[]{:S(2)}) copy-start(f32[1024]{0:T(1024)} %param.23) | copy-start | bytes 12292
  1033.2 16.4 %copy-start.23 = (f32[2048]{0:T(1024)S(1)}, f32[2048]{0:T(1024)}, u32[]{:S(2)}) copy-start(f32[2048]{0:T(1024)} %get-tuple-element.118) | copy-start | bytes 24580
  1049.5 246.1 %collective-permute-start.6 = (bf16[2304,1024]{1,0:T(8,128)(2,1)}, bf16[2304,1024]{1,0:T(8,128)(2,1)}, u32[]{:S(2)}, u32[]{:S(2)}) collective-permute-start(bf16[2304,1024]{1,0:T(8,128)(2,1)} %all-reduce.4.cloned.1.call-done.refs_10_.refs_4_.own_ref), channel_id=1, source_target_pairs={{0,2},{2,0},{1,3},{3,1},{4,6},{6,4},{5,7},{7,5},{8,10},{10,8},{9,1... | collective-permute-start | bytes 14155784 | tf_op jit(solution)/shard_map/ppermute | solution.py:1212
  1180.5 110.3 %all-reduce.6.cloned.1.call-start = ((), (), s32[]{:S(2)}) async-start(), calls=%async_computation.3 | async-start | bytes 6291456 | tf_op jit(solution)/shard_map/psum | solution.py:1211
  (16 other events, 76.8 us)
Sparse Core Ops, SparseCore 0:
  123.2 59.7 all-gather.4
  185.2 75.9 all-gather.6
  582.2 139.6 reduce-scatter.1
  803.9 180.3 all-reduce.3
  1185.5 105.1 all-reduce.5

commit v2 on v1

--- a/solution.py
+++ b/solution.py
@@ -66,7 +66,7 @@
 
 
 def cost(flops, moved):
-    return pl.CostEstimate(flops=flops // 8, bytes_accessed=moved // 8, transcendentals=0)
+    return pl.CostEstimate(flops=flops // 64, bytes_accessed=moved // 64, transcendentals=0)
 
 
 def project_kernel(x_ref, w_ref, cos_ref, sin_ref, q_ref, k_ref, v_ref):
@@ -471,19 +471,15 @@
     return found
 
 
-def half_back_kernel(near_only, ends_ref, part_ref, *refs):
+def half_back_kernel(near_only, given_partial, finish, ends_ref, part_ref, *refs):
     refs = list(refs)
     sides = (0,) if near_only else (0, 1)
     given = {side: [refs.pop(0) for _ in range(8)] for side in sides}
-    if near_only:
-        partial_ref = refs.pop(0)
-        while len(refs) > 1 + 7:
-            refs.pop(0)
-        out_ref = refs.pop(0)
-    else:
-        while len(refs) > 2 + 7:
-            refs.pop(0)
-        out_ref, partial_ref = refs.pop(0), refs.pop(0)
+    partial_in = refs.pop(0) if given_partial else None
+    while len(refs) > (1 if near_only else 2) + 7:
+        refs.pop(0)
+    out_ref = None if near_only else refs.pop(0)
+    near_ref = refs.pop(0)
     kaug, vaug, qaug, gaug, pair, dq, sums = refs
     rank = part_ref[0]
     half = given[0][0].shape[1]
@@ -519,11 +515,11 @@
         gaug[:HEAD_DIM, there] = g
         gaug[HEAD_DIM : HEAD_DIM + SEGS, there] = split3(-delta).astype(BF)
         pair[there, :] = jnp.concatenate([q, g], 0).T
-    if near_only:
-        dq[...] = partial_ref[0, 0]
-        sums[...] = partial_ref[1:, 0]
+    dq[...] = jnp.zeros_like(dq)
+    if given_partial:
+        dq[:, :half] = partial_in[0, 0]
+        sums[...] = partial_in[1:, 0]
     else:
-        dq[...] = jnp.zeros_like(dq)
         sums[...] = jnp.zeros_like(sums)
 
     def chunk(side, k0, n, queries):
@@ -538,14 +534,11 @@
             dv = dv + dot(probs.astype(BF), pair[there, HEAD_DIM:])
             dk = dk + dot(tilt, pair[there, :HEAD_DIM])
             dq[:, there] += dot(kt, tilt)
-        if side == 0 and not near_only:
-            sums[0, :, pl.ds(k0, n)] = dk.T
-            sums[1, :, pl.ds(k0, n)] = dv.T
+        dk, dv = dk.T, dv.T
+        if side == 0:
+            sums[0, :, pl.ds(k0, n)] += dk
+            sums[1, :, pl.ds(k0, n)] += dv
             return
-        dk, dv = dk.T, dv.T
-        if near_only:
-            dk = dk + sums[0, :, pl.ds(k0, n)]
-            dv = dv + sums[1, :, pl.ds(k0, n)]
         c, s = given[side][6][:, pl.ds(k0, n)], given[side][7][:, pl.ds(k0, n)]
         out_ref[1, 0, :, pl.ds(k0, n)] = turn_back(dk, c, s, LN2)
         out_ref[2, 0, :, pl.ds(k0, n)] = dv.astype(BF)
@@ -574,20 +567,22 @@
 
                     lax.fori_loop(0, total // n, step, 0)
 
-    if near_only:
+    if not near_only:
+        out_ref[0, 0] = turn_back(dq[:, half:], given[1][6][...], given[1][7][...], 0.125)
+    if finish:
         c, s = given[0][6][...], given[0][7][...]
-        out_ref[0, 0] = turn_back(dq[...], c, s, 0.125)
+        near_ref[0, 0] = turn_back(dq[:, :half], c, s, 0.125)
+        near_ref[1, 0] = turn_back(sums[0], c, s, LN2)
+        near_ref[2, 0] = sums[1].astype(BF)
     else:
-        c, s = given[1][6][...], given[1][7][...]
-        out_ref[0, 0] = turn_back(dq[:, half:], c, s, 0.125)
-        partial_ref[0, 0] = dq[:, :half]
-        partial_ref[1:, 0] = sums[...]
-
-
-def half_back(name, ends, rank, sides, first, count, partial=None, written=(), after=None):
+        near_ref[0, 0] = dq[:, :half]
+        near_ref[1:, 0] = sums[...]
+
+
+def half_back(name, ends, rank, sides, first, count, finish, partial=None, written=(), after=None):
     rows, half = sides[0][0].shape
     heads = rows // HEAD_DIM
-    near_only = partial is not None
+    near_only = len(sides) == 1
     head = pl.BlockSpec((HEAD_DIM, half), lambda h, e, r: (h + first, 0))
     line = pl.BlockSpec((1, 1, half), lambda h, e, r: (h + first, 0, 0))
     table = pl.BlockSpec((HALF, half), lambda h, e, r: (0, 0))
@@ -598,20 +593,24 @@
         operands += list(side)
         specs += [head] * 5 + [line, table, table]
     result = jax.ShapeDtypeStruct((3, heads, HEAD_DIM, half), BF)
-    if near_only:
+    if partial is not None:
         operands.append(partial)
         specs.append(block)
-    aliases = {2 + len(operands) + i: i for i in range(len(written))}
-    operands += list(written)
-    specs += [anywhere] * len(written)
+    aliases = {}
+    for i, array in enumerate(written):
+        if array is not None:
+            aliases[2 + len(operands)] = i
+            operands.append(array)
+            specs.append(anywhere)
     if after is not None:
         operands.append(after)
         specs.append(anywhere)
-    out_specs = [block] if near_only else [block, block]
-    out_shape = [result, jax.ShapeDtypeStruct(result.shape, F32)][: len(out_specs)]
+    near_result = result if finish else jax.ShapeDtypeStruct(result.shape, F32)
+    out_shape = [near_result] if near_only else [result, near_result]
+    out_specs = [block] * len(out_shape)
     wide = half * len(sides)
     return pl.pallas_call(
-        functools.partial(half_back_kernel, near_only),
+        functools.partial(half_back_kernel, near_only, partial is not None, finish),
         grid_spec=pltpu.PrefetchScalarGridSpec(
             num_scalar_prefetch=2,
             grid=(count,),
@@ -761,11 +760,11 @@
     )(src, dst, *operands)
 
 
-def out_back_kernel(mixed_ref, grad_ref, sums_ref, after_ref, out_ref):
+def out_back_kernel(mixed_ref, grad_ref, sums_ref, out_ref):
     out_ref[0, 0] = dot(mixed_ref[...], grad_ref[...]).astype(BF)
 
 
-def out_back(mixed_rows, grad, sums, extra, after):
+def out_back(mixed_rows, grad, sums, extra):
     heads, rows = mixed_rows.shape
     _, parts, total, depth = sums.shape
     return pl.pallas_call(
@@ -775,7 +774,6 @@
             pl.BlockSpec((extra, rows), lambda p, c: (2 * p + c, 0)),
             pl.BlockSpec((rows, depth), lambda p, c: (0, 0)),
             pl.BlockSpec(memory_space=pl.ANY),
-            pl.BlockSpec(memory_space=pl.ANY),
         ],
         out_specs=pl.BlockSpec((1, 1, extra, depth), lambda p, c: (c, p, total // extra - 1, 0)),
         out_shape=jax.ShapeDtypeStruct(sums.shape, BF),
@@ -783,7 +781,7 @@
         compiler_params=params(),
         name="out_back",
         cost_estimate=cost(2 * rows * depth * heads, 2 * heads * depth),
-    )(mixed_rows, grad, sums, after)
+    )(mixed_rows, grad, sums)
 
 
 def project_back_kernel(*refs):
@@ -792,7 +790,7 @@
     total = dot(pairs[1][...], pairs[0][...])
     for i in range(2, len(pairs), 2):
         total = total + dot(pairs[i + 1][...], pairs[i][...])
-    out_ref[...] = total.T.astype(BF)
+    out_ref[...] = total.astype(BF)
 
 
 def project_back(pairs, after):
@@ -810,169 +808,236 @@
         project_back_kernel,
         grid=(3,),
         in_specs=specs + [pl.BlockSpec(memory_space=pl.ANY)],
-        out_specs=pl.BlockSpec((depth, block), lambda i: (0, i)),
-        out_shape=jax.ShapeDtypeStruct((depth, total), BF),
+        out_specs=pl.BlockSpec((block, depth), lambda i: (i, 0)),
+        out_shape=jax.ShapeDtypeStruct((total, depth), BF),
         compiler_params=params(),
         name="project_back",
         cost_estimate=cost(4 * pairs[0][0].shape[0] * depth * total, 8 * depth * total),
     )(*operands, after)
 
 
+def turn_kernel(x_ref, *out_refs):
+    for i, out_ref in enumerate(out_refs):
+
+        @pl.when(pl.program_id(0) == i)
+        def _():
+            out_ref[...] = x_ref[...].astype(F32).T
+
+
+def turn(x, parts):
+    rows, depth = x.shape
+    block = rows // parts
+    return pl.pallas_call(
+        turn_kernel,
+        grid=(parts,),
+        in_specs=[pl.BlockSpec((block, depth), lambda i: (i, 0))],
+        out_specs=[pl.BlockSpec((depth, block), lambda i: (0, 0))] * parts,
+        out_shape=[jax.ShapeDtypeStruct((depth, block), F32)] * parts,
+        compiler_params=params(),
+        name="turn",
+        cost_estimate=cost(rows * depth, 6 * rows * depth),
+    )(x)
+
+
 MESH = pl.DeviceIdType.MESH
 
 
 def sum_all_kernel(
-    big_ref, small_ref, after_ref, out_ref, small_out_ref,
-    buf, done, core_in, x_in, y_in, z_in, small, small_in, small_z, local, send, recv, small_send, small_recv,
+    big_ref, side_ref, small_ref, out_ref, side_out_ref, small_out_ref,
+    buf, done, core_in, x_in, y_in, z_in, side, side_done, side_core, side_y, side_z,
+    small, small_in, small_z, local, send, recv, side_send, side_recv, small_send, small_recv,
 ):
     o, c, m = lax.axis_index("dpo"), lax.axis_index("core"), lax.axis_index("mp")
     y, z = lax.rem(o, 2), lax.div(o, 2)
     zs = 4
     half = buf.shape[0] // 2
     quarter, eighth, last = half // 2, half // 4, half // 16
+    side_half = side.shape[0] // 2
+    side_quarter, side_last = side_half // 2, side_half // 8
     sibling = (o, 1 - c, m)
     across = (o, c, 1 - m)
     beside = (z * 2 + 1 - y, c, m)
+    others = [lax.rem(z + d, zs) for d in range(1, zs)]
 
     def along(j):
         return (j * 2 + y, c, m)
 
-    load = pltpu.make_async_copy(big_ref, buf, local.at[0])
-    load.start()
+    loads = [
+        pltpu.make_async_copy(big_ref, buf, local.at[0]),
+        pltpu.make_async_copy(side_ref, side, local.at[1]),
+    ]
+    for load in loads:
+        load.start()
     barrier = pltpu.get_barrier_semaphore()
-    others = [lax.rem(z + d, zs) for d in range(1, zs)]
     for device in [sibling, across, beside] + [along(j) for j in others]:
         pl.semaphore_signal(barrier, inc=1, device_id=device, device_id_type=MESH)
     pl.semaphore_wait(barrier, 6)
     small[0] = small_ref[...]
-    load.wait()
-
-    def copy(src, dst, i, device, sems=(send, recv)):
-        return pltpu.make_async_remote_copy(
+
+    started = []
+
+    def go(src, dst, sems, i, device):
+        one = pltpu.make_async_remote_copy(
             src_ref=src, dst_ref=dst, send_sem=sems[0].at[i], recv_sem=sems[1].at[i],
             device_id=device, device_id_type=MESH,
         )
-
-    def rows(first, n, of=buf):
-        return of.at[pl.ds(pl.multiple_of(first, last), n)]
-
-    def back(first, n, i, device):
-        return copy(rows(first, n, done), rows(first, n, done), i, device)
-
-    def add(first, n, arrived):
-        step = min(128, n)
-
-        def one(i, carry):
-            there = pl.ds(pl.multiple_of(first + i * step, last), step)
-            here = pl.ds(pl.multiple_of(i * step, step), step)
-            buf[there, :] = (
-                buf[there, :].astype(F32) + arrived[here, :].astype(F32)
-            ).astype(BF)
-            return carry
-
-        lax.fori_loop(0, n // step, one, 0)
-
-    started = []
-
-    def go(*args, **kwargs):
-        one = copy(*args, **kwargs)
         one.start()
         started.append(one)
         return one
 
-    tiny = (small_send, small_recv)
-    mine = c * half
-    theirs = (1 - c) * half
-    core_a = go(rows(theirs + (1 - m) * quarter, quarter), core_in.at[0], 0, sibling)
-    core_b = go(rows(theirs + m * quarter, quarter), core_in.at[1], 1, sibling)
-    tiny_core = go(small.at[0], small_in.at[0], 0, sibling, sems=tiny)
+    def arrived(dst, sems, i, device):
+        pltpu.make_async_remote_copy(
+            src_ref=dst, dst_ref=dst, send_sem=sems[0].at[i], recv_sem=sems[1].at[i],
+            device_id=device, device_id_type=MESH,
+        ).wait_recv()
+
+    def view(of, first, n, unit):
+        return of.at[pl.ds(pl.multiple_of(first, unit), n)]
+
+    def rows(first, n, of=buf):
+        return view(of, first, n, last)
+
+    def side_rows(first, n, of=side):
+        return view(of, first, n, side_last)
+
+    def add(of, first, n, unit, got):
+        step = unit if n % 128 or 128 % unit else 128
+
+        def one(i, carry):
+            there = pl.ds(pl.multiple_of(first + i * step, unit), step)
+            here = pl.ds(pl.multiple_of(i * step, step), step)
+            of[there, :] = (of[there, :].astype(F32) + got[here, :].astype(F32)).astype(BF)
+            return carry
+
+        lax.fori_loop(0, n // step, one, 0)
+
+    main, extra, tiny = (send, recv), (side_send, side_recv), (small_send, small_recv)
+    mine, theirs = c * half, (1 - c) * half
+    side_mine, side_theirs = c * side_half, (1 - c) * side_half
     base_far, base = mine + (1 - m) * quarter, mine + m * quarter
+    far_y, near_y = base + (1 - y) * eighth, base + y * eighth
+    side_far, side_near = side_mine + (1 - y) * side_quarter, side_mine + y * side_quarter
+    own, side_own = near_y + z * last, side_near + z * side_last
+
+    loads[0].wait()
+    core_a = go(rows(theirs + (1 - m) * quarter, quarter), core_in.at[0], main, 0, sibling)
+    loads[1].wait()
+    side_a = go(
+        side_rows(side_theirs + (1 - y) * side_quarter, side_quarter), side_core.at[0], extra, 0,
+        sibling,
+    )
+    core_b = go(rows(theirs + m * quarter, quarter), core_in.at[1], main, 1, sibling)
+    side_b = go(
+        side_rows(side_theirs + y * side_quarter, side_quarter), side_core.at[1], extra, 1, sibling
+    )
+    tiny_core = go(small.at[0], small_in.at[0], tiny, 0, sibling)
     core_a.wait_recv()
-    add(base_far, quarter, core_in.at[0])
-    x_a = go(rows(base_far + (1 - y) * eighth, eighth), x_in.at[0], 2, across)
-    x_b = go(rows(base_far + y * eighth, eighth), x_in.at[1], 3, across)
+    add(buf, base_far, quarter, last, core_in.at[0])
+    x_a = go(rows(base_far + (1 - y) * eighth, eighth), x_in.at[0], main, 2, across)
+    x_b = go(rows(base_far + y * eighth, eighth), x_in.at[1], main, 3, across)
+    side_a.wait_recv()
+    add(side, side_far, side_quarter, side_last, side_core.at[0])
+    side_c = go(side_rows(side_far, side_quarter), side_y, extra, 2, beside)
     tiny_core.wait_recv()
     small[1] = small[0] + small_in[0]
-    tiny_x = go(small.at[1], small_in.at[1], 1, across, sems=tiny)
+    tiny_x = go(small.at[1], small_in.at[1], tiny, 1, across)
     core_b.wait_recv()
-    add(base, quarter, core_in.at[1])
-    far_y, near_y = base + (1 - y) * eighth, base + y * eighth
+    add(buf, base, quarter, last, core_in.at[1])
+    side_b.wait_recv()
+    add(side, side_near, side_quarter, side_last, side_core.at[1])
     x_a.wait_recv()
-    add(far_y, eighth, x_in.at[0])
-    y_a = go(rows(far_y, eighth), y_in, 4, beside)
+    add(buf, far_y, eighth, last, x_in.at[0])
+    y_a = go(rows(far_y, eighth), y_in, main, 4, beside)
     tiny_x.wait_recv()
     small[2] = small[1] + small_in[1]
-    tiny_y = go(small.at[2], small_in.at[2], 2, beside, sems=tiny)
+    tiny_y = go(small.at[2], small_in.at[2], tiny, 2, beside)
+    side_c.wait_recv()
+    add(side, side_near, side_quarter, side_last, side_y)
+    for j in others:
+        go(side_rows(side_near + j * side_last, side_last), side_z.at[z], extra, 3 + z, along(j))
     x_b.wait_recv()
-    add(near_y, eighth, x_in.at[1])
+    add(buf, near_y, eighth, last, x_in.at[1])
     y_a.wait_recv()
-    add(near_y, eighth, y_in)
-    for d in range(1, zs):
-        j = lax.rem(z + d, zs)
-        there = copy(rows(near_y + j * last, last), z_in.at[z], 5 + z, along(j))
-        there.start()
-        started.append(there)
+    add(buf, near_y, eighth, last, y_in)
+    for j in others:
+        go(rows(near_y + j * last, last), z_in.at[z], main, 5 + z, along(j))
     tiny_y.wait_recv()
     small_z[z] = small[2] + small_in[2]
-    for d in range(1, zs):
-        j = lax.rem(z + d, zs)
-        there = copy(small_z.at[z], small_z.at[z], 3 + z, along(j), sems=tiny)
-        there.start()
-        started.append(there)
-    own = near_y + z * last
+    for j in others:
+        go(small_z.at[z], small_z.at[z], tiny, 3 + z, along(j))
+    total = side[pl.ds(pl.multiple_of(side_own, side_last), side_last), :].astype(F32)
+    for j in others:
+        arrived(side_z.at[j], extra, 3 + j, along(j))
+        total = total + side_z[j].astype(F32)
+    side_done[pl.ds(pl.multiple_of(side_own, side_last), side_last), :] = total.astype(BF)
+
+    def hand(first, n, i, device):
+        there = rows(first, n, done)
+        return go(there, there, main, i, device)
+
+    def side_hand(first, n, i, device):
+        there = side_rows(first, n, side_done)
+        return go(there, there, extra, i, device)
+
+    for j in others:
+        side_hand(side_own, side_last, 7 + z, along(j))
     total = buf[pl.ds(pl.multiple_of(own, last), last), :].astype(F32)
-    for d in range(1, zs):
-        j = lax.rem(z + d, zs)
-        copy(rows(own, last), z_in.at[j], 5 + j, along(j)).wait_recv()
+    for j in others:
+        arrived(z_in.at[j], main, 5 + j, along(j))
         total = total + z_in[j].astype(F32)
     done[pl.ds(pl.multiple_of(own, last), last), :] = total.astype(BF)
-
-    def hand(first, n, i, device):
-        one = back(first, n, i, device)
-        one.start()
-        started.append(one)
-        return one
-
-    for d in range(1, zs):
-        hand(own, last, 9 + z, along(lax.rem(z + d, zs)))
-    for d in range(1, zs):
-        j = lax.rem(z + d, zs)
-        back(near_y + j * last, last, 9 + j, along(j)).wait_recv()
+    for j in others:
+        hand(own, last, 9 + z, along(j))
+    for j in others:
+        arrived(rows(near_y + j * last, last, done), main, 9 + j, along(j))
+    x_back = hand(near_y, eighth, 14, across)
     y_back = hand(near_y, eighth, 13, beside)
-    x_back = hand(near_y, eighth, 14, across)
     core_back = hand(near_y, eighth, 15, sibling)
+    for j in others:
+        there = side_rows(side_near + j * side_last, side_last, side_done)
+        arrived(there, extra, 7 + j, along(j))
+    side_back = side_hand(side_near, side_quarter, 11, beside)
+    side_core_back = side_hand(side_near, side_quarter, 12, sibling)
     y_back.wait_recv()
     x_more = hand(far_y, eighth, 16, across)
     core_more = hand(far_y, eighth, 17, sibling)
     x_back.wait_recv()
     core_x = hand(base_far + y * eighth, eighth, 18, sibling)
+    side_back.wait_recv()
+    side_core_more = side_hand(side_far, side_quarter, 13, sibling)
     x_more.wait_recv()
     core_y = hand(base_far + (1 - y) * eighth, eighth, 19, sibling)
-    for d in range(1, zs):
-        j = lax.rem(z + d, zs)
-        copy(small_z.at[j], small_z.at[j], 3 + j, along(j), sems=tiny).wait_recv()
+    for j in others:
+        arrived(small_z.at[j], tiny, 3 + j, along(j))
     small_out_ref[...] = (small_z[0] + small_z[1]) + (small_z[2] + small_z[3])
+    for one in (side_core_back, side_core_more):
+        one.wait_recv()
+    stores = [pltpu.make_async_copy(side_done, side_out_ref, local.at[1])]
+    stores[0].start()
     for one in (core_back, core_more, core_x, core_y):
         one.wait_recv()
+    stores.append(pltpu.make_async_copy(done, out_ref, local.at[0]))
+    stores[1].start()
     for one in started:
         one.wait_send()
-    store = pltpu.make_async_copy(done, out_ref, local.at[1])
-    store.start()
-    store.wait()
-
-
-def sum_all(big, small, after):
+    for store in stores:
+        store.wait()
+
+
+def sum_all(big, side, small):
     rows, width = big.shape
     quarter, eighth, last = rows // 4, rows // 8, rows // 32
+    side_quarter, side_last = side.shape[0] // 4, side.shape[0] // 16
     anywhere = pl.BlockSpec(memory_space=pl.ANY)
     whole = pl.BlockSpec(memory_space=pltpu.VMEM)
     dma = pltpu.SemaphoreType.DMA
     return pl.pallas_call(
         sum_all_kernel,
-        in_specs=[anywhere, whole, anywhere],
-        out_specs=[anywhere, whole],
+        in_specs=[anywhere, anywhere, whole],
+        out_specs=[anywhere, anywhere, whole],
         out_shape=[
             jax.ShapeDtypeStruct(big.shape, BF),
+            jax.ShapeDtypeStruct(side.shape, BF),
             jax.ShapeDtypeStruct(small.shape, F32),
         ],
         scratch_shapes=[
@@ -982,12 +1047,19 @@
             pltpu.VMEM((2, eighth, width), BF),
             pltpu.VMEM((eighth, width), BF),
             pltpu.VMEM((4, last, width), BF),
+            pltpu.VMEM(side.shape, BF),
+            pltpu.VMEM(side.shape, BF),
+            pltpu.VMEM((2, side_quarter, width), BF),
+            pltpu.VMEM((side_quarter, width), BF),
+            pltpu.VMEM((4, side_last, width), BF),
             pltpu.VMEM((3,) + small.shape, F32),
             pltpu.VMEM((3,) + small.shape, F32),
             pltpu.VMEM((4,) + small.shape, F32),
             dma((2,)),
             dma((20,)),
             dma((20,)),
+            dma((14,)),
+            dma((14,)),
             dma((7,)),
             dma((7,)),
         ],
@@ -996,7 +1068,7 @@
         ),
         name="sum_all",
         cost_estimate=cost(rows * width, 8 * rows * width),
-    )(big, small, after)
+    )(big, side, small)
 
 
 def join_back_kernel(grad_ref, w_ref, first_ref, second_ref):
@@ -1094,7 +1166,12 @@
     h0 = dot(joined, w_concat) + b_concat
     scale_one = lax.rsqrt(jnp.mean(h0 * h0, axis=-1, keepdims=True) + EPS)
     n1 = (h0 * scale_one * gain_attn).astype(BF)
-    n1_far = across(n1) if paired else lax.all_gather(n1, "mp", axis=0, tiled=True)
+    if paired:
+        bias_far, out_far = across(b_up), across(w_out)
+        n1, bias_far, out_far = lax.optimization_barrier((n1, bias_far, out_far))
+        n1_far = across(n1)
+    else:
+        n1_far = lax.all_gather(n1, "mp", axis=0, tiled=True)
     def gather(w):
         half = w.shape[0] // 2
         return lax.all_gather(piece(w, core, half), ("core", "mp"), axis=0).reshape(
@@ -1104,8 +1181,6 @@
     w_qkv = jnp.concatenate([w_query, w_key, w_value], axis=1)
     w_turned = w_qkv.T
     if paired:
-        bias_far = across(b_up)
-        out_far = across(w_out)
         tables_near = tables(piece(pos_all, rank, rows))
         q_near, k_near, v_near = project(n1, w_turned, *tables_near)
         start = attend_half(
@@ -1166,12 +1241,11 @@
     if paired:
         grad_far = across(dot_nt(out_far, grad_h1_low).astype(BF))
         grad_near = dot_nt(w_out, grad_h1_low).astype(BF)
-        landed = grad_far
     else:
-        landed = grad_mixed = lax.all_to_all(
+        grad_mixed = lax.all_to_all(
             dot_nt(w_out_all, grad_h1_low).astype(BF), "mp", 0, 1, tiled=True
         )
-    sums = out_back(mixed_rows, grad_h1_low, sums, extra, landed)
+    sums = out_back(mixed_rows, grad_h1_low, sums, extra)
     small = [jnp.sum(grad_rows, 0), grad_gain_ffn, jnp.sum(grad_h1, 0)]
     part = lax.psum_scatter(
         sums.reshape((2 * parts,) + sums.shape[2:]), ("core", "mp"), scatter_dimension=0, tiled=True
@@ -1182,24 +1256,31 @@
         near = (q_near, k_near, v_near, grad_near, mixed_near, log_near) + tables_near
         far = (q_far, k_far, v_far, grad_far, mixed_far, log_far) + tables_far
         heads = each // HEAD_DIM
-        calls = 4
-        step = heads // calls
-        written = ()
-        for i in range(calls):
-            written = half_back(
-                f"back_far{i}", ends, index, (near, far), i * step, step, written=written,
-                after=part if i == calls // 2 else None,
+        back = functools.partial(half_back, ends=ends, rank=index)
+        both = (near, far)
+        middle = heads // 2
+        opening = back("back_near0", sides=(near,), first=0, count=middle, finish=False)[0]
+        written, at = (), 0
+        for i, count in enumerate((middle // 2, middle // 4, middle - middle // 2 - middle // 4)):
+            written = back(
+                f"back_first{i}", sides=both, first=at, count=count, finish=True,
+                partial=opening, written=written, after=part if i == 2 else None,
             )
-        back_far, partial = written
+            at += count
+        back_far, back_near = written
+        partial = None
+        for i in range(2):
+            back_far, partial = back(
+                f"back_second{i}", sides=both, first=at, count=middle // 2, finish=False,
+                written=(back_far, partial),
+            )
+            at += middle // 2
         back_far = back_far.reshape(3 * each, rows)
         sent = across(dot(back_far, w_qkv, ((0,), (1,))).astype(BF))
-        written = ()
-        for i in range(2):
-            written = half_back(
-                f"back_near{i}", ends, index, (near,), i * heads // 2, heads // 2,
-                partial=partial, written=written, after=summed if i else None,
-            )
-        back_near = written[0].reshape(3 * each, rows)
+        back_near = back(
+            "back_near1", sides=(near,), first=middle, count=heads - middle, finish=True,
+            partial=partial, written=(back_near,),
+        )[0].reshape(3 * each, rows)
         grad_n1 = dot(back_near, w_qkv, ((0,), (1,))) + sent.astype(F32)
         pairs = [(n1, back_near), (n1_far, back_far)]
     else:
@@ -1207,8 +1288,6 @@
         grad_n1 = dot(back, w_qkv, ((0,), (1,))).astype(BF)
         grad_n1 = lax.psum_scatter(grad_n1, "mp", scatter_dimension=0, tiled=True).astype(F32)
         pairs = [(n1_far, back)]
-    turned = project_back(pairs, summed)
-    grad_qkv = lax.psum(turned, dp).astype(F32)
     sibling = lax.ppermute(summed, "core", [(0, 1), (1, 0)])
     grad_up, grad_down = unpack(core.reshape(1), summed, sibling, hidden)
     own_out, sibling_out = summed[hidden:].astype(F32), sibling[hidden:].astype(F32)
@@ -1218,6 +1297,8 @@
         jnp.concatenate([sibling_out, own_out]),
     )
 
+    grad_qkv = project_back(pairs, grad_up)
+
     grad_h0, grad_gain_attn = norm_back(grad_n1, h0, scale_one, gain_attn)
     grad_h0_low = (grad_h0 + grad_h1).astype(BF)
     grad_w_concat = dot_tn(joined, grad_h0_low).astype(BF)
@@ -1225,11 +1306,12 @@
     small = jnp.concatenate(small + [grad_bias.reshape(-1)]).reshape(-1, width)
     small = jnp.pad(small, ((0, -small.shape[0] % 8), (0, 0)))
     if paired and lax.axis_size("dpo") == 8:
-        tail, small = sum_all(grad_w_concat, small, turned)
+        tail, grad_qkv, small = sum_all(grad_w_concat, grad_qkv, small)
     else:
         tail, small = lax.psum((grad_w_concat, small), dp + ("mp",))
+        grad_qkv = lax.psum(grad_qkv, dp)
     grad_inputs, grad_skip = join_back(grad_h0_low, w_concat)
-    wide = w_query.shape[1]
+    grad_query, grad_key, grad_value = turn(grad_qkv, 3)
     return (
         output,
         grad_inputs,
@@ -1237,9 +1319,9 @@
         tail.astype(F32),
         small[3],
         small[4],
-        grad_qkv[:, :wide],
-        grad_qkv[:, wide : 2 * wide],
-        grad_qkv[:, 2 * wide :],
+        grad_query,
+        grad_key,
+        grad_value,
         grad_out,
         small[2],
         small[1],

time: 1320 us -> 1170 us (0.89)
  waiting for transfers between devices: 284 us -> 90.1 us
  Pallas kernels: 833 us -> 884 us
    psum x1 -> x0, waiting for transfers between devices: 86.3 us -> none  [body(): grad_qkv = lax.psum(turned, dp).astype(F32)]
    ppermute x6, waiting for transfers between devices: 148 us -> 89.5 us  [across(): return lax.ppermute(x, 'mp', [(0, 1), (1, 0)])]
    pallas_call x7 -> x9, Pallas kernels: 458 us -> 509 us  [the longest x7 373 us: half_back(): pl.pallas_call(functools.partial(half_back_kernel, near_only, partial is...]
    psum x1, waiting for transfers between devices: 48.2 us -> 0.01 us  [body(): summed = lax.psum(part, 'dpo')]
  transfers between devices with their start and end apart: 12 -> 11, of which waited for: 5 -> 5; matrix products, arithmetic and copies ran while one was open for 7% -> 10% of each run, Pallas kernels for 51% -> 53%
where the time goes in v2:
time: 1170 us; the launch traced here: 1160 us
  Pallas kernels  884 us (76%)
  waiting for transfers between devices  90.1 us (8%)
  matrix products  73 us (6%)
  other arithmetic  63.7 us (5%)
  local copies, waits for them, and re-layouts  26.2 us (2%)
  between operations  14.6 us (1%)
    pallas_call x7, Pallas kernels, half_back(): pl.pallas_call(functools.partial(half_back_kernel, near_only, partial is...  373 us
    pallas_call x3, Pallas kernels, attend_half(): pl.pallas_call(functools.partial(half_kernel, query_far, sides, carry is...  172 us
    pallas_call x1, Pallas kernels, sum_all(): pl.pallas_call(sum_all_kernel, in_specs=[anywhere, anywhere, whole], out_...  130 us
    pallas_call x2, Pallas kernels, ffn(): pl.pallas_call(functools.partial(ffn_kernel, step, before is not None), g...  126 us
    ppermute x6, waiting for transfers between devices, across(): return lax.ppermute(x, 'mp', [(0, 1), (1, 0)])  89.5 us
    dot_general x8, matrix products, dot(): lax.dot_general(left, right, (dims, ((), ())), preferred_element_type=F32)  73 us
  transfers between devices with their start and end apart: 11, of which 5 were waited for; matrix products, arithmetic and copies ran while one was open for 10% of the time, Pallas kernels for 53%

profile of v2, /device:TPU:0, one launch (start us, length us, event | category | flops | bytes accessed | tf_op | source)
XLA Modules:
  0.0 1162.1 jit_solution(11372177881158452527)
XLA Ops:
  13.7 9.3 multiply_reduce_fusion.5
  43.6 11.3 project.2
  54.9 44.0 %near_near.1 = (f32[8,80,2048]{2,1,0:T(8,128)}, f32[8,1,2048]{2,1,0:T(1,128)}) custom-call(s32[8]{0:T(128)} %bitcast.63, s32[1]{0:T(128)} %bitcast.3.part_ref.dst_ref, bf16[512,2048]{1,0:T(8,128)(2,1)} %get-tuple-element.65.refs_0_, bf16[512,2048]{1,0:T(8,128)(2,1)} %get-tuple-element.66.refs_1_, bf16[512,2048]{1,0:T(8,128)(2,1)} %get-tuple-element.67.refs_2_), custom_call_target="tpu_custom_call" | custom-call | flops 536870912 | bytes 131072 | tf_op jit(solution)/shard_map/near_near/pallas_call | solution.py:322
  98.9 27.0 %collective-permute-done.2.x_ref.refs_2_ = bf16[2048,1024]{1,0:T(8,128)(2,1)} collective-permute-done((bf16[2048,1024]{1,0:T(8,128)(2,1)}, bf16[2048,1024]{1,0:T(8,128)(2,1)}, u32[]{:S(2)}, u32[]{:S(2)}) %collective-permute-start.2) | collective-permute-done | bytes 4194336 | tf_op jit(solution)/shard_map/ppermute | solution.py:1155
  132.3 11.3 project.3
  143.6 84.0 %far_all.1 = (bf16[512,2048]{1,0:T(8,128)(2,1)}, f32[8,1,2048]{2,1,0:T(1,128)}) custom-call(s32[8]{0:T(128)} %bitcast.64, s32[1]{0:T(128)} %bitcast.3.part_ref.dst_ref, bf16[512,2048]{1,0:T(8,128)(2,1)} %get-tuple-element.76.refs_0_.refs_8_, bf16[512,2048]{1,0:T(8,128)(2,1)} %get-tuple-element.66.refs_1_, bf16[512,2048]{1,0:T(8,128)(2,1)} %get-tuple-element.67.refs_2_, ...), custom_call_target="tpu_custom_call" | custom-call | flops 1073741824 | bytes 131072 | tf_op jit(solution)/shard_map/far_all/pallas_call | solution.py:322
  235.1 44.5 %near_far.1 = (bf16[512,2048]{1,0:T(8,128)(2,1)}, f32[8,1,2048]{2,1,0:T(1,128)}) custom-call(s32[8]{0:T(128)} %bitcast.65, s32[1]{0:T(128)} %bitcast.3.part_ref.dst_ref, bf16[512,2048]{1,0:T(8,128)(2,1)} %get-tuple-element.65.refs_0_, bf16[512,2048]{1,0:T(8,128)(2,1)} %get-tuple-element.71.refs_1_.refs_3_.refs_9_, ...), custom_call_target="tpu_custom_call" | custom-call | flops 536870912 | bytes 131072 | tf_op jit(solution)/shard_map/near_far/pallas_call | solution.py:322
  283.9 8.4 collective-permute-done.3
  292.3 8.1 multiply_reduce_fusion.4
  305.1 63.3 %ffn_near.1 = (f32[2048,1024]{1,0:T(8,128)}, f32[2048,1024]{1,0:T(8,128)}, bf16[2,2,2304,1024]{3,2,1,0:T(8,128)(2,1)}, f32[1,1,2048]{2,1,0:T(1,128)}) custom-call(s32[1]{0:T(128)} %constant.42.clone.1.src_ref, s32[1]{0:T(128)} %bitcast.3.part_ref.dst_ref, bf16[2048,1024]{1,0:T(8,128)(2,1)} %multiply_convert_fusion.n_ref, bf16[2048,1024]{1,0:T(8,128)(2,1)} %fusion.1.g_ref, ...), custom_call_target="tpu_custom_call" | custom-call | flops 805306368 | bytes 262144 | tf_op jit(solution)/shard_map/ffn_near/pallas_call | solution.py:726
  373.6 63.2 %ffn_far.1 = (f32[2048,1024]{1,0:T(8,128)}, f32[2048,1024]{1,0:T(8,128)}, bf16[2,2,2304,1024]{3,2,1,0:T(8,128)(2,1)}, f32[1,1,2048]{2,1,0:T(1,128)}) custom-call(s32[1]{0:T(128)S(6)} %sub.22.src_ref.dst_ref, s32[1]{0:T(128)S(6)} %sub.22.src_ref.dst_ref, bf16[2048,1024]{1,0:T(8,128)(2,1)} %multiply_convert_fusion.n_ref, ...), custom_call_target="tpu_custom_call", output_to_operand_aliasing={{2}: (9, {})} | custom-call | flops 805306368 | bytes 262144 | tf_op jit(solution)/shard_map/ffn_far/pallas_call | solution.py:726
  436.9 7.5 multiply_reduce_fusion.1
  446.2 11.8 %fusion.6 = (f32[1024]{0:T(1024)S(1)}, f32[2048,1024]{1,0:T(8,128)S(1)}, f32[2048,1024]{1,0:T(8,128)}, f32[1024]{0:T(1024)S(1)}) fusion(f32[2048]{0:T(1024)S(1)} %fusion.3, bf16[2048,1024]{1,0:T(8,128)(2,1)S(1)} %copy-done.6, f32[2048]{0:T(1024)S(1)} %broadcast_multiply_fusion.1, f32[2048,1024]{1,0:T(8,128)} %copy-done, f32[2048]{0:T(1024)S(1)} %get-tuple-element.135, ...), kind=kLoop, calls=%fused_computation.62 | loop fusion | flops 27260928 | bytes 46186496 | tf_op jit(solution)/shard_map/reduce_sum | solution.py:1249
  462.7 8.6 out_back.1
  481.7 49.4 %back_near0.1.refs_16_ = f32[3,8,64,2048]{3,2,1,0:T(8,128)} custom-call(s32[8]{0:T(128)} %bitcast.66, s32[1]{0:T(128)} %bitcast.3.part_ref.dst_ref, bf16[512,2048]{1,0:T(8,128)(2,1)} %get-tuple-element.65.refs_0_, bf16[512,2048]{1,0:T(8,128)(2,1)} %get-tuple-element.66.refs_1_, bf16[512,2048]{1,0:T(8,128)(2,1)} %get-tuple-element.67.refs_2_, ...), custom_call_target="tpu_custom_call" | custom-call | flops 671088640 | bytes 327680 | tf_op jit(solution)/shard_map/back_near0/pallas_call | solution.py:612
  531.1 11.5 collective-permute-done.4.refs_11_
  544.0 62.1 %back_first0.1 = (bf16[3,8,64,2048]{3,2,1,0:T(8,128)(2,1)}, bf16[3,8,64,2048]{3,2,1,0:T(8,128)(2,1)}) custom-call(s32[8]{0:T(128)} %bitcast.67, s32[1]{0:T(128)} %bitcast.3.part_ref.dst_ref, bf16[512,2048]{1,0:T(8,128)(2,1)} %get-tuple-element.65.refs_0_, bf16[512,2048]{1,0:T(8,128)(2,1)} %get-tuple-element.66.refs_1_, ...), custom_call_target="tpu_custom_call" | custom-call | flops 1006632960 | bytes 163840 | tf_op jit(solution)/shard_map/back_first0/pallas_call | solution.py:612
  606.2 33.4 %back_first1.1 = (bf16[3,8,64,2048]{3,2,1,0:T(8,128)(2,1)}, bf16[3,8,64,2048]{3,2,1,0:T(8,128)(2,1)}) custom-call(s32[8]{0:T(128)} %bitcast.68, s32[1]{0:T(128)} %bitcast.3.part_ref.dst_ref, bf16[512,2048]{1,0:T(8,128)(2,1)} %get-tuple-element.65.refs_0_, ...), custom_call_target="tpu_custom_call", output_to_operand_aliasing={{0}: (19, {}), {1}: (20, {})} | custom-call | flops 503316480 | bytes 81920 | tf_op jit(solution)/shard_map/back_first1/pallas_call | solution.py:612
  639.6 33.5 %back_first2.1 = (bf16[3,8,64,2048]{3,2,1,0:T(8,128)(2,1)}, bf16[3,8,64,2048]{3,2,1,0:T(8,128)(2,1)}) custom-call(s32[8]{0:T(128)} %bitcast.69, s32[1]{0:T(128)} %bitcast.3.part_ref.dst_ref, bf16[512,2048]{1,0:T(8,128)(2,1)} %get-tuple-element.65.refs_0_, ...), custom_call_target="tpu_custom_call", output_to_operand_aliasing={{0}: (19, {}), {1}: (20, {})} | custom-call | flops 503316480 | bytes 81920 | tf_op jit(solution)/shard_map/back_first2/pallas_call | solution.py:612
  673.6 70.8 %back_second0.1 = (bf16[3,8,64,2048]{3,2,1,0:T(8,128)(2,1)}, f32[3,8,64,2048]{3,2,1,0:T(8,128)}) custom-call(s32[8]{0:T(128)} %bitcast.70, s32[1]{0:T(128)} %bitcast.3.part_ref.dst_ref, bf16[512,2048]{1,0:T(8,128)(2,1)} %get-tuple-element.65.refs_0_, bf16[512,2048]{1,0:T(8,128)(2,1)} %get-tuple-element.66.refs_1_, ...), custom_call_target="tpu_custom_call", output_to_operand_aliasing={{0}: (18, {})} | custom-call | flops 1006632960 | bytes 163840 | tf_op jit(solution)/shard_map/back_second0/pallas_call | solution.py:612
  744.5 74.2 %back_second1.1 = (bf16[3,8,64,2048]{3,2,1,0:T(8,128)(2,1)}, f32[3,8,64,2048]{3,2,1,0:T(8,128)}) custom-call(s32[8]{0:T(128)} %bitcast.71, s32[1]{0:T(128)} %bitcast.3.part_ref.dst_ref, bf16[512,2048]{1,0:T(8,128)(2,1)} %get-tuple-element.65.refs_0_, bf16[512,2048]{1,0:T(8,128)(2,1)} %get-tuple-element.66.refs_1_, ...), custom_call_target="tpu_custom_call", output_to_operand_aliasing={{0}: (18, {}), {1}: (19, {})} | custom-call | flops 1006632960 | bytes 163840 | tf_op jit(solution)/shard_map/back_second1/pallas_call | solution.py:612
  818.7 11.1 convolution_convert_fusion
  834.9 49.4 %back_near1.1 = bf16[3,8,64,2048]{3,2,1,0:T(8,128)(2,1)} custom-call(s32[8]{0:T(128)} %bitcast.72, s32[1]{0:T(128)} %bitcast.3.part_ref.dst_ref, bf16[512,2048]{1,0:T(8,128)(2,1)} %get-tuple-element.65.refs_0_, bf16[512,2048]{1,0:T(8,128)(2,1)} %get-tuple-element.66.refs_1_, ...), custom_call_target="tpu_custom_call", output_to_operand_aliasing={{}: (11, {})} | custom-call | flops 671088640 | bytes 327680 | tf_op jit(solution)/shard_map/back_near1/pallas_call | solution.py:612
  884.4 36.6 %collective-permute-done.5 = bf16[2048,1024]{1,0:T(8,128)(2,1)} collective-permute-done((bf16[2048,1024]{1,0:T(8,128)(2,1)}, bf16[2048,1024]{1,0:T(8,128)(2,1)}, u32[]{:S(2)}, u32[]{:S(2)}) %collective-permute-start.5) | collective-permute-done | bytes 4194336 | tf_op jit(solution)/shard_map/ppermute | solution.py:1155
  921.1 16.2 %multiply_reduce_fusion = (f32[1024]{0:T(1024)S(1)}, f32[2048]{0:T(1024)S(1)}, f32[2048,1024]{1,0:T(8,128)S(1)}) fusion(f32[2048,1024]{1,0:T(8,128)} %copy-done.2, f32[2048]{0:T(1024)S(1)} %copy-done.21, f32[1024]{0:T(1024)S(1)} %copy-done.26, f32[1024]{0:T(1024)S(1)} %copy-done.29, bf16[2048,1024]{1,0:T(8,128)(2,1)} %collective-permute-done.5, ...), kind=kOutput, calls=%fused_computation | convolution fusion | flops 6470759424 | bytes 30437376 | tf_op jit(solution)/shard_map/dot_general | solution.py:26
  937.2 8.7 convert_reduce_fusion
  946.6 14.1 %join_back.1 = (f32[2048,1024]{1,0:T(8,128)}, f32[2048,1024]{1,0:T(8,128)}) custom-call(bf16[2048,1024]{1,0:T(8,128)(2,1)} %get-tuple-element.117.grad_ref, bf16[2048,1024]{1,0:T(8,128)(2,1)} %w_ref.1), custom_call_target="tpu_custom_call" | custom-call | flops 33554432 | bytes 262144 | tf_op jit(solution)/shard_map/join_back/pallas_call | solution.py:1086
  960.6 14.0 %convolution_convert_fusion.1.big_ref = bf16[2048,1024]{1,0:T(8,128)(2,1)} fusion(bf16[2048,2048]{1,0:T(8,128)(2,1)} %copy-done.17, bf16[2048,1024]{1,0:T(8,128)(2,1)} %get-tuple-element.117.grad_ref), kind=kOutput, calls=%fused_computation.19 | convolution fusion | flops 8592031744 | bytes 16777216 | tf_op jit(solution)/shard_map/dot_general | solution.py:26
  974.6 11.9 %unpack.1 = (f32[1024,2048]{1,0:T(8,128)}, f32[2048,1024]{1,0:T(8,128)}) custom-call(s32[1]{0:T(128)} %bitcast.17.core_ref, bf16[2304,1024]{1,0:T(8,128)(2,1)} %all-reduce.3.cloned.1.call-done.own_ref, bf16[2304,1024]{1,0:T(8,128)(2,1)} %collective-permute-done.6.sibling_ref), custom_call_target="tpu_custom_call" | custom-call | flops 32768 | bytes 393216 | tf_op jit(solution)/shard_map/unpack/pallas_call | solution.py:1114
  986.5 19.2 %project_back.1.side_ref = bf16[1536,1024]{1,0:T(8,128)(2,1)} custom-call(bf16[2048,1024]{1,0:T(8,128)(2,1)} %multiply_convert_fusion.1.x_ref.refs_0_, bf16[1536,2048]{1,0:T(8,128)(2,1)} %bitcast.54, bf16[2048,1024]{1,0:T(8,128)(2,1)} %collective-permute-done.2.x_ref.refs_2_, bf16[1536,2048]{1,0:T(8,128)(2,1)} %bitcast.52, ...), custom_call_target="tpu_custom_call" | custom-call | flops 201326592 | bytes 196608 | tf_op jit(solution)/shard_map/project_back/pallas_call | solution.py:807
  1006.8 130.2 %sum_all.1 = (bf16[2048,1024]{1,0:T(8,128)(2,1)}, bf16[1536,1024]{1,0:T(8,128)(2,1)}, f32[16,1024]{1,0:T(8,128)}) custom-call(bf16[2048,1024]{1,0:T(8,128)(2,1)} %convolution_convert_fusion.1.big_ref, bf16[1536,1024]{1,0:T(8,128)(2,1)} %project_back.1.side_ref, f32[16,1024]{1,0:T(8,128)} %pad.4.small_ref), custom_call_target="tpu_custom_call" | custom-call | flops 32768 | bytes 262144 | tf_op jit(solution)/shard_map/sum_all/pallas_call | solution.py:1034
  1139.4 6.6 convert_element_type.74
  (147 shorter events, 92.5 us)
Async XLA Ops:
  7.2 366.4 %all-gather.5.cloned.1.call-start = ((), (), s32[]{:S(2)}) async-start(), calls=%async_computation.3 | async-start | bytes 10485760 | tf_op jit(solution)/shard_map/all_gather | solution.py:1177
  7.3 26.5 %collective-permute-start.1 = (bf16[512,1024]{1,0:T(8,128)(2,1)}, bf16[512,1024]{1,0:T(8,128)(2,1)}, u32[]{:S(2)}, u32[]{:S(2)}) collective-permute-start(bf16[512,1024]{1,0:T(8,128)(2,1)} %param.27), channel_id=1, source_target_pairs={{0,1},{1,0},{2,3},{3,2},{4,5},{5,4},{6,7},{7,6},{8,9},{9,8},{10,11... | collective-permute-start | bytes 3145736 | tf_op jit(solution)/shard_map/ppermute | solution.py:1155
  10.3 23.5 %collective-permute-start = (bf16[2048]{0:T(1024)(128)(2,1)}, bf16[2048]{0:T(1024)(128)(2,1)S(1)}, u32[]{:S(2)}, u32[]{:S(2)}) collective-permute-start(bf16[2048]{0:T(1024)(128)(2,1)} %param.31), channel_id=1, source_target_pairs={{0,1},{1,0},{2,3},{3,2},{4,5},{5,4},{6,7},{7,6},{8,9},{9,8},{10,11... | collective-permute-start | bytes 12296 | tf_op jit(solution)/shard_map/ppermute | solution.py:1155
  13.7 10.0 copy-start.28
  23.6 11.9 %copy-start.36 = (s32[1,8]{1,0:T(1,128)S(1)}, s32[1,8]{1,0:T(1,128)}, u32[]{:S(2)}) copy-start(s32[1,8]{1,0:T(1,128)} %param.20) | copy-start | bytes 100
  23.6 12.1 %copy-start.18 = (bf16[1024,512]{1,0:T(8,128)(2,1)S(1)}, bf16[1024,512]{1,0:T(8,128)(2,1)}, u32[]{:S(2)}) copy-start(bf16[1024,512]{1,0:T(8,128)(2,1)} %param.24) | copy-start | bytes 3145732
  23.7 12.6 %copy-start.19 = (bf16[1024,512]{1,0:T(8,128)(2,1)S(1)}, bf16[1024,512]{1,0:T(8,128)(2,1)}, u32[]{:S(2)}) copy-start(bf16[1024,512]{1,0:T(8,128)(2,1)} %param.25) | copy-start | bytes 3145732
  33.8 92.1 %collective-permute-start.2 = (bf16[2048,1024]{1,0:T(8,128)(2,1)}, bf16[2048,1024]{1,0:T(8,128)(2,1)}, u32[]{:S(2)}, u32[]{:S(2)}) collective-permute-start(bf16[2048,1024]{1,0:T(8,128)(2,1)} %multiply_convert_fusion.1.x_ref.refs_0_), channel_id=1, source_target_pairs={{0,1},{1,0},{2,3},{3,2},{4,5},{5,4},{6,7},{7,6},{8,9},{9,8},{10,11... | collective-permute-start | bytes 12582920 | tf_op jit(solution)/shard_map/ppermute | solution.py:1155
  36.3 18.6 %copy-start.11 = (bf16[1024,512]{0,1:T(8,128)(2,1)}, bf16[1024,512]{0,1:T(8,128)(2,1)S(1)}, u32[]{:S(2)}) copy-start(bf16[1024,512]{0,1:T(8,128)(2,1)S(1)} %copy.52) | copy-start | bytes 3145732
  36.8 18.1 %copy-start.13 = (bf16[1024,512]{0,1:T(8,128)(2,1)}, bf16[1024,512]{0,1:T(8,128)(2,1)S(1)}, u32[]{:S(2)}) copy-start(bf16[1024,512]{0,1:T(8,128)(2,1)S(1)} %copy.53) | copy-start | bytes 3145732
  38.7 16.2 %copy-start.15 = (bf16[1024,512]{0,1:T(8,128)(2,1)}, bf16[1024,512]{0,1:T(8,128)(2,1)S(1)}, u32[]{:S(2)}) copy-start(bf16[1024,512]{0,1:T(8,128)(2,1)S(1)} %copy.54) | copy-start | bytes 3145732
  129.1 244.6 %all-gather.7.cloned.1.call-start = ((), (), s32[]{:S(2)}) async-start(), calls=%async_computation.4 | async-start | bytes 10485760 | tf_op jit(solution)/shard_map/all_gather | solution.py:1177
  132.3 507.3 %reduce-scatter.2.cloned.1.call-start = ((), (), s32[]{:S(2)}) async-start(), calls=%async_computation.1 | async-start | bytes 23592960 | tf_op jit(solution)/shard_map/reduce_scatter | solution.py:1250
  143.6 84.1 %copy-start.23 = (s32[8,1]{0,1:T(1,128)S(1)}, s32[8,1]{0,1:T(1,128)}, u32[]{:S(2)}) copy-start(s32[8,1]{0,1:T(1,128)} %copy-done.22) | copy-start | bytes 100
  143.6 84.6 %copy-start.34 = (bf16[2048]{0:T(1024)(128)(2,1)S(1)}, bf16[2048]{0:T(1024)(128)(2,1)}, u32[]{:S(2)}) copy-start(bf16[2048]{0:T(1024)(128)(2,1)} %param.31) | copy-start | bytes 12292
  227.6 64.8 %collective-permute-start.3 = (bf16[512,2048]{1,0:T(8,128)(2,1)}, bf16[512,2048]{1,0:T(8,128)(2,1)S(1)}, u32[]{:S(2)}, u32[]{:S(2)}) collective-permute-start(bf16[512,2048]{1,0:T(8,128)(2,1)} %get-tuple-element.77.refs_12_), channel_id=1, source_target_pairs={{0,1},{1,0},{2,3},{3,2},{4,5},{5,4},{6,7},{7,6},{8,9},{9,8},{10,11... | collective-permute-start | bytes 6291464 | tf_op jit(solution)/shard_map/ppermute | solution.py:1155
  279.6 12.7 %copy-start.32 = (f32[1024]{0:T(1024)S(1)}, f32[1024]{0:T(1024)}, u32[]{:S(2)}) copy-start(f32[1024]{0:T(1024)} %param.28) | copy-start | bytes 12292
  283.9 16.5 %copy-start.24 = (f32[1024]{0:T(1024)S(1)}, f32[1024]{0:T(1024)}, u32[]{:S(2)}) copy-start(f32[1024]{0:T(1024)} %param.29) | copy-start | bytes 12292
  305.1 63.3 %copy-start.1 = (bf16[512,2048]{1,0:T(8,128)(2,1)S(1)}, bf16[512,2048]{1,0:T(8,128)(2,1)}, u32[]{:S(2)}) copy-start(bf16[512,2048]{1,0:T(8,128)(2,1)} %get-tuple-element.75.refs_4_) | copy-start | bytes 6291460
  477.7 65.0 %collective-permute-start.4 = (bf16[512,2048]{1,0:T(8,128)(2,1)}, bf16[512,2048]{1,0:T(8,128)(2,1)S(1)}, u32[]{:S(2)}, u32[]{:S(2)}) collective-permute-start(bf16[512,2048]{1,0:T(8,128)(2,1)} %convolution_convert_fusion.2), channel_id=1, source_target_pairs={{0,1},{1,0},{2,3},{3,2},{4,5},{5,4},{6,7},{7,6},{8,9},{9,8},{10,11... | collective-permute-start | bytes 6291464 | tf_op jit(solution)/shard_map/ppermute | solution.py:1155
  673.1 211.3 %all-reduce.3.cloned.1.call-start = ((), (), s32[]{:S(2)}) async-start(), calls=%async_computation.2 | async-start | bytes 9437184 | tf_op jit(solution)/shard_map/psum | solution.py:1253
  744.4 74.2 %copy-start.12 = (bf16[1024,512]{0,1:T(8,128)(2,1)S(1)}, bf16[1024,512]{0,1:T(8,128)(2,1)}, u32[]{:S(2)}) copy-start(bf16[1024,512]{0,1:T(8,128)(2,1)} %copy-done.11) | copy-start | bytes 3145732
  744.4 74.2 %copy-start.14 = (bf16[1024,512]{0,1:T(8,128)(2,1)S(1)}, bf16[1024,512]{0,1:T(8,128)(2,1)}, u32[]{:S(2)}) copy-start(bf16[1024,512]{0,1:T(8,128)(2,1)} %copy-done.13) | copy-start | bytes 3145732
  744.4 74.2 %copy-start.16 = (bf16[1024,512]{0,1:T(8,128)(2,1)S(1)}, bf16[1024,512]{0,1:T(8,128)(2,1)}, u32[]{:S(2)}) copy-start(bf16[1024,512]{0,1:T(8,128)(2,1)} %copy-done.15) | copy-start | bytes 3145732
  818.6 16.2 %copy-start.30 = (f32[1,1,2048]{2,1,0:T(1,128)S(1)}, f32[1,1,2048]{2,1,0:T(1,128)}, u32[]{:S(2)}) copy-start(f32[1,1,2048]{2,1,0:T(1,128)} %get-tuple-element.103) | copy-start | bytes 24580
  818.7 16.2 %copy-start.31 = (f32[1,1,2048]{2,1,0:T(1,128)S(1)}, f32[1,1,2048]{2,1,0:T(1,128)}, u32[]{:S(2)}) copy-start(f32[1,1,2048]{2,1,0:T(1,128)} %get-tuple-element.104) | copy-start | bytes 24580
  829.8 91.2 %collective-permute-start.5 = (bf16[2048,1024]{1,0:T(8,128)(2,1)}, bf16[2048,1024]{1,0:T(8,128)(2,1)}, u32[]{:S(2)}, u32[]{:S(2)}) collective-permute-start(bf16[2048,1024]{1,0:T(8,128)(2,1)} %convolution_convert_fusion), channel_id=1, source_target_pairs={{0,1},{1,0},{2,3},{3,2},{4,5},{5,4},{6,7},{7,6},{8,9},{9,8},{10,11... | collective-permute-start | bytes 12582920 | tf_op jit(solution)/shard_map/ppermute | solution.py:1155
  834.9 86.2 %copy-start.21 = (f32[2048]{0:T(1024)S(1)}, f32[2048]{0:T(1024)}, u32[]{:S(2)}) copy-start(f32[2048]{0:T(1024)} %copy-done.20) | copy-start | bytes 24580
  834.9 86.1 %copy-start.26 = (f32[1024]{0:T(1024)S(1)}, f32[1024]{0:T(1024)}, u32[]{:S(2)}) copy-start(f32[1024]{0:T(1024)} %param.22) | copy-start | bytes 12292
  834.9 86.1 %copy-start.29 = (f32[1024]{0:T(1024)S(1)}, f32[1024]{0:T(1024)}, u32[]{:S(2)}) copy-start(f32[1024]{0:T(1024)} %param.23) | copy-start | bytes 12292
  884.3 90.3 %collective-permute-start.6 = (bf16[2304,1024]{1,0:T(8,128)(2,1)}, bf16[2304,1024]{1,0:T(8,128)(2,1)}, u32[]{:S(2)}, u32[]{:S(2)}) collective-permute-start(bf16[2304,1024]{1,0:T(8,128)(2,1)} %all-reduce.3.cloned.1.call-done.own_ref), channel_id=1, source_target_pairs={{0,2},{2,0},{1,3},{3,1},{4,6},{6,4},{5,7},{7,5},{8,10},{10,8},{9,1... | collective-permute-start | bytes 14155784 | tf_op jit(solution)/shard_map/ppermute | solution.py:1291
  921.0 16.2 %copy-start.27 = (f32[2048]{0:T(1024)S(1)}, f32[2048]{0:T(1024)}, u32[]{:S(2)}) copy-start(f32[2048]{0:T(1024)} %get-tuple-element.133) | copy-start | bytes 24580
  (16 other events, 101.2 us)
Sparse Core Ops, SparseCore 0:
  129.2 59.4 all-gather.4
  190.8 76.1 all-gather.6
  471.4 155.8 reduce-scatter.1
  677.6 176.7 all-reduce.2

commit v3 on v1

--- a/solution.py
+++ b/solution.py
@@ -66,10 +66,11 @@
 
 
 def cost(flops, moved):
-    return pl.CostEstimate(flops=flops // 8, bytes_accessed=moved // 8, transcendentals=0)
-
-
-def project_kernel(x_ref, w_ref, cos_ref, sin_ref, q_ref, k_ref, v_ref):
+    return pl.CostEstimate(flops=flops // 64, bytes_accessed=moved // 64, transcendentals=0)
+
+
+def project_kernel(x_ref, w_ref, cos_ref, sin_ref, *refs):
+    q_ref, k_ref, v_ref = refs[-3:]
     x = x_ref[...]
     c, s = cos_ref[...], sin_ref[...]
     width = q_ref.shape[0]
@@ -82,12 +83,14 @@
     v_ref[...] = dot_nt(w_ref[2 * width :, :], x).astype(BF)
 
 
-def project(x, w, cosine, sine):
+def project(x, w, cosine, sine, first=0, written=()):
     count, depth = x.shape
+    total = cosine.shape[1]
     width = w.shape[0] // 3
     block = min(512, count)
-    table = pl.BlockSpec((HALF, block), lambda i: (0, i))
-    out = pl.BlockSpec((width, block), lambda i: (0, i))
+    start = first // block
+    table = pl.BlockSpec((HALF, block), lambda i: (0, i + start))
+    out = pl.BlockSpec((width, block), lambda i: (0, i + start))
     return pl.pallas_call(
         project_kernel,
         grid=(count // block,),
@@ -96,12 +99,183 @@
             pl.BlockSpec(w.shape, lambda i: (0, 0)),
             table,
             table,
+        ]
+        + [pl.BlockSpec(memory_space=pl.ANY)] * len(written),
+        out_specs=[out] * 3,
+        out_shape=[jax.ShapeDtypeStruct((width, total), BF)] * 3,
+        input_output_aliases={4 + i: i for i in range(len(written))},
+        compiler_params=params(),
+        name="project",
+    )(x, w, cosine, sine, *written)
+
+
+def scale_of(stream):
+    return lax.rsqrt(jnp.mean(stream * stream, axis=-1, keepdims=True) + EPS)
+
+
+def norm_back_rows(grad, stream, gain):
+    scale = scale_of(stream)
+    tilted = grad * gain
+    back = scale * tilted - stream * (scale * scale * scale) * jnp.mean(
+        tilted * stream, axis=-1, keepdims=True
+    )
+    return back, jnp.sum(grad * stream * scale, axis=0, keepdims=True)
+
+
+def add_up(ref, terms):
+    for i, term in enumerate(terms):
+
+        @pl.when(pl.program_id(0) == 0)
+        def _():
+            ref[i : i + 1, :] = term
+
+        @pl.when(pl.program_id(0) > 0)
+        def _():
+            ref[i : i + 1, :] += term
+
+
+def row_specs(rows, width, block, first=0):
+    def tall(columns=width):
+        return pl.BlockSpec((block, columns), lambda i: (i + first, 0))
+
+    def whole(*shape):
+        return pl.BlockSpec(shape, lambda i: (0, 0))
+
+    return tall, whole
+
+
+def enter_kernel(x_ref, s_ref, w_ref, b_ref, gain_ref, *refs):
+    h_ref, n_ref = refs[-2:]
+    width = x_ref.shape[1]
+    h = dot(x_ref[...], w_ref[:width, :]) + dot(s_ref[...], w_ref[width:, :]) + b_ref[...]
+    h_ref[...] = h
+    n_ref[...] = (h * scale_of(h) * gain_ref[...]).astype(BF)
+
+
+def enter(x, skip, w, bias, gain, first, count, written=()):
+    rows, width = x.shape
+    block = min(256, count)
+    tall, whole = row_specs(rows, width, block, first // block)
+    return pl.pallas_call(
+        enter_kernel,
+        grid=(count // block,),
+        in_specs=[tall(), tall(), whole(*w.shape), whole(1, width), whole(1, width)]
+        + [pl.BlockSpec(memory_space=pl.ANY)] * len(written),
+        out_specs=[tall(), tall()],
+        out_shape=[jax.ShapeDtypeStruct((rows, width), F32), jax.ShapeDtypeStruct((rows, width), BF)],
+        input_output_aliases={5 + i: i for i in range(len(written))},
+        compiler_params=params(),
+        name="enter",
+        cost_estimate=cost(4 * count * width * width, 10 * count * width),
+    )(x, skip, w, bias[None], gain[None], *written)
+
+
+def upper_kernel(h_ref, near_ref, in_ref, own_ref, far_ref, b_ref, gain_ref, h1_ref, n_ref):
+    h = h_ref[...] + dot_tn(near_ref[...], own_ref[...]) + dot_tn(in_ref[...], far_ref[...])
+    h = h + b_ref[...]
+    h1_ref[...] = h
+    n_ref[...] = (h * scale_of(h) * gain_ref[...]).astype(BF)
+
+
+def upper(h0, near, arrived, own, far, bias, gain):
+    rows, width = h0.shape
+    block = min(256, rows)
+    tall, whole = row_specs(rows, width, block)
+    flat = pl.BlockSpec((near.shape[0], block), lambda i: (0, i))
+    return pl.pallas_call(
+        upper_kernel,
+        grid=(rows // block,),
+        in_specs=[
+            tall(), flat, flat, whole(*own.shape), whole(*far.shape), whole(1, width), whole(1, width)
         ],
-        out_specs=[out] * 3,
-        out_shape=[jax.ShapeDtypeStruct((width, count), BF)] * 3,
-        compiler_params=params(),
-        name="project",
-    )(x, w, cosine, sine)
+        out_specs=[tall(), tall()],
+        out_shape=[jax.ShapeDtypeStruct((rows, width), F32), jax.ShapeDtypeStruct((rows, width), BF)],
+        compiler_params=params(),
+        name="upper",
+        cost_estimate=cost(2 * rows * width * width, 12 * rows * width),
+    )(h0, near, arrived, own, far, bias[None], gain[None])
+
+
+def middle_kernel(
+    h_ref, branch_ref, dn_ref, g_ref, valid_ref, bias_ref, gain_ref, own_ref, far_ref,
+    out_ref, dh_ref, low_ref, near_ref, sent_ref, sums_ref,
+):
+    valid = valid_ref[...]
+    h = h_ref[...]
+    out_ref[...] = valid * (h + branch_ref[...] + bias_ref[...])
+    g = g_ref[...].astype(F32) * valid
+    back, gain_sum = norm_back_rows(dn_ref[...], h, gain_ref[...])
+    dh = g + back
+    dh_ref[...] = dh
+    low = dh.astype(BF)
+    low_ref[...] = low
+    near_ref[...] = dot_nt(own_ref[...], low).astype(BF)
+    sent_ref[...] = dot_nt(far_ref[...], low).astype(BF)
+    add_up(
+        sums_ref,
+        [jnp.sum(g, 0, keepdims=True), gain_sum, jnp.sum(dh, 0, keepdims=True)],
+    )
+
+
+def middle(h1, branch, dn, cotangent, valid, bias, gain, own, far):
+    rows, width = h1.shape
+    block = min(256, rows)
+    tall, whole = row_specs(rows, width, block)
+    flat = pl.BlockSpec((own.shape[0], block), lambda i: (0, i))
+    return pl.pallas_call(
+        middle_kernel,
+        grid=(rows // block,),
+        in_specs=[tall(), tall(), tall(), tall(), tall(1), whole(1, width), whole(1, width)]
+        + [whole(*own.shape)] * 2,
+        out_specs=[tall(), tall(), tall(), flat, flat, whole(3, width)],
+        out_shape=[
+            jax.ShapeDtypeStruct((rows, width), F32),
+            jax.ShapeDtypeStruct((rows, width), F32),
+            jax.ShapeDtypeStruct((rows, width), BF),
+            jax.ShapeDtypeStruct((own.shape[0], rows), BF),
+            jax.ShapeDtypeStruct((own.shape[0], rows), BF),
+            jax.ShapeDtypeStruct((3, width), F32),
+        ],
+        compiler_params=params(),
+        name="middle",
+        cost_estimate=cost(2 * rows * width * width, 24 * rows * width),
+    )(h1, branch, dn, cotangent, valid, bias[None], gain[None], own, far)
+
+
+def leave_kernel(back_ref, w_ref, sent_ref, h_ref, dh_ref, gain_ref, *refs):
+    low_ref, sums_ref = refs[-2:]
+    grad = dot_tn(back_ref[...], w_ref[...]) + sent_ref[...].astype(F32)
+    back, gain_sum = norm_back_rows(grad, h_ref[...], gain_ref[...])
+    low = (back + dh_ref[...]).astype(BF)
+    low_ref[...] = low
+    add_up(sums_ref, [jnp.sum(low.astype(F32), 0, keepdims=True), gain_sum])
+
+
+def leave(back, w, sent, h0, dh1, gain, after):
+    rows, width = h0.shape
+    block = min(256, rows)
+    tall, whole = row_specs(rows, width, block)
+    return pl.pallas_call(
+        leave_kernel,
+        grid=(rows // block,),
+        in_specs=[
+            pl.BlockSpec((back.shape[0], block), lambda i: (0, i)),
+            whole(*w.shape),
+            tall(),
+            tall(),
+            tall(),
+            whole(1, width),
+        ]
+        + [pl.BlockSpec(memory_space=pl.ANY)] * len(after),
+        out_specs=[tall(), whole(2, width)],
+        out_shape=[
+            jax.ShapeDtypeStruct((rows, width), BF),
+            jax.ShapeDtypeStruct((2, width), F32),
+        ],
+        compiler_params=params(),
+        name="leave",
+        cost_estimate=cost(2 * rows * width * back.shape[0], 16 * rows * width),
+    )(back, w, sent, h0, dh1, gain[None], *after)
 
 
 def segments(ends_ref, first, count):
@@ -471,19 +645,15 @@
     return found
 
 
-def half_back_kernel(near_only, ends_ref, part_ref, *refs):
+def half_back_kernel(near_only, given_partial, finish, ends_ref, part_ref, *refs):
     refs = list(refs)
     sides = (0,) if near_only else (0, 1)
     given = {side: [refs.pop(0) for _ in range(8)] for side in sides}
-    if near_only:
-        partial_ref = refs.pop(0)
-        while len(refs) > 1 + 7:
-            refs.pop(0)
-        out_ref = refs.pop(0)
-    else:
-        while len(refs) > 2 + 7:
-            refs.pop(0)
-        out_ref, partial_ref = refs.pop(0), refs.pop(0)
+    partial_in = refs.pop(0) if given_partial else None
+    while len(refs) > (1 if near_only else 2) + 7:
+        refs.pop(0)
+    out_ref = None if near_only else refs.pop(0)
+    near_ref = refs.pop(0)
     kaug, vaug, qaug, gaug, pair, dq, sums = refs
     rank = part_ref[0]
     half = given[0][0].shape[1]
@@ -519,11 +689,11 @@
         gaug[:HEAD_DIM, there] = g
         gaug[HEAD_DIM : HEAD_DIM + SEGS, there] = split3(-delta).astype(BF)
         pair[there, :] = jnp.concatenate([q, g], 0).T
-    if near_only:
-        dq[...] = partial_ref[0, 0]
-        sums[...] = partial_ref[1:, 0]
+    dq[...] = jnp.zeros_like(dq)
+    if given_partial:
+        dq[:, :half] = partial_in[0, 0]
+        sums[...] = partial_in[1:, 0]
     else:
-        dq[...] = jnp.zeros_like(dq)
         sums[...] = jnp.zeros_like(sums)
 
     def chunk(side, k0, n, queries):
@@ -538,14 +708,11 @@
             dv = dv + dot(probs.astype(BF), pair[there, HEAD_DIM:])
             dk = dk + dot(tilt, pair[there, :HEAD_DIM])
             dq[:, there] += dot(kt, tilt)
-        if side == 0 and not near_only:
-            sums[0, :, pl.ds(k0, n)] = dk.T
-            sums[1, :, pl.ds(k0, n)] = dv.T
+        dk, dv = dk.T, dv.T
+        if side == 0:
+            sums[0, :, pl.ds(k0, n)] += dk
+            sums[1, :, pl.ds(k0, n)] += dv
             return
-        dk, dv = dk.T, dv.T
-        if near_only:
-            dk = dk + sums[0, :, pl.ds(k0, n)]
-            dv = dv + sums[1, :, pl.ds(k0, n)]
         c, s = given[side][6][:, pl.ds(k0, n)], given[side][7][:, pl.ds(k0, n)]
         out_ref[1, 0, :, pl.ds(k0, n)] = turn_back(dk, c, s, LN2)
         out_ref[2, 0, :, pl.ds(k0, n)] = dv.astype(BF)
@@ -574,20 +741,22 @@
 
                     lax.fori_loop(0, total // n, step, 0)
 
-    if near_only:
+    if not near_only:
+        out_ref[0, 0] = turn_back(dq[:, half:], given[1][6][...], given[1][7][...], 0.125)
+    if finish:
         c, s = given[0][6][...], given[0][7][...]
-        out_ref[0, 0] = turn_back(dq[...], c, s, 0.125)
+        near_ref[0, 0] = turn_back(dq[:, :half], c, s, 0.125)
+        near_ref[1, 0] = turn_back(sums[0], c, s, LN2)
+        near_ref[2, 0] = sums[1].astype(BF)
     else:
-        c, s = given[1][6][...], given[1][7][...]
-        out_ref[0, 0] = turn_back(dq[:, half:], c, s, 0.125)
-        partial_ref[0, 0] = dq[:, :half]
-        partial_ref[1:, 0] = sums[...]
-
-
-def half_back(name, ends, rank, sides, first, count, partial=None, written=(), after=None):
+        near_ref[0, 0] = dq[:, :half]
+        near_ref[1:, 0] = sums[...]
+
+
+def half_back(name, ends, rank, sides, first, count, finish, partial=None, written=(), after=None):
     rows, half = sides[0][0].shape
     heads = rows // HEAD_DIM
-    near_only = partial is not None
+    near_only = len(sides) == 1
     head = pl.BlockSpec((HEAD_DIM, half), lambda h, e, r: (h + first, 0))
     line = pl.BlockSpec((1, 1, half), lambda h, e, r: (h + first, 0, 0))
     table = pl.BlockSpec((HALF, half), lambda h, e, r: (0, 0))
@@ -598,20 +767,24 @@
         operands += list(side)
         specs += [head] * 5 + [line, table, table]
     result = jax.ShapeDtypeStruct((3, heads, HEAD_DIM, half), BF)
-    if near_only:
+    if partial is not None:
         operands.append(partial)
         specs.append(block)
-    aliases = {2 + len(operands) + i: i for i in range(len(written))}
-    operands += list(written)
-    specs += [anywhere] * len(written)
+    aliases = {}
+    for i, array in enumerate(written):
+        if array is not None:
+            aliases[2 + len(operands)] = i
+            operands.append(array)
+            specs.append(anywhere)
     if after is not None:
         operands.append(after)
         specs.append(anywhere)
-    out_specs = [block] if near_only else [block, block]
-    out_shape = [result, jax.ShapeDtypeStruct(result.shape, F32)][: len(out_specs)]
+    near_result = result if finish else jax.ShapeDtypeStruct(result.shape, F32)
+    out_shape = [near_result] if near_only else [result, near_result]
+    out_specs = [block] * len(out_shape)
     wide = half * len(sides)
     return pl.pallas_call(
-        functools.partial(half_back_kernel, near_only),
+        functools.partial(half_back_kernel, near_only, partial is not None, finish),
         grid_spec=pltpu.PrefetchScalarGridSpec(
             num_scalar_prefetch=2,
             grid=(count,),
@@ -761,29 +934,39 @@
     )(src, dst, *operands)
 
 
-def out_back_kernel(mixed_ref, grad_ref, sums_ref, after_ref, out_ref):
-    out_ref[0, 0] = dot(mixed_ref[...], grad_ref[...]).astype(BF)
-
-
-def out_back(mixed_rows, grad, sums, extra, after):
-    heads, rows = mixed_rows.shape
-    _, parts, total, depth = sums.shape
+def out_back_kernel(part_ref, near_ref, in_ref, grad_ref, sums_ref, out_ref):
+    for side, mixed_ref in enumerate((near_ref, in_ref)):
+
+        @pl.when(pl.program_id(0) == side)
+        def _():
+            out_ref[0, 0] = dot(mixed_ref[...], grad_ref[...]).astype(BF)
+
+
+def out_back(mixed, grad, sums, extra, parts):
+    heads, rows = mixed[0].shape
+    total, depth = sums.shape[2:]
+    piece = pl.BlockSpec((extra, rows), lambda p, c, t: (c, 0))
     return pl.pallas_call(
         out_back_kernel,
-        grid=(parts, 2),
-        in_specs=[
-            pl.BlockSpec((extra, rows), lambda p, c: (2 * p + c, 0)),
-            pl.BlockSpec((rows, depth), lambda p, c: (0, 0)),
-            pl.BlockSpec(memory_space=pl.ANY),
-            pl.BlockSpec(memory_space=pl.ANY),
-        ],
-        out_specs=pl.BlockSpec((1, 1, extra, depth), lambda p, c: (c, p, total // extra - 1, 0)),
+        grid_spec=pltpu.PrefetchScalarGridSpec(
+            num_scalar_prefetch=1,
+            grid=(2, 2),
+            in_specs=[
+                piece,
+                piece,
+                pl.BlockSpec((rows, depth), lambda p, c, t: (0, 0)),
+                pl.BlockSpec(memory_space=pl.ANY),
+            ],
+            out_specs=pl.BlockSpec(
+                (1, 1, extra, depth), lambda p, c, t: (c, t[p], total // extra - 1, 0)
+            ),
+        ),
         out_shape=jax.ShapeDtypeStruct(sums.shape, BF),
-        input_output_aliases={2: 0},
+        input_output_aliases={4: 0},
         compiler_params=params(),
         name="out_back",
-        cost_estimate=cost(2 * rows * depth * heads, 2 * heads * depth),
-    )(mixed_rows, grad, sums, after)
+        cost_estimate=cost(4 * rows * depth * heads, 4 * heads * depth),
+    )(parts, *mixed, grad, sums)
 
 
 def project_back_kernel(*refs):
@@ -792,7 +975,7 @@
     total = dot(pairs[1][...], pairs[0][...])
     for i in range(2, len(pairs), 2):
         total = total + dot(pairs[i + 1][...], pairs[i][...])
-    out_ref[...] = total.T.astype(BF)
+    out_ref[...] = total.astype(BF)
 
 
 def project_back(pairs, after):
@@ -800,29 +983,52 @@
     depth = pairs[0][0].shape[1]
     block = total // 3
     specs, operands = [], []
-    for x, grad in pairs:
+    for x, grad, at in pairs:
         specs += [
             pl.BlockSpec(x.shape, lambda i: (0, 0)),
-            pl.BlockSpec((block, x.shape[0]), lambda i: (i, 0)),
+            pl.BlockSpec((block, x.shape[0]), functools.partial(lambda at, i: (i, at), at)),
         ]
         operands += [x, grad]
     return pl.pallas_call(
         project_back_kernel,
         grid=(3,),
         in_specs=specs + [pl.BlockSpec(memory_space=pl.ANY)],
-        out_specs=pl.BlockSpec((depth, block), lambda i: (0, i)),
-        out_shape=jax.ShapeDtypeStruct((depth, total), BF),
+        out_specs=pl.BlockSpec((block, depth), lambda i: (i, 0)),
+        out_shape=jax.ShapeDtypeStruct((total, depth), BF),
         compiler_params=params(),
         name="project_back",
         cost_estimate=cost(4 * pairs[0][0].shape[0] * depth * total, 8 * depth * total),
     )(*operands, after)
 
 
+def turn_kernel(x_ref, *out_refs):
+    for i, out_ref in enumerate(out_refs):
+
+        @pl.when(pl.program_id(0) == i)
+        def _():
+            out_ref[...] = x_ref[...].astype(F32).T
+
+
+def turn(x, parts):
+    rows, depth = x.shape
+    block = rows // parts
+    return pl.pallas_call(
+        turn_kernel,
+        grid=(parts,),
+        in_specs=[pl.BlockSpec((block, depth), lambda i: (i, 0))],
+        out_specs=[pl.BlockSpec((depth, block), lambda i: (0, 0))] * parts,
+        out_shape=[jax.ShapeDtypeStruct((depth, block), F32)] * parts,
+        compiler_params=params(),
+        name="turn",
+        cost_estimate=cost(rows * depth, 6 * rows * depth),
+    )(x)
+
+
 MESH = pl.DeviceIdType.MESH
 
 
 def sum_all_kernel(
-    big_ref, small_ref, after_ref, out_ref, small_out_ref,
+    big_ref, small_ref, out_ref, small_out_ref,
     buf, done, core_in, x_in, y_in, z_in, small, small_in, small_z, local, send, recv, small_send, small_recv,
 ):
     o, c, m = lax.axis_index("dpo"), lax.axis_index("core"), lax.axis_index("mp")
@@ -961,7 +1167,7 @@
     store.wait()
 
 
-def sum_all(big, small, after):
+def sum_all(big, small):
     rows, width = big.shape
     quarter, eighth, last = rows // 4, rows // 8, rows // 32
     anywhere = pl.BlockSpec(memory_space=pl.ANY)
@@ -969,7 +1175,7 @@
     dma = pltpu.SemaphoreType.DMA
     return pl.pallas_call(
         sum_all_kernel,
-        in_specs=[anywhere, whole, anywhere],
+        in_specs=[anywhere, whole],
         out_specs=[anywhere, whole],
         out_shape=[
             jax.ShapeDtypeStruct(big.shape, BF),
@@ -996,7 +1202,7 @@
         ),
         name="sum_all",
         cost_estimate=cost(rows * width, 8 * rows * width),
-    )(big, small, after)
+    )(big, small)
 
 
 def join_back_kernel(grad_ref, w_ref, first_ref, second_ref):
@@ -1024,6 +1230,54 @@
         name="join_back",
         cost_estimate=cost(rows * depth * width, 8 * rows * width),
     )(grad, w)
+
+
+def concat_back_kernel(x_ref, s_ref, grad_ref, out_ref):
+    for i, ref in enumerate((x_ref, s_ref)):
+
+        @pl.when(pl.program_id(0) == i)
+        def _():
+            out_ref[...] = dot_tn(ref[...], grad_ref[...]).astype(BF)
+
+
+def concat_back(x, skip, grad):
+    rows, width = grad.shape
+    block = min(512, width)
+    per = width // block
+    return pl.pallas_call(
+        concat_back_kernel,
+        grid=(2, per),
+        in_specs=[
+            pl.BlockSpec((rows, block), lambda i, j: (0, jnp.where(i == 0, j, per - 1))),
+            pl.BlockSpec((rows, block), lambda i, j: (0, jnp.where(i == 0, 0, j))),
+            pl.BlockSpec((rows, width), lambda i, j: (0, 0)),
+        ],
+        out_specs=pl.BlockSpec((block, width), lambda i, j: (i * per + j, 0)),
+        out_shape=jax.ShapeDtypeStruct((2 * width, width), BF),
+        compiler_params=params(),
+        name="concat_back",
+        cost_estimate=cost(4 * rows * width * width, 8 * rows * width),
+    )(x, skip, grad)
+
+
+def hold_kernel(x_ref, *refs):
+    refs[-1][...] = x_ref[...]
+
+
+def hold(x, after):
+    rows, width = x.shape
+    block = rows // 9 if rows % 9 == 0 else rows
+    piece = pl.BlockSpec((block, width), lambda i: (i, 0))
+    return pl.pallas_call(
+        hold_kernel,
+        grid=(rows // block,),
+        in_specs=[piece] + [pl.BlockSpec(memory_space=pl.ANY)] * len(after),
+        out_specs=piece,
+        out_shape=jax.ShapeDtypeStruct(x.shape, x.dtype),
+        compiler_params=params(),
+        name="hold",
+        cost_estimate=cost(rows * width, 4 * rows * width),
+    )(x, *after)
 
 
 def unpack_kernel(core_ref, own_ref, sibling_ref, up_ref, down_ref):
@@ -1090,33 +1344,31 @@
             rank == 0, jnp.concatenate([near, far], axis), jnp.concatenate([far, near], axis)
         )
 
-    joined = jnp.concatenate([inputs, skip_in], axis=1)
-    h0 = dot(joined, w_concat) + b_concat
-    scale_one = lax.rsqrt(jnp.mean(h0 * h0, axis=-1, keepdims=True) + EPS)
-    n1 = (h0 * scale_one * gain_attn).astype(BF)
-    n1_far = across(n1) if paired else lax.all_gather(n1, "mp", axis=0, tiled=True)
-    def gather(w):
-        half = w.shape[0] // 2
-        return lax.all_gather(piece(w, core, half), ("core", "mp"), axis=0).reshape(
-            2, parts, half, w.shape[1]
-        )
-
-    w_qkv = jnp.concatenate([w_query, w_key, w_value], axis=1)
-    w_turned = w_qkv.T
+    def core_half(w):
+        return piece(w, core, w.shape[0] // 2)
+
+    def gather(half):
+        return lax.all_gather(half, ("core", "mp"), axis=0).reshape((2, parts) + half.shape)
+
+    w_turned = jnp.concatenate([w_query.T, w_key.T, w_value.T], axis=0)
+    grad_rows = cotangent.astype(F32) * valid_here
+    grad_low = grad_rows.astype(BF)
+    half_up, half_down = core_half(w_up), core_half(w_down)
     if paired:
-        bias_far = across(b_up)
-        out_far = across(w_out)
+        bias_far, out_far = across(b_up), across(w_out)
+        h0, n1 = enter(inputs, skip_in, w_concat, b_concat, gain_attn, 0, rows)
+        n1, bias_far, out_far = lax.optimization_barrier((n1, bias_far, out_far))
+        n1_far = across(n1)
         tables_near = tables(piece(pos_all, rank, rows))
         q_near, k_near, v_near = project(n1, w_turned, *tables_near)
         start = attend_half(
             "near_near", ends, index, q_near, False, {0: (k_near, v_near)}, last=False
         )
-        n1_far, start, w_up_late, w_down_late = lax.optimization_barrier(
-            (n1_far, start, w_up, w_down)
+        tables_far = tables(piece(pos_all, 1 - rank, rows))
+        n1_far, start, half_up, half_down = lax.optimization_barrier(
+            (n1_far, start, half_up, half_down)
         )
-        up_all = gather(w_up_late)
-        down_all = gather(w_down_late)
-        tables_far = tables(piece(pos_all, 1 - rank, rows))
+        up_all, down_all = gather(half_up), gather(half_down)
         q_far, k_far, v_far = project(n1_far, w_turned, *tables_far)
         mixed_far, log_far = attend_half(
             "far_all", ends, index, q_far, True, {0: (k_near, v_near), 1: (k_far, v_far)}
@@ -1125,24 +1377,7 @@
         mixed_near, log_near = attend_half(
             "near_far", ends, index, q_near, False, {1: (k_far, v_far)}, carry=start
         )
-        mixed_rows = order(mixed_near, mixed_in, 0)
-        attended = dot_tn(mixed_near, w_out) + dot_tn(mixed_in, out_far)
-    else:
-        bias_all = lax.all_gather(b_up, "mp", axis=0).reshape(parts, 1, -1)
-        w_out_all = lax.all_gather(w_out, "mp", axis=0, tiled=True)
-        up_all = gather(w_up)
-        down_all = gather(w_down)
-        cosine, sine = tables(pos_all)
-        query, keys, values = project(n1_far, w_turned, cosine, sine)
-        mixed, logsum = attend(ends, zero, query, keys, values, 1)
-        mixed_rows = lax.all_to_all(mixed, "mp", 1, 0, tiled=True)
-        attended = dot_tn(mixed_rows, w_out_all)
-    h1 = h0 + attended + b_out
-    scale_two = lax.rsqrt(jnp.mean(h1 * h1, axis=-1, keepdims=True) + EPS)
-    n2 = (h1 * scale_two * gain_ffn).astype(BF)
-    grad_rows = cotangent.astype(F32) * valid_here
-    grad_low = grad_rows.astype(BF)
-    if paired:
+        h1, n2 = upper(h0, mixed_near, mixed_in, w_out, out_far, b_out, gain_ffn)
         branch, grad_n2, sums, bias_near = ffn(
             "ffn_near", n2, grad_low, w_up.reshape(2, 1, width // 2, hidden),
             b_up.reshape(1, 1, hidden), w_down.reshape(2, 1, hidden // 2, width),
@@ -1154,82 +1389,114 @@
             before=(branch, grad_n2, sums),
         )
         grad_bias = order(bias_near, grad_bias, 0)
+        output, grad_h1, grad_h1_low, grad_near, grad_sent, early = middle(
+            h1, branch, grad_n2, cotangent, valid_here, b_down, gain_ffn, w_out, out_far
+        )
+        grad_far = across(grad_sent)
+        sums = out_back(
+            (mixed_near, mixed_in), grad_h1_low, sums, extra, jnp.concatenate([index, other])
+        )
     else:
+        joined = jnp.concatenate([inputs, skip_in], axis=1)
+        h0 = dot(joined, w_concat) + b_concat
+        scale_one = lax.rsqrt(jnp.mean(h0 * h0, axis=-1, keepdims=True) + EPS)
+        n1 = (h0 * scale_one * gain_attn).astype(BF)
+        n1_all = lax.all_gather(n1, "mp", axis=0, tiled=True)
+        bias_all = lax.all_gather(b_up, "mp", axis=0).reshape(parts, 1, -1)
+        w_out_all = lax.all_gather(w_out, "mp", axis=0, tiled=True)
+        up_all, down_all = gather(half_up), gather(half_down)
+        cosine, sine = tables(pos_all)
+        query, keys, values = project(n1_all, w_turned, cosine, sine)
+        mixed, logsum = attend(ends, zero, query, keys, values, 1)
+        mixed_rows = lax.all_to_all(mixed, "mp", 1, 0, tiled=True)
+        h1 = h0 + dot_tn(mixed_rows, w_out_all) + b_out
+        scale_two = lax.rsqrt(jnp.mean(h1 * h1, axis=-1, keepdims=True) + EPS)
+        n2 = (h1 * scale_two * gain_ffn).astype(BF)
         every = jnp.arange(parts, dtype=jnp.int32)
         branch, grad_n2, sums, grad_bias = ffn(
             "ffn", n2, grad_low, up_all, bias_all, down_all, extra, parts, every, every
         )
-    output = valid_here * (h1 + branch + b_down)
-    grad_h1, grad_gain_ffn = norm_back(grad_n2, h1, scale_two, gain_ffn)
-    grad_h1 = grad_h1 + grad_rows
-    grad_h1_low = grad_h1.astype(BF)
-    if paired:
-        grad_far = across(dot_nt(out_far, grad_h1_low).astype(BF))
-        grad_near = dot_nt(w_out, grad_h1_low).astype(BF)
-        landed = grad_far
-    else:
-        landed = grad_mixed = lax.all_to_all(
+        output = valid_here * (h1 + branch + b_down)
+        grad_h1, grad_gain_ffn = norm_back(grad_n2, h1, scale_two, gain_ffn)
+        grad_h1 = grad_h1 + grad_rows
+        grad_h1_low = grad_h1.astype(BF)
+        grad_mixed = lax.all_to_all(
             dot_nt(w_out_all, grad_h1_low).astype(BF), "mp", 0, 1, tiled=True
         )
-    sums = out_back(mixed_rows, grad_h1_low, sums, extra, landed)
-    small = [jnp.sum(grad_rows, 0), grad_gain_ffn, jnp.sum(grad_h1, 0)]
+        grad_out = dot(mixed_rows, grad_h1_low).astype(BF)
+        grad_out = grad_out.reshape(parts, 2, extra, width).transpose(1, 0, 2, 3)
+        sums = lax.dynamic_update_slice(sums, grad_out, (0, 0, hidden, 0))
+        early = jnp.stack([jnp.sum(grad_rows, 0), grad_gain_ffn, jnp.sum(grad_h1, 0)])
+    def unpack_all(own):
+        sibling = lax.ppermute(own, "core", [(0, 1), (1, 0)])
+        up, down = unpack(core.reshape(1), own, sibling, hidden)
+        first, second = own[hidden:].astype(F32), sibling[hidden:].astype(F32)
+        out = jnp.where(
+            core == 0, jnp.concatenate([first, second]), jnp.concatenate([second, first])
+        )
+        return up, down, out
+
     part = lax.psum_scatter(
         sums.reshape((2 * parts,) + sums.shape[2:]), ("core", "mp"), scatter_dimension=0, tiled=True
     )[0]
     summed = lax.psum(part, "dpo")
-
     if paired:
         near = (q_near, k_near, v_near, grad_near, mixed_near, log_near) + tables_near
         far = (q_far, k_far, v_far, grad_far, mixed_far, log_far) + tables_far
         heads = each // HEAD_DIM
-        calls = 4
-        step = heads // calls
-        written = ()
-        for i in range(calls):
-            written = half_back(
-                f"back_far{i}", ends, index, (near, far), i * step, step, written=written,
-                after=part if i == calls // 2 else None,
+        back = functools.partial(half_back, ends=ends, rank=index)
+        both = (near, far)
+        middle_head = heads // 2
+        opening = back("back_near0", sides=(near,), first=0, count=middle_head, finish=False)[0]
+        written, at = (), 0
+        quarter = middle_head // 4
+        for i, count in enumerate((2 * quarter, quarter, middle_head - 3 * quarter)):
+            written = back(
+                f"back_first{i}", sides=both, first=at, count=count, finish=True,
+                partial=opening, written=written, after=part if i == 2 else None,
             )
-        back_far, partial = written
+            at += count
+        back_far, back_near = written
+        partial = None
+        for i in range(2):
+            back_far, partial = back(
+                f"back_second{i}", sides=both, first=at, count=middle_head // 2, finish=False,
+                written=(back_far, partial),
+            )
+            at += middle_head // 2
         back_far = back_far.reshape(3 * each, rows)
-        sent = across(dot(back_far, w_qkv, ((0,), (1,))).astype(BF))
-        written = ()
-        for i in range(2):
-            written = half_back(
-                f"back_near{i}", ends, index, (near,), i * heads // 2, heads // 2,
-                partial=partial, written=written, after=summed if i else None,
-            )
-        back_near = written[0].reshape(3 * each, rows)
-        grad_n1 = dot(back_near, w_qkv, ((0,), (1,))) + sent.astype(F32)
-        pairs = [(n1, back_near), (n1_far, back_far)]
+        grad_far_rows = dot_tn(back_far, w_turned).astype(BF)
+        sent = across(grad_far_rows)
+        back_near = back(
+            "back_near1", sides=(near,), first=middle_head, count=heads - middle_head, finish=True,
+            partial=partial, written=(back_near,), after=grad_far_rows,
+        )[0].reshape(3 * each, rows)
+        pairs = [(n1, back_near, 0), (n1_far, back_far, 0)]
+        grad_qkv = project_back(pairs, index)
+        grad_up, grad_down, grad_out = unpack_all(hold(summed, (grad_qkv, sent)))
+        grad_h0_low, late = leave(
+            back_near, w_turned, sent, h0, grad_h1, gain_attn, (grad_qkv,)
+        )
     else:
         back = attend_back(ends, query, keys, values, grad_mixed, mixed, logsum, cosine, sine)
-        grad_n1 = dot(back, w_qkv, ((0,), (1,))).astype(BF)
+        grad_n1 = dot_tn(back, w_turned).astype(BF)
         grad_n1 = lax.psum_scatter(grad_n1, "mp", scatter_dimension=0, tiled=True).astype(F32)
-        pairs = [(n1_far, back)]
-    turned = project_back(pairs, summed)
-    grad_qkv = lax.psum(turned, dp).astype(F32)
-    sibling = lax.ppermute(summed, "core", [(0, 1), (1, 0)])
-    grad_up, grad_down = unpack(core.reshape(1), summed, sibling, hidden)
-    own_out, sibling_out = summed[hidden:].astype(F32), sibling[hidden:].astype(F32)
-    grad_out = jnp.where(
-        core == 0,
-        jnp.concatenate([own_out, sibling_out]),
-        jnp.concatenate([sibling_out, own_out]),
-    )
-
-    grad_h0, grad_gain_attn = norm_back(grad_n1, h0, scale_one, gain_attn)
-    grad_h0_low = (grad_h0 + grad_h1).astype(BF)
-    grad_w_concat = dot_tn(joined, grad_h0_low).astype(BF)
-    small = small + [jnp.sum(grad_h0_low.astype(F32), axis=0), grad_gain_attn]
-    small = jnp.concatenate(small + [grad_bias.reshape(-1)]).reshape(-1, width)
+        grad_up, grad_down, grad_out = unpack_all(summed)
+        grad_qkv = project_back([(n1_all, back, 0)], index)
+        grad_h0, grad_gain_attn = norm_back(grad_n1, h0, scale_one, gain_attn)
+        grad_h0_low = (grad_h0 + grad_h1).astype(BF)
+        late = jnp.stack([jnp.sum(grad_h0_low.astype(F32), axis=0), grad_gain_attn])
+    grad_w_concat = concat_back(inputs, skip_in, grad_h0_low)
+    small = jnp.concatenate([early, late, grad_bias.reshape(-1, width)])
     small = jnp.pad(small, ((0, -small.shape[0] % 8), (0, 0)))
     if paired and lax.axis_size("dpo") == 8:
-        tail, small = sum_all(grad_w_concat, small, turned)
+        tail, small = sum_all(grad_w_concat, small)
+        grad_qkv = lax.psum(grad_qkv, dp)
     else:
         tail, small = lax.psum((grad_w_concat, small), dp + ("mp",))
+        grad_qkv = lax.psum(grad_qkv, dp)
     grad_inputs, grad_skip = join_back(grad_h0_low, w_concat)
-    wide = w_query.shape[1]
+    grad_query, grad_key, grad_value = turn(grad_qkv, 3)
     return (
         output,
         grad_inputs,
@@ -1237,9 +1504,9 @@
         tail.astype(F32),
         small[3],
         small[4],
-        grad_qkv[:, :wide],
-        grad_qkv[:, wide : 2 * wide],
-        grad_qkv[:, 2 * wide :],
+        grad_query,
+        grad_key,
+        grad_value,
         grad_out,
         small[2],
         small[1],

time: 1320 us -> 1100 us (0.83)
  waiting for transfers between devices: 284 us -> 67.1 us
  Pallas kernels: 833 us -> 947 us
  matrix products: 72.4 us -> 11.2 us
  other arithmetic: 61.7 us -> 22.5 us
    pallas_call x8 -> x16, Pallas kernels: 466 us -> 580 us  [the longest x7 372 us: half_back(): pl.pallas_call(functools.partial(half_back_kernel, near_only, partial is...]
    psum x1, waiting for transfers between devices: 86.3 us -> 0.02 us  [body(): grad_qkv = lax.psum(grad_qkv, dp)]
    ppermute x6, waiting for transfers between devices: 148 us -> 65.2 us  [across(): return lax.ppermute(x, 'mp', [(0, 1), (1, 0)])]
    dot_general x8 -> x1, matrix products: 72.4 us -> 11.2 us  [dot(): lax.dot_general(left, right, (dims, ((), ())), preferred_element_type=F32)]
    psum x1, waiting for transfers between devices: 48.2 us -> 0.01 us  [body(): summed = lax.psum(part, 'dpo')]
    reduce_sum x3 -> x0, other arithmetic: 28.7 us -> none  [the longest x1 12.1 us: body(): small = [jnp.sum(grad_rows, 0), grad_gain_ffn, jnp.sum(grad_h1, 0)]]
  transfers between devices with their start and end apart: 12 -> 12, of which waited for: 5 -> 5; matrix products, arithmetic and copies ran while one was open for 7% -> 4% of each run, Pallas kernels for 51% -> 73%
where the time goes in v3:
time: 1100 us; the launch traced here: 1090 us
  Pallas kernels  947 us (86%)
  waiting for transfers between devices  67.1 us (6%)
  other arithmetic  22.5 us (2%)
  local copies, waits for them, and re-layouts  18.6 us (2%)
  between operations  14.3 us (1%)
  matrix products  11.2 us (1%)
    pallas_call x7, Pallas kernels, half_back(): pl.pallas_call(functools.partial(half_back_kernel, near_only, partial is...  372 us
    pallas_call x3, Pallas kernels, attend_half(): pl.pallas_call(functools.partial(half_kernel, query_far, sides, carry is...  173 us
    pallas_call x2, Pallas kernels, ffn(): pl.pallas_call(functools.partial(ffn_kernel, step, before is not None), g...  126 us
    pallas_call x1, Pallas kernels, sum_all(): pl.pallas_call(sum_all_kernel, in_specs=[anywhere, whole], out_specs=[any...  97.7 us
    ppermute x6, waiting for transfers between devices, across(): return lax.ppermute(x, 'mp', [(0, 1), (1, 0)])  65.2 us
    pallas_call x1, Pallas kernels, middle(): pl.pallas_call(middle_kernel, grid=(rows // block,), in_specs=[tall(), ta...  25 us
    pallas_call x2, Pallas kernels, project(): pl.pallas_call(project_kernel, grid=(count // block,), in_specs=[pl.Block...  22.6 us
  transfers between devices with their start and end apart: 12, of which 5 were waited for; matrix products, arithmetic and copies ran while one was open for 4% of the time, Pallas kernels for 73%

profile of v3, /device:TPU:0, one launch (start us, length us, event | category | flops | bytes accessed | tf_op | source)
XLA Modules:
  0.0 1091.3 jit_solution(6481195160477720316)
XLA Ops:
  10.3 15.7 %enter.1 = (f32[2048,1024]{1,0:T(8,128)}, bf16[2048,1024]{1,0:T(8,128)(2,1)}) custom-call(bf16[2048,1024]{1,0:T(8,128)(2,1)} %x_ref.3, bf16[2048,1024]{1,0:T(8,128)(2,1)} %s_ref.3, bf16[2048,1024]{1,0:T(8,128)(2,1)} %w_ref.3, f32[1,1024]{1,0:T(1,128)} %bitcast.75, f32[1,1024]{1,0:T(1,128)} %bitcast.73), custom_call_target="tpu_custom_call" | custom-call | flops 134217728 | bytes 327680 | tf_op jit(solution)/shard_map/enter/pallas_call | solution.py:159
  26.1 7.6 collective-permute-done
  52.1 11.3 %project.2 = (bf16[512,2048]{1,0:T(8,128)(2,1)}, bf16[512,2048]{1,0:T(8,128)(2,1)}, bf16[512,2048]{1,0:T(8,128)(2,1)}) custom-call(bf16[2048,1024]{1,0:T(8,128)(2,1)} %get-tuple-element.77.x_ref.refs_0_, bf16[1536,1024]{1,0:T(8,128)(2,1)} %pad_maximum_fusion.w_ref, f32[32,2048]{1,0:T(8,128)} %get-tuple-element.145.cos_ref.refs_6_, ...), custom_call_target="tpu_custom_call" | custom-call | tf_op jit(solution)/shard_map/project/pallas_call | solution.py:94
  63.3 44.5 %near_near.1 = (f32[8,80,2048]{2,1,0:T(8,128)}, f32[8,1,2048]{2,1,0:T(1,128)}) custom-call(s32[8]{0:T(128)} %bitcast.60, s32[1]{0:T(128)} %bitcast.4.part_ref.dst_ref.refs_4_, bf16[512,2048]{1,0:T(8,128)(2,1)} %get-tuple-element.78.refs_0_, bf16[512,2048]{1,0:T(8,128)(2,1)} %get-tuple-element.79.refs_1_, bf16[512,2048]{1,0:T(8,128)(2,1)} %get-tuple-element.80.refs_2_), custom_call_target="tpu_custom_call" | custom-call | flops 536870912 | bytes 131072 | tf_op jit(solution)/shard_map/near_near/pallas_call | solution.py:496
  107.8 17.9 %collective-permute-done.2.x_ref.refs_2_ = bf16[2048,1024]{1,0:T(8,128)(2,1)} collective-permute-done((bf16[2048,1024]{1,0:T(8,128)(2,1)}, bf16[2048,1024]{1,0:T(8,128)(2,1)}, u32[]{:S(2)}, u32[]{:S(2)}) %collective-permute-start.2) | collective-permute-done | bytes 4194336 | tf_op jit(solution)/shard_map/ppermute | solution.py:1337
  126.6 11.3 %project.3 = (bf16[512,2048]{1,0:T(8,128)(2,1)}, bf16[512,2048]{1,0:T(8,128)(2,1)}, bf16[512,2048]{1,0:T(8,128)(2,1)}) custom-call(bf16[2048,1024]{1,0:T(8,128)(2,1)} %collective-permute-done.2.x_ref.refs_2_, bf16[1536,1024]{1,0:T(8,128)(2,1)} %pad_maximum_fusion.w_ref, f32[32,2048]{1,0:T(8,128)} %get-tuple-element.142.cos_ref.refs_14_, ...), custom_call_target="tpu_custom_call" | custom-call | tf_op jit(solution)/shard_map/project/pallas_call | solution.py:94
  137.9 84.1 %far_all.1 = (bf16[512,2048]{1,0:T(8,128)(2,1)}, f32[8,1,2048]{2,1,0:T(1,128)}) custom-call(s32[8]{0:T(128)} %bitcast.61, s32[1]{0:T(128)} %bitcast.4.part_ref.dst_ref.refs_4_, bf16[512,2048]{1,0:T(8,128)(2,1)} %get-tuple-element.89.refs_0_.refs_8_, bf16[512,2048]{1,0:T(8,128)(2,1)} %get-tuple-element.79.refs_1_, ...), custom_call_target="tpu_custom_call" | custom-call | flops 1073741824 | bytes 131072 | tf_op jit(solution)/shard_map/far_all/pallas_call | solution.py:496
  231.5 44.5 %near_far.1 = (bf16[512,2048]{1,0:T(8,128)(2,1)}, f32[8,1,2048]{2,1,0:T(1,128)}) custom-call(s32[8]{0:T(128)} %bitcast.62, s32[1]{0:T(128)} %bitcast.4.part_ref.dst_ref.refs_4_, bf16[512,2048]{1,0:T(8,128)(2,1)} %get-tuple-element.78.refs_0_, bf16[512,2048]{1,0:T(8,128)(2,1)} %get-tuple-element.84.refs_1_.refs_3_.refs_9_, ...), custom_call_target="tpu_custom_call" | custom-call | flops 536870912 | bytes 131072 | tf_op jit(solution)/shard_map/near_far/pallas_call | solution.py:496
  276.0 12.4 %collective-permute-done.3.in_ref = bf16[512,2048]{1,0:T(8,128)(2,1)S(1)} collective-permute-done((bf16[512,2048]{1,0:T(8,128)(2,1)}, bf16[512,2048]{1,0:T(8,128)(2,1)S(1)}, u32[]{:S(2)}, u32[]{:S(2)}) %collective-permute-start.3) | collective-permute-done | bytes 2097184 | tf_op jit(solution)/shard_map/ppermute | solution.py:1337
  289.8 14.0 %upper.1 = (f32[2048,1024]{1,0:T(8,128)}, bf16[2048,1024]{1,0:T(8,128)(2,1)}) custom-call(f32[2048,1024]{1,0:T(8,128)} %get-tuple-element.75.h_ref, bf16[512,2048]{1,0:T(8,128)(2,1)} %get-tuple-element.88.near_ref.refs_4_, bf16[512,2048]{1,0:T(8,128)(2,1)} %copy-done.1, bf16[512,1024]{1,0:T(8,128)(2,1)} %own_ref.3, bf16[512,1024]{1,0:T(8,128)(2,1)} %copy-done.2, ...), custom_call_target="tpu_custom_call" | custom-call | flops 67108864 | bytes 393216 | tf_op jit(solution)/shard_map/upper/pallas_call | solution.py:185
  303.8 62.9 %ffn_near.1 = (f32[2048,1024]{1,0:T(8,128)}, f32[2048,1024]{1,0:T(8,128)}, bf16[2,2,2304,1024]{3,2,1,0:T(8,128)(2,1)}, f32[1,1,2048]{2,1,0:T(1,128)}) custom-call(s32[1]{0:T(128)} %constant.32.clone.1.src_ref, s32[1]{0:T(128)} %bitcast.4.part_ref.dst_ref.refs_4_, bf16[2048,1024]{1,0:T(8,128)(2,1)} %get-tuple-element.93.n_ref, ...), custom_call_target="tpu_custom_call" | custom-call | flops 805306368 | bytes 262144 | tf_op jit(solution)/shard_map/ffn_near/pallas_call | solution.py:900
  366.8 63.2 %ffn_far.1 = (f32[2048,1024]{1,0:T(8,128)}, f32[2048,1024]{1,0:T(8,128)}, bf16[2,2,2304,1024]{3,2,1,0:T(8,128)(2,1)}, f32[1,1,2048]{2,1,0:T(1,128)}) custom-call(s32[1]{0:T(128)S(6)} %sub.16.src_ref.dst_ref, s32[1]{0:T(128)S(6)} %sub.16.src_ref.dst_ref, bf16[2048,1024]{1,0:T(8,128)(2,1)} %get-tuple-element.93.n_ref, ...), custom_call_target="tpu_custom_call", output_to_operand_aliasing={{2}: (9, {})} | custom-call | flops 805306368 | bytes 262144 | tf_op jit(solution)/shard_map/ffn_far/pallas_call | solution.py:900
  430.0 25.0 %middle.1 = (f32[2048,1024]{1,0:T(8,128)}, f32[2048,1024]{1,0:T(8,128)}, bf16[2048,1024]{1,0:T(8,128)(2,1)}, bf16[512,2048]{1,0:T(8,128)(2,1)}, bf16[512,2048]{1,0:T(8,128)(2,1)}, /*index=5*/f32[3,1024]{1,0:T(4,128)}) custom-call(f32[2048,1024]{1,0:T(8,128)} %get-tuple-element.92.h_ref, f32[2048,1024]{1,0:T(8,128)} %get-tuple-element.100.branch_ref, ...), custom_call_target="tpu_custom_call" | custom-call | flops 67108864 | bytes 786432 | tf_op jit(solution)/shard_map/middle/pallas_call | solution.py:225
  455.0 10.0 out_back.1
  465.4 48.9 %back_near0.1.refs_16_ = f32[3,8,64,2048]{3,2,1,0:T(8,128)} custom-call(s32[8]{0:T(128)} %bitcast.63, s32[1]{0:T(128)} %bitcast.4.part_ref.dst_ref.refs_4_, bf16[512,2048]{1,0:T(8,128)(2,1)} %get-tuple-element.78.refs_0_, bf16[512,2048]{1,0:T(8,128)(2,1)} %get-tuple-element.79.refs_1_, bf16[512,2048]{1,0:T(8,128)(2,1)} %get-tuple-element.80.refs_2_, ...), custom_call_target="tpu_custom_call" | custom-call | flops 671088640 | bytes 327680 | tf_op jit(solution)/shard_map/back_near0/pallas_call | solution.py:786
  514.2 9.6 collective-permute-done.4.refs_11_
  525.1 62.1 %back_first0.1 = (bf16[3,8,64,2048]{3,2,1,0:T(8,128)(2,1)}, bf16[3,8,64,2048]{3,2,1,0:T(8,128)(2,1)}) custom-call(s32[8]{0:T(128)} %bitcast.64, s32[1]{0:T(128)} %bitcast.4.part_ref.dst_ref.refs_4_, bf16[512,2048]{1,0:T(8,128)(2,1)} %get-tuple-element.78.refs_0_, bf16[512,2048]{1,0:T(8,128)(2,1)} %get-tuple-element.79.refs_1_, ...), custom_call_target="tpu_custom_call" | custom-call | flops 1006632960 | bytes 163840 | tf_op jit(solution)/shard_map/back_first0/pallas_call | solution.py:786
  587.2 33.6 %back_first1.1 = (bf16[3,8,64,2048]{3,2,1,0:T(8,128)(2,1)}, bf16[3,8,64,2048]{3,2,1,0:T(8,128)(2,1)}) custom-call(s32[8]{0:T(128)} %bitcast.65, s32[1]{0:T(128)} %bitcast.4.part_ref.dst_ref.refs_4_, bf16[512,2048]{1,0:T(8,128)(2,1)} %get-tuple-element.78.refs_0_, ...), custom_call_target="tpu_custom_call", output_to_operand_aliasing={{0}: (19, {}), {1}: (20, {})} | custom-call | flops 503316480 | bytes 81920 | tf_op jit(solution)/shard_map/back_first1/pallas_call | solution.py:786
  620.8 33.5 %back_first2.1 = (bf16[3,8,64,2048]{3,2,1,0:T(8,128)(2,1)}, bf16[3,8,64,2048]{3,2,1,0:T(8,128)(2,1)}) custom-call(s32[8]{0:T(128)} %bitcast.66, s32[1]{0:T(128)} %bitcast.4.part_ref.dst_ref.refs_4_, bf16[512,2048]{1,0:T(8,128)(2,1)} %get-tuple-element.78.refs_0_, ...), custom_call_target="tpu_custom_call", output_to_operand_aliasing={{0}: (19, {}), {1}: (20, {})} | custom-call | flops 503316480 | bytes 81920 | tf_op jit(solution)/shard_map/back_first2/pallas_call | solution.py:786
  654.9 70.8 %back_second0.1 = (bf16[3,8,64,2048]{3,2,1,0:T(8,128)(2,1)}, f32[3,8,64,2048]{3,2,1,0:T(8,128)}) custom-call(s32[8]{0:T(128)} %bitcast.67, s32[1]{0:T(128)} %bitcast.4.part_ref.dst_ref.refs_4_, bf16[512,2048]{1,0:T(8,128)(2,1)} %get-tuple-element.78.refs_0_, bf16[512,2048]{1,0:T(8,128)(2,1)} %get-tuple-element.79.refs_1_, ...), custom_call_target="tpu_custom_call", output_to_operand_aliasing={{0}: (18, {})} | custom-call | flops 1006632960 | bytes 163840 | tf_op jit(solution)/shard_map/back_second0/pallas_call | solution.py:786
  725.7 74.1 %back_second1.1 = (bf16[3,8,64,2048]{3,2,1,0:T(8,128)(2,1)}, f32[3,8,64,2048]{3,2,1,0:T(8,128)}) custom-call(s32[8]{0:T(128)} %bitcast.68, s32[1]{0:T(128)} %bitcast.4.part_ref.dst_ref.refs_4_, bf16[512,2048]{1,0:T(8,128)(2,1)} %get-tuple-element.78.refs_0_, ...), custom_call_target="tpu_custom_call", output_to_operand_aliasing={{0}: (18, {}), {1}: (19, {})} | custom-call | flops 1006632960 | bytes 163840 | tf_op jit(solution)/shard_map/back_second1/pallas_call | solution.py:786
  799.8 11.2 %convolution_convert_fusion.refs_10_ = bf16[2048,1024]{1,0:T(8,128)(2,1)} fusion(bf16[1536,2048]{1,0:T(8,128)(2,1)} %bitcast.44, bf16[512,1024]{1,0:T(8,128)(2,1)S(1)} %bitcast.53, bf16[512,1024]{1,0:T(8,128)(2,1)S(1)} %bitcast.55, bf16[512,1024]{1,0:T(8,128)(2,1)S(1)} %bitcast.57), kind=kOutput, calls=%fused_computation.1 | convolution fusion | flops 6453985280 | bytes 13631488 | tf_op jit(solution)/shard_map/dot_general | solution.py:26
  815.9 49.2 %back_near1.1 = bf16[3,8,64,2048]{3,2,1,0:T(8,128)(2,1)} custom-call(s32[8]{0:T(128)} %bitcast.69, s32[1]{0:T(128)} %bitcast.4.part_ref.dst_ref.refs_4_, bf16[512,2048]{1,0:T(8,128)(2,1)} %get-tuple-element.78.refs_0_, bf16[512,2048]{1,0:T(8,128)(2,1)} %get-tuple-element.79.refs_1_, ...), custom_call_target="tpu_custom_call", output_to_operand_aliasing={{}: (11, {})} | custom-call | flops 671088640 | bytes 327680 | tf_op jit(solution)/shard_map/back_near1/pallas_call | solution.py:786
  865.1 19.4 %project_back.1.refs_0_ = bf16[1536,1024]{1,0:T(8,128)(2,1)} custom-call(bf16[2048,1024]{1,0:T(8,128)(2,1)} %get-tuple-element.77.x_ref.refs_0_, bf16[1536,2048]{1,0:T(8,128)(2,1)} %bitcast.42, bf16[2048,1024]{1,0:T(8,128)(2,1)} %collective-permute-done.2.x_ref.refs_2_, bf16[1536,2048]{1,0:T(8,128)(2,1)} %bitcast.45, s32[1]{0:T(128)} %bitcast.4.part_ref.dst_ref.refs_4_), custom_call_target="tpu_custom_call" | custom-call | flops 201326592 | bytes 196608 | tf_op jit(solution)/shard_map/project_back/pallas_call | solution.py:992
  884.5 17.6 %collective-permute-done.5.sent_ref.refs_1_ = bf16[2048,1024]{1,0:T(8,128)(2,1)} collective-permute-done((bf16[2048,1024]{1,0:T(8,128)(2,1)}, bf16[2048,1024]{1,0:T(8,128)(2,1)}, u32[]{:S(2)}, u32[]{:S(2)}) %collective-permute-start.5) | collective-permute-done | bytes 4194336 | tf_op jit(solution)/shard_map/ppermute | solution.py:1337
  902.1 7.3 hold.1.own_ref
  909.4 18.5 %leave.1 = (bf16[2048,1024]{1,0:T(8,128)(2,1)}, f32[2,1024]{1,0:T(2,128)}) custom-call(bf16[1536,2048]{1,0:T(8,128)(2,1)} %bitcast.43, bf16[1536,1024]{1,0:T(8,128)(2,1)} %pad_maximum_fusion.w_ref, bf16[2048,1024]{1,0:T(8,128)(2,1)} %collective-permute-done.5.sent_ref.refs_1_, f32[2048,1024]{1,0:T(8,128)} %get-tuple-element.75.h_ref, ...), custom_call_target="tpu_custom_call" | custom-call | flops 100663296 | bytes 524288 | tf_op jit(solution)/shard_map/leave/pallas_call | solution.py:258
  928.6 14.1 %concat_back.1.big_ref = bf16[2048,1024]{1,0:T(8,128)(2,1)} custom-call(bf16[2048,1024]{1,0:T(8,128)(2,1)} %x_ref.3, bf16[2048,1024]{1,0:T(8,128)(2,1)} %s_ref.3, bf16[2048,1024]{1,0:T(8,128)(2,1)} %get-tuple-element.120.grad_ref), custom_call_target="tpu_custom_call" | custom-call | flops 134217728 | bytes 262144 | tf_op jit(solution)/shard_map/concat_back/pallas_call | solution.py:1247
  943.4 97.7 %sum_all.1 = (bf16[2048,1024]{1,0:T(8,128)(2,1)}, f32[16,1024]{1,0:T(8,128)}) custom-call(bf16[2048,1024]{1,0:T(8,128)(2,1)} %concat_back.1.big_ref, f32[16,1024]{1,0:T(8,128)} %select_maximum_fusion.small_ref), custom_call_target="tpu_custom_call" | custom-call | flops 32768 | bytes 262144 | tf_op jit(solution)/shard_map/sum_all/pallas_call | solution.py:1176
  1041.1 6.7 convert_element_type.35
  1048.4 14.1 %join_back.1 = (f32[2048,1024]{1,0:T(8,128)}, f32[2048,1024]{1,0:T(8,128)}) custom-call(bf16[2048,1024]{1,0:T(8,128)(2,1)} %get-tuple-element.120.grad_ref, bf16[2048,1024]{1,0:T(8,128)(2,1)} %w_ref.3), custom_call_target="tpu_custom_call" | custom-call | flops 33554432 | bytes 262144 | tf_op jit(solution)/shard_map/join_back/pallas_call | solution.py:1220
  1072.9 11.6 %unpack.1 = (f32[1024,2048]{1,0:T(8,128)}, f32[2048,1024]{1,0:T(8,128)}) custom-call(s32[1]{0:T(128)} %bitcast.28.core_ref, bf16[2304,1024]{1,0:T(8,128)(2,1)} %hold.1.own_ref, bf16[2304,1024]{1,0:T(8,128)(2,1)} %collective-permute-done.6.sibling_ref), custom_call_target="tpu_custom_call" | custom-call | flops 32768 | bytes 393216 | tf_op jit(solution)/shard_map/unpack/pallas_call | solution.py:1296
  (94 shorter events, 52.5 us)
Async XLA Ops:
  7.2 359.6 %all-gather.5.cloned.1.call-start = ((), (), s32[]{:S(2)}) async-start(), calls=%async_computation.4 | async-start | bytes 10485760 | tf_op jit(solution)/shard_map/all_gather | solution.py:1351
  7.2 26.5 %collective-permute-start.1 = (bf16[512,1024]{1,0:T(8,128)(2,1)}, bf16[512,1024]{1,0:T(8,128)(2,1)S(1)}, u32[]{:S(2)}, u32[]{:S(2)}) collective-permute-start(bf16[512,1024]{1,0:T(8,128)(2,1)} %own_ref.3), channel_id=1, source_target_pairs={{0,1},{1,0},{2,3},{3,2},{4,5},{5,4},{6,7},{7,6},{8,9},{9,8},{10,11... | collective-permute-start | bytes 3145736 | tf_op jit(solution)/shard_map/ppermute | solution.py:1337
  10.2 23.5 %collective-permute-start = (bf16[2048]{0:T(1024)(128)(2,1)}, bf16[2048]{0:T(1024)(128)(2,1)S(1)}, u32[]{:S(2)}, u32[]{:S(2)}) collective-permute-start(bf16[2048]{0:T(1024)(128)(2,1)} %param.31), channel_id=1, source_target_pairs={{0,1},{1,0},{2,3},{3,2},{4,5},{5,4},{6,7},{7,6},{8,9},{9,8},{10,11... | collective-permute-start | bytes 12296 | tf_op jit(solution)/shard_map/ppermute | solution.py:1337
  10.3 25.1 %copy-start.17 = (s32[1,8]{1,0:T(1,128)S(1)}, s32[1,8]{1,0:T(1,128)}, u32[]{:S(2)}) copy-start(s32[1,8]{1,0:T(1,128)} %param.20) | copy-start | bytes 100
  10.3 25.3 %copy-start.8 = (bf16[1024,512]{1,0:T(8,128)(2,1)S(1)}, bf16[1024,512]{1,0:T(8,128)(2,1)}, u32[]{:S(2)}) copy-start(bf16[1024,512]{1,0:T(8,128)(2,1)} %param.26) | copy-start | bytes 3145732
  33.7 10.4 copy-start.2
  33.7 92.1 %collective-permute-start.2 = (bf16[2048,1024]{1,0:T(8,128)(2,1)}, bf16[2048,1024]{1,0:T(8,128)(2,1)}, u32[]{:S(2)}, u32[]{:S(2)}) collective-permute-start(bf16[2048,1024]{1,0:T(8,128)(2,1)} %get-tuple-element.77.x_ref.refs_0_), channel_id=1, source_target_pairs={{0,1},{1,0},{2,3},{3,2},{4,5},{5,4},{6,7},{7,6},{8,9},{9,8},{10,11... | collective-permute-start | bytes 12582920 | tf_op jit(solution)/shard_map/ppermute | solution.py:1337
  35.6 8.5 copy-start.9
  36.2 11.2 %copy-start.3 = (bf16[1024,512]{0,1:T(8,128)(2,1)}, bf16[1024,512]{0,1:T(8,128)(2,1)S(1)}, u32[]{:S(2)}) copy-start(bf16[1024,512]{0,1:T(8,128)(2,1)S(1)} %copy.53) | copy-start | bytes 3145732
  38.0 9.3 copy-start.5
  44.1 3.3 copy-start.7
  125.8 241.0 %all-gather.7.cloned.1.call-start = ((), (), s32[]{:S(2)}) async-start(), calls=%async_computation.5 | async-start | bytes 10485760 | tf_op jit(solution)/shard_map/all_gather | solution.py:1351
  126.5 494.3 %reduce-scatter.2.cloned.1.call-start = ((), (), s32[]{:S(2)}) async-start(), calls=%async_computation.1 | async-start | bytes 23592960 | tf_op jit(solution)/shard_map/reduce_scatter | solution.py:1439
  137.9 84.2 %copy-start.10 = (s32[8,1]{0,1:T(1,128)S(1)}, s32[8,1]{0,1:T(1,128)}, u32[]{:S(2)}) copy-start(s32[8,1]{0,1:T(1,128)} %copy-done.9) | copy-start | bytes 100
  137.9 84.7 %copy-start.16 = (bf16[2048]{0:T(1024)(128)(2,1)S(1)}, bf16[2048]{0:T(1024)(128)(2,1)}, u32[]{:S(2)}) copy-start(bf16[2048]{0:T(1024)(128)(2,1)} %param.31) | copy-start | bytes 12292
  222.0 66.4 %collective-permute-start.3 = (bf16[512,2048]{1,0:T(8,128)(2,1)}, bf16[512,2048]{1,0:T(8,128)(2,1)S(1)}, u32[]{:S(2)}, u32[]{:S(2)}) collective-permute-start(bf16[512,2048]{1,0:T(8,128)(2,1)} %get-tuple-element.90.refs_12_), channel_id=1, source_target_pairs={{0,1},{1,0},{2,3},{3,2},{4,5},{5,4},{6,7},{7,6},{8,9},{9,8},{10,11... | collective-permute-start | bytes 6291464 | tf_op jit(solution)/shard_map/ppermute | solution.py:1337
  288.5 1.3 copy-start.1
  465.0 58.8 %collective-permute-start.4 = (bf16[512,2048]{1,0:T(8,128)(2,1)}, bf16[512,2048]{1,0:T(8,128)(2,1)S(1)}, u32[]{:S(2)}, u32[]{:S(2)}) collective-permute-start(bf16[512,2048]{1,0:T(8,128)(2,1)} %get-tuple-element.105), channel_id=1, source_target_pairs={{0,1},{1,0},{2,3},{3,2},{4,5},{5,4},{6,7},{7,6},{8,9},{9,8},{10,11... | collective-permute-start | bytes 6291464 | tf_op jit(solution)/shard_map/ppermute | solution.py:1337
  523.8 1.3 copy-start
  654.3 247.8 %all-reduce.6.cloned.1.call-start = ((), (), s32[]{:S(2)}) async-start(), calls=%async_computation.3 | async-start | bytes 9437184 | tf_op jit(solution)/shard_map/psum | solution.py:1442
  725.6 74.2 %copy-start.4 = (bf16[1024,512]{0,1:T(8,128)(2,1)S(1)}, bf16[1024,512]{0,1:T(8,128)(2,1)}, u32[]{:S(2)}) copy-start(bf16[1024,512]{0,1:T(8,128)(2,1)} %copy-done.3) | copy-start | bytes 3145732
  725.7 74.2 %copy-start.6 = (bf16[1024,512]{0,1:T(8,128)(2,1)S(1)}, bf16[1024,512]{0,1:T(8,128)(2,1)}, u32[]{:S(2)}) copy-start(bf16[1024,512]{0,1:T(8,128)(2,1)} %copy-done.5) | copy-start | bytes 3145732
  811.0 91.1 %collective-permute-start.5 = (bf16[2048,1024]{1,0:T(8,128)(2,1)}, bf16[2048,1024]{1,0:T(8,128)(2,1)}, u32[]{:S(2)}, u32[]{:S(2)}) collective-permute-start(bf16[2048,1024]{1,0:T(8,128)(2,1)} %convolution_convert_fusion.refs_10_), channel_id=1, source_target_pairs={{0,1},{1,0},{2,3},{3,2},{4,5},{5,4},{6,7},{7,6},{8,9},{9,8},{10,11... | collective-permute-start | bytes 12582920 | tf_op jit(solution)/shard_map/ppermute | solution.py:1337
  909.4 160.8 %collective-permute-start.6 = (bf16[2304,1024]{1,0:T(8,128)(2,1)}, bf16[2304,1024]{1,0:T(8,128)(2,1)}, u32[]{:S(2)}, u32[]{:S(2)}) collective-permute-start(bf16[2304,1024]{1,0:T(8,128)(2,1)} %hold.1.own_ref), channel_id=1, source_target_pairs={{0,2},{2,0},{1,3},{3,1},{4,6},{6,4},{5,7},{7,5},{8,10},{10,8},{9,1... | collective-permute-start | bytes 14155784 | tf_op jit(solution)/shard_map/ppermute | solution.py:1431
  909.4 19.1 %copy-start.13 = (f32[1,1,2048]{2,1,0:T(1,128)S(1)}, f32[1,1,2048]{2,1,0:T(1,128)}, u32[]{:S(2)}) copy-start(f32[1,1,2048]{2,1,0:T(1,128)} %get-tuple-element.125) | copy-start | bytes 24580
  909.4 19.1 %copy-start.14 = (f32[1,1,2048]{2,1,0:T(1,128)S(1)}, f32[1,1,2048]{2,1,0:T(1,128)}, u32[]{:S(2)}) copy-start(f32[1,1,2048]{2,1,0:T(1,128)} %get-tuple-element.126) | copy-start | bytes 24580
  927.9 136.4 %all-reduce.4.cloned.1.call-start = ((), (), s32[]{:S(2)}) async-start(), calls=%async_computation.2 | async-start | bytes 6291456 | tf_op jit(solution)/shard_map/psum | solution.py:1494
  928.6 14.1 %copy-start.12 = (f32[3,1024]{1,0:T(4,128)S(1)}, f32[3,1024]{1,0:T(4,128)}, u32[]{:S(2)}) copy-start(f32[3,1024]{1,0:T(4,128)} %get-tuple-element.123) | copy-start | bytes 36868
  928.6 14.1 %copy-start.15 = (f32[2,1024]{1,0:T(2,128)S(1)}, f32[2,1024]{1,0:T(2,128)}, u32[]{:S(2)}) copy-start(f32[2,1024]{1,0:T(2,128)} %get-tuple-element.124) | copy-start | bytes 24580
  1041.1 6.7 copy-start.11
Sparse Core Ops, SparseCore 0:
  125.9 59.4 all-gather.4
  187.0 77.7 all-gather.6
  465.1 149.5 reduce-scatter.1
  658.8 176.3 all-reduce.5
  932.4 112.7 all-reduce.3

commit v4 on v3

--- a/solution.py
+++ b/solution.py
@@ -83,14 +83,12 @@
     v_ref[...] = dot_nt(w_ref[2 * width :, :], x).astype(BF)
 
 
-def project(x, w, cosine, sine, first=0, written=()):
+def project(x, w, cosine, sine, after=()):
     count, depth = x.shape
-    total = cosine.shape[1]
     width = w.shape[0] // 3
     block = min(512, count)
-    start = first // block
-    table = pl.BlockSpec((HALF, block), lambda i: (0, i + start))
-    out = pl.BlockSpec((width, block), lambda i: (0, i + start))
+    table = pl.BlockSpec((HALF, block), lambda i: (0, i))
+    out = pl.BlockSpec((width, block), lambda i: (0, i))
     return pl.pallas_call(
         project_kernel,
         grid=(count // block,),
@@ -100,13 +98,12 @@
             table,
             table,
         ]
-        + [pl.BlockSpec(memory_space=pl.ANY)] * len(written),
+        + [pl.BlockSpec(memory_space=pl.ANY)] * len(after),
         out_specs=[out] * 3,
-        out_shape=[jax.ShapeDtypeStruct((width, total), BF)] * 3,
-        input_output_aliases={4 + i: i for i in range(len(written))},
+        out_shape=[jax.ShapeDtypeStruct((width, count), BF)] * 3,
         compiler_params=params(),
         name="project",
-    )(x, w, cosine, sine, *written)
+    )(x, w, cosine, sine, *after)
 
 
 def scale_of(stream):
@@ -154,7 +151,7 @@
 
 def enter(x, skip, w, bias, gain, first, count, written=()):
     rows, width = x.shape
-    block = min(256, count)
+    block = min(512, count)
     tall, whole = row_specs(rows, width, block, first // block)
     return pl.pallas_call(
         enter_kernel,
@@ -179,7 +176,7 @@
 
 def upper(h0, near, arrived, own, far, bias, gain):
     rows, width = h0.shape
-    block = min(256, rows)
+    block = min(512, rows)
     tall, whole = row_specs(rows, width, block)
     flat = pl.BlockSpec((near.shape[0], block), lambda i: (0, i))
     return pl.pallas_call(
@@ -219,7 +216,7 @@
 
 def middle(h1, branch, dn, cotangent, valid, bias, gain, own, far):
     rows, width = h1.shape
-    block = min(256, rows)
+    block = min(512, rows)
     tall, whole = row_specs(rows, width, block)
     flat = pl.BlockSpec((own.shape[0], block), lambda i: (0, i))
     return pl.pallas_call(
@@ -253,7 +250,7 @@
 
 def leave(back, w, sent, h0, dh1, gain, after):
     rows, width = h0.shape
-    block = min(256, rows)
+    block = min(512, rows)
     tall, whole = row_specs(rows, width, block)
     return pl.pallas_call(
         leave_kernel,
@@ -970,15 +967,15 @@
 
 
 def project_back_kernel(*refs):
-    out_ref = refs[-1]
-    pairs = refs[:-2]
+    out_ref = refs[-2]
+    pairs = refs[:-3]
     total = dot(pairs[1][...], pairs[0][...])
     for i in range(2, len(pairs), 2):
         total = total + dot(pairs[i + 1][...], pairs[i][...])
     out_ref[...] = total.astype(BF)
 
 
-def project_back(pairs, after):
+def project_back(pairs, passed):
     total = pairs[0][1].shape[0]
     depth = pairs[0][0].shape[1]
     block = total // 3
@@ -993,12 +990,19 @@
         project_back_kernel,
         grid=(3,),
         in_specs=specs + [pl.BlockSpec(memory_space=pl.ANY)],
-        out_specs=pl.BlockSpec((block, depth), lambda i: (i, 0)),
-        out_shape=jax.ShapeDtypeStruct((total, depth), BF),
+        out_specs=[
+            pl.BlockSpec((block, depth), lambda i: (i, 0)),
+            pl.BlockSpec(memory_space=pl.ANY),
+        ],
+        out_shape=[
+            jax.ShapeDtypeStruct((total, depth), BF),
+            jax.ShapeDtypeStruct(passed.shape, passed.dtype),
+        ],
+        input_output_aliases={len(operands): 1},
         compiler_params=params(),
         name="project_back",
         cost_estimate=cost(4 * pairs[0][0].shape[0] * depth * total, 8 * depth * total),
-    )(*operands, after)
+    )(*operands, passed)
 
 
 def turn_kernel(x_ref, *out_refs):
@@ -1029,16 +1033,18 @@
 
 def sum_all_kernel(
     big_ref, small_ref, out_ref, small_out_ref,
-    buf, done, core_in, x_in, y_in, z_in, small, small_in, small_z, local, send, recv, small_send, small_recv,
+    buf, done, core_in, first_in, second_in, z_in, small, small_in, small_z,
+    local, send, recv, small_send, small_recv,
 ):
     o, c, m = lax.axis_index("dpo"), lax.axis_index("core"), lax.axis_index("mp")
     y, z = lax.rem(o, 2), lax.div(o, 2)
     zs = 4
-    half = buf.shape[0] // 2
-    quarter, eighth, last = half // 2, half // 4, half // 16
+    size = buf.shape[0] // 2
+    half, quarter, eighth, last = size // 2, size // 4, size // 8, size // 32
     sibling = (o, 1 - c, m)
     across = (o, c, 1 - m)
     beside = (z * 2 + 1 - y, c, m)
+    others = [lax.rem(z + d, zs) for d in range(1, zs)]
 
     def along(j):
         return (j * 2 + y, c, m)
@@ -1046,130 +1052,137 @@
     load = pltpu.make_async_copy(big_ref, buf, local.at[0])
     load.start()
     barrier = pltpu.get_barrier_semaphore()
-    others = [lax.rem(z + d, zs) for d in range(1, zs)]
     for device in [sibling, across, beside] + [along(j) for j in others]:
         pl.semaphore_signal(barrier, inc=1, device_id=device, device_id_type=MESH)
     pl.semaphore_wait(barrier, 6)
     small[0] = small_ref[...]
-    load.wait()
-
-    def copy(src, dst, i, device, sems=(send, recv)):
+
+    main, tiny = (send, recv), (small_send, small_recv)
+    started = []
+
+    def copy(src, dst, sems, i, device):
         return pltpu.make_async_remote_copy(
             src_ref=src, dst_ref=dst, send_sem=sems[0].at[i], recv_sem=sems[1].at[i],
             device_id=device, device_id_type=MESH,
         )
 
-    def rows(first, n, of=buf):
-        return of.at[pl.ds(pl.multiple_of(first, last), n)]
-
-    def back(first, n, i, device):
-        return copy(rows(first, n, done), rows(first, n, done), i, device)
-
-    def add(first, n, arrived):
-        step = min(128, n)
-
-        def one(i, carry):
-            there = pl.ds(pl.multiple_of(first + i * step, last), step)
-            here = pl.ds(pl.multiple_of(i * step, step), step)
-            buf[there, :] = (
-                buf[there, :].astype(F32) + arrived[here, :].astype(F32)
-            ).astype(BF)
-            return carry
-
-        lax.fori_loop(0, n // step, one, 0)
-
-    started = []
-
-    def go(*args, **kwargs):
-        one = copy(*args, **kwargs)
+    def go(src, dst, sems, i, device):
+        one = copy(src, dst, sems, i, device)
         one.start()
         started.append(one)
         return one
 
-    tiny = (small_send, small_recv)
-    mine = c * half
-    theirs = (1 - c) * half
-    core_a = go(rows(theirs + (1 - m) * quarter, quarter), core_in.at[0], 0, sibling)
-    core_b = go(rows(theirs + m * quarter, quarter), core_in.at[1], 1, sibling)
-    tiny_core = go(small.at[0], small_in.at[0], 0, sibling, sems=tiny)
-    base_far, base = mine + (1 - m) * quarter, mine + m * quarter
-    core_a.wait_recv()
-    add(base_far, quarter, core_in.at[0])
-    x_a = go(rows(base_far + (1 - y) * eighth, eighth), x_in.at[0], 2, across)
-    x_b = go(rows(base_far + y * eighth, eighth), x_in.at[1], 3, across)
+    def rows(first, n, of=buf):
+        return of.at[pl.ds(pl.multiple_of(first, last), n)]
+
+    def add(first, n, got):
+        def one(i, carry):
+            there = pl.ds(pl.multiple_of(first + i * 128, last), 128)
+            here = pl.ds(pl.multiple_of(i * 128, 128), 128)
+            buf[there, :] = (buf[there, :].astype(F32) + got[here, :].astype(F32)).astype(BF)
+            return carry
+
+        lax.fori_loop(0, n // 128, one, 0)
+
+    turn_of = ((m, y), (y, m))
+    device_of = ((across, beside), (beside, across))
+    far, near, far_next, near_next, own, theirs = [], [], [], [], [], []
+    for s in range(2):
+        a, b = turn_of[s]
+        mine = s * size + c * half
+        theirs.append(s * size + (1 - c) * half)
+        far.append(mine + (1 - a) * quarter)
+        near.append(mine + a * quarter)
+        far_next.append(near[s] + (1 - b) * eighth)
+        near_next.append(near[s] + b * eighth)
+        own.append(near_next[s] + z * last)
+
+    load.wait()
+    arrivals = []
+    for part in range(2):
+        for s in range(2):
+            a = turn_of[s][0]
+            start = theirs[s] + ((1 - a) if part == 0 else a) * quarter
+            i = 2 * part + s
+            arrivals.append(go(rows(start, quarter), core_in.at[i], main, i, sibling))
+    tiny_core = go(small.at[0], small_in.at[0], tiny, 0, sibling)
+    firsts = []
+    for s in range(2):
+        arrivals[s].wait_recv()
+        add(far[s], quarter, core_in.at[s])
+        firsts.append(go(rows(far[s], quarter), first_in.at[s], main, 4 + s, device_of[s][0]))
     tiny_core.wait_recv()
     small[1] = small[0] + small_in[0]
-    tiny_x = go(small.at[1], small_in.at[1], 1, across, sems=tiny)
-    core_b.wait_recv()
-    add(base, quarter, core_in.at[1])
-    far_y, near_y = base + (1 - y) * eighth, base + y * eighth
-    x_a.wait_recv()
-    add(far_y, eighth, x_in.at[0])
-    y_a = go(rows(far_y, eighth), y_in, 4, beside)
+    tiny_x = go(small.at[1], small_in.at[1], tiny, 1, across)
+    for s in range(2):
+        arrivals[2 + s].wait_recv()
+        add(near[s], quarter, core_in.at[2 + s])
     tiny_x.wait_recv()
     small[2] = small[1] + small_in[1]
-    tiny_y = go(small.at[2], small_in.at[2], 2, beside, sems=tiny)
-    x_b.wait_recv()
-    add(near_y, eighth, x_in.at[1])
-    y_a.wait_recv()
-    add(near_y, eighth, y_in)
-    for d in range(1, zs):
-        j = lax.rem(z + d, zs)
-        there = copy(rows(near_y + j * last, last), z_in.at[z], 5 + z, along(j))
-        there.start()
-        started.append(there)
+    tiny_y = go(small.at[2], small_in.at[2], tiny, 2, beside)
+    seconds = []
+    for s in range(2):
+        firsts[s].wait_recv()
+        add(near[s], quarter, first_in.at[s])
+        seconds.append(go(rows(far_next[s], eighth), second_in.at[s], main, 6 + s, device_of[s][1]))
     tiny_y.wait_recv()
     small_z[z] = small[2] + small_in[2]
-    for d in range(1, zs):
-        j = lax.rem(z + d, zs)
-        there = copy(small_z.at[z], small_z.at[z], 3 + z, along(j), sems=tiny)
-        there.start()
-        started.append(there)
-    own = near_y + z * last
-    total = buf[pl.ds(pl.multiple_of(own, last), last), :].astype(F32)
-    for d in range(1, zs):
-        j = lax.rem(z + d, zs)
-        copy(rows(own, last), z_in.at[j], 5 + j, along(j)).wait_recv()
-        total = total + z_in[j].astype(F32)
-    done[pl.ds(pl.multiple_of(own, last), last), :] = total.astype(BF)
+    for j in others:
+        go(small_z.at[z], small_z.at[z], tiny, 3 + z, along(j))
+    for s in range(2):
+        seconds[s].wait_recv()
+        add(near_next[s], eighth, second_in.at[s])
+        for j in others:
+            go(
+                rows(near_next[s] + j * last, last), z_in.at[s, z], main, 8 + 4 * s + z, along(j)
+            )
 
     def hand(first, n, i, device):
-        one = back(first, n, i, device)
-        one.start()
-        started.append(one)
-        return one
-
-    for d in range(1, zs):
-        hand(own, last, 9 + z, along(lax.rem(z + d, zs)))
-    for d in range(1, zs):
-        j = lax.rem(z + d, zs)
-        back(near_y + j * last, last, 9 + j, along(j)).wait_recv()
-    y_back = hand(near_y, eighth, 13, beside)
-    x_back = hand(near_y, eighth, 14, across)
-    core_back = hand(near_y, eighth, 15, sibling)
-    y_back.wait_recv()
-    x_more = hand(far_y, eighth, 16, across)
-    core_more = hand(far_y, eighth, 17, sibling)
-    x_back.wait_recv()
-    core_x = hand(base_far + y * eighth, eighth, 18, sibling)
-    x_more.wait_recv()
-    core_y = hand(base_far + (1 - y) * eighth, eighth, 19, sibling)
-    for d in range(1, zs):
-        j = lax.rem(z + d, zs)
-        copy(small_z.at[j], small_z.at[j], 3 + j, along(j), sems=tiny).wait_recv()
+        there = rows(first, n, done)
+        return go(there, there, main, i, device)
+
+    for s in range(2):
+        total = buf[pl.ds(pl.multiple_of(own[s], last), last), :].astype(F32)
+        for j in others:
+            copy(z_in.at[s, j], z_in.at[s, j], main, 8 + 4 * s + j, along(j)).wait_recv()
+            total = total + z_in[s, j].astype(F32)
+        done[pl.ds(pl.multiple_of(own[s], last), last), :] = total.astype(BF)
+        for j in others:
+            hand(own[s], last, 16 + 4 * s + z, along(j))
+    back_second, back_first, cores = [], [], []
+    for s in range(2):
+        for j in others:
+            there = rows(near_next[s] + j * last, last, done)
+            copy(there, there, main, 16 + 4 * s + j, along(j)).wait_recv()
+        back_second.append(hand(near_next[s], eighth, 24 + s, device_of[s][1]))
+        back_first.append(hand(near_next[s], eighth, 26 + s, device_of[s][0]))
+        cores.append(hand(near_next[s], eighth, 28 + s, sibling))
+    back_more = []
+    for s in range(2):
+        back_second[s].wait_recv()
+        back_more.append(hand(far_next[s], eighth, 30 + s, device_of[s][0]))
+        cores.append(hand(far_next[s], eighth, 32 + s, sibling))
+    for j in others:
+        copy(small_z.at[j], small_z.at[j], tiny, 3 + j, along(j)).wait_recv()
     small_out_ref[...] = (small_z[0] + small_z[1]) + (small_z[2] + small_z[3])
-    for one in (core_back, core_more, core_x, core_y):
+    for s in range(2):
+        back_first[s].wait_recv()
+        cores.append(hand(far[s] + turn_of[s][1] * eighth, eighth, 34 + s, sibling))
+    for s in range(2):
+        back_more[s].wait_recv()
+        cores.append(hand(far[s] + (1 - turn_of[s][1]) * eighth, eighth, 36 + s, sibling))
+    for one in cores:
         one.wait_recv()
+    store = pltpu.make_async_copy(done, out_ref, local.at[1])
+    store.start()
     for one in started:
         one.wait_send()
-    store = pltpu.make_async_copy(done, out_ref, local.at[1])
-    store.start()
     store.wait()
 
 
 def sum_all(big, small):
     rows, width = big.shape
-    quarter, eighth, last = rows // 4, rows // 8, rows // 32
+    quarter, eighth, last = rows // 8, rows // 16, rows // 64
     anywhere = pl.BlockSpec(memory_space=pl.ANY)
     whole = pl.BlockSpec(memory_space=pltpu.VMEM)
     dma = pltpu.SemaphoreType.DMA
@@ -1184,16 +1197,16 @@
         scratch_shapes=[
             pltpu.VMEM((rows, width), BF),
             pltpu.VMEM((rows, width), BF),
+            pltpu.VMEM((4, quarter, width), BF),
             pltpu.VMEM((2, quarter, width), BF),
             pltpu.VMEM((2, eighth, width), BF),
-            pltpu.VMEM((eighth, width), BF),
-            pltpu.VMEM((4, last, width), BF),
+            pltpu.VMEM((2, 4, last, width), BF),
             pltpu.VMEM((3,) + small.shape, F32),
             pltpu.VMEM((3,) + small.shape, F32),
             pltpu.VMEM((4,) + small.shape, F32),
             dma((2,)),
-            dma((20,)),
-            dma((20,)),
+            dma((38,)),
+            dma((38,)),
             dma((7,)),
             dma((7,)),
         ],
@@ -1215,7 +1228,7 @@
 def join_back(grad, w):
     rows, depth = grad.shape
     width = w.shape[0] // 2
-    block = min(256, rows)
+    block = min(512, rows)
     out = pl.BlockSpec((block, width), lambda i: (i, 0))
     return pl.pallas_call(
         join_back_kernel,
@@ -1258,26 +1271,6 @@
         name="concat_back",
         cost_estimate=cost(4 * rows * width * width, 8 * rows * width),
     )(x, skip, grad)
-
-
-def hold_kernel(x_ref, *refs):
-    refs[-1][...] = x_ref[...]
-
-
-def hold(x, after):
-    rows, width = x.shape
-    block = rows // 9 if rows % 9 == 0 else rows
-    piece = pl.BlockSpec((block, width), lambda i: (i, 0))
-    return pl.pallas_call(
-        hold_kernel,
-        grid=(rows // block,),
-        in_specs=[piece] + [pl.BlockSpec(memory_space=pl.ANY)] * len(after),
-        out_specs=piece,
-        out_shape=jax.ShapeDtypeStruct(x.shape, x.dtype),
-        compiler_params=params(),
-        name="hold",
-        cost_estimate=cost(rows * width, 4 * rows * width),
-    )(x, *after)
 
 
 def unpack_kernel(core_ref, own_ref, sibling_ref, up_ref, down_ref):
@@ -1355,12 +1348,18 @@
     grad_low = grad_rows.astype(BF)
     half_up, half_down = core_half(w_up), core_half(w_down)
     if paired:
-        bias_far, out_far = across(b_up), across(w_out)
+        bias_far, out_piece = across(b_up), across(core_half(w_out))
         h0, n1 = enter(inputs, skip_in, w_concat, b_concat, gain_attn, 0, rows)
-        n1, bias_far, out_far = lax.optimization_barrier((n1, bias_far, out_far))
+        n1, bias_far, out_piece = lax.optimization_barrier((n1, bias_far, out_piece))
         n1_far = across(n1)
+        out_rest = lax.ppermute(out_piece, "core", [(0, 1), (1, 0)])
+        out_far = jnp.where(
+            core == 0,
+            jnp.concatenate([out_piece, out_rest]),
+            jnp.concatenate([out_rest, out_piece]),
+        )
         tables_near = tables(piece(pos_all, rank, rows))
-        q_near, k_near, v_near = project(n1, w_turned, *tables_near)
+        q_near, k_near, v_near = project(n1, w_turned, *tables_near, after=(out_far,))
         start = attend_half(
             "near_near", ends, index, q_near, False, {0: (k_near, v_near)}, last=False
         )
@@ -1472,8 +1471,7 @@
             partial=partial, written=(back_near,), after=grad_far_rows,
         )[0].reshape(3 * each, rows)
         pairs = [(n1, back_near, 0), (n1_far, back_far, 0)]
-        grad_qkv = project_back(pairs, index)
-        grad_up, grad_down, grad_out = unpack_all(hold(summed, (grad_qkv, sent)))
+        grad_qkv, summed = project_back(pairs, summed)
         grad_h0_low, late = leave(
             back_near, w_turned, sent, h0, grad_h1, gain_attn, (grad_qkv,)
         )
@@ -1481,11 +1479,11 @@
         back = attend_back(ends, query, keys, values, grad_mixed, mixed, logsum, cosine, sine)
         grad_n1 = dot_tn(back, w_turned).astype(BF)
         grad_n1 = lax.psum_scatter(grad_n1, "mp", scatter_dimension=0, tiled=True).astype(F32)
-        grad_up, grad_down, grad_out = unpack_all(summed)
-        grad_qkv = project_back([(n1_all, back, 0)], index)
+        grad_qkv, summed = project_back([(n1_all, back, 0)], summed)
         grad_h0, grad_gain_attn = norm_back(grad_n1, h0, scale_one, gain_attn)
         grad_h0_low = (grad_h0 + grad_h1).astype(BF)
         late = jnp.stack([jnp.sum(grad_h0_low.astype(F32), axis=0), grad_gain_attn])
+    grad_up, grad_down, grad_out = unpack_all(summed)
     grad_w_concat = concat_back(inputs, skip_in, grad_h0_low)
     small = jnp.concatenate([early, late, grad_bias.reshape(-1, width)])
     small = jnp.pad(small, ((0, -small.shape[0] % 8), (0, 0)))

time: 1100 us -> 1060 us (0.964)
  Pallas kernels: 947 us -> 914 us
    pallas_call x1, Pallas kernels: 97.7 us -> 76.7 us  [sum_all(): pl.pallas_call(sum_all_kernel, in_specs=[anywhere, whole], out_specs=[any...]
  transfers between devices with their start and end apart: 12 -> 13, of which waited for: 5 -> 4; matrix products, arithmetic and copies ran while one was open for 4% -> 5% of each run, Pallas kernels for 73% -> 73%
where the time goes in v4:
time: 1060 us; the launch traced here: 1050 us
  Pallas kernels  914 us (86%)
  waiting for transfers between devices  59.8 us (6%)
  other arithmetic  25.8 us (2%)
  local copies, waits for them, and re-layouts  17.5 us (2%)
  between operations  14.3 us (1%)
  matrix products  11.1 us (1%)
    pallas_call x7, Pallas kernels, half_back(): pl.pallas_call(functools.partial(half_back_kernel, near_only, partial is...  372 us
    pallas_call x3, Pallas kernels, attend_half(): pl.pallas_call(functools.partial(half_kernel, query_far, sides, carry is...  173 us
    pallas_call x2, Pallas kernels, ffn(): pl.pallas_call(functools.partial(ffn_kernel, step, before is not None), g...  126 us
    pallas_call x1, Pallas kernels, sum_all(): pl.pallas_call(sum_all_kernel, in_specs=[anywhere, whole], out_specs=[any...  76.7 us
    ppermute x6, waiting for transfers between devices, across(): return lax.ppermute(x, 'mp', [(0, 1), (1, 0)])  57.9 us
    pallas_call x1, Pallas kernels, middle(): pl.pallas_call(middle_kernel, grid=(rows // block,), in_specs=[tall(), ta...  23.8 us
    pallas_call x2, Pallas kernels, project(): pl.pallas_call(project_kernel, grid=(count // block,), in_specs=[pl.Block...  22.6 us
  transfers between devices with their start and end apart: 13, of which 4 were waited for; matrix products, arithmetic and copies ran while one was open for 5% of the time, Pallas kernels for 73%

profile of v4, /device:TPU:0, one launch (start us, length us, event | category | flops | bytes accessed | tf_op | source)
XLA Modules:
  0.0 1053.2 jit_solution(13769532057617434209)
XLA Ops:
  11.4 14.8 %enter.1 = (f32[2048,1024]{1,0:T(8,128)}, bf16[2048,1024]{1,0:T(8,128)(2,1)}) custom-call(bf16[2048,1024]{1,0:T(8,128)(2,1)} %x_ref.3, bf16[2048,1024]{1,0:T(8,128)(2,1)} %s_ref.3, bf16[2048,1024]{1,0:T(8,128)(2,1)} %w_ref.3, f32[1,1024]{1,0:T(1,128)} %bitcast.75, f32[1,1024]{1,0:T(1,128)} %bitcast.73), custom_call_target="tpu_custom_call" | custom-call | flops 134217728 | bytes 327680 | tf_op jit(solution)/shard_map/enter/pallas_call | solution.py:156
  45.4 11.3 %project.2 = (bf16[512,2048]{1,0:T(8,128)(2,1)}, bf16[512,2048]{1,0:T(8,128)(2,1)}, bf16[512,2048]{1,0:T(8,128)(2,1)}) custom-call(bf16[2048,1024]{1,0:T(8,128)(2,1)} %get-tuple-element.79.x_ref.refs_0_, bf16[1536,1024]{1,0:T(8,128)(2,1)} %pad_maximum_fusion.w_ref, f32[32,2048]{1,0:T(8,128)} %get-tuple-element.149.cos_ref.refs_6_, ...), custom_call_target="tpu_custom_call" | custom-call | tf_op jit(solution)/shard_map/project/pallas_call | solution.py:92
  56.6 44.5 %near_near.1 = (f32[8,80,2048]{2,1,0:T(8,128)}, f32[8,1,2048]{2,1,0:T(1,128)}) custom-call(s32[8]{0:T(128)} %bitcast.60, s32[1]{0:T(128)} %bitcast.4.part_ref.dst_ref, bf16[512,2048]{1,0:T(8,128)(2,1)} %get-tuple-element.81.refs_0_, bf16[512,2048]{1,0:T(8,128)(2,1)} %get-tuple-element.82.refs_1_, bf16[512,2048]{1,0:T(8,128)(2,1)} %get-tuple-element.83.refs_2_), custom_call_target="tpu_custom_call" | custom-call | flops 536870912 | bytes 131072 | tf_op jit(solution)/shard_map/near_near/pallas_call | solution.py:493
  101.1 17.5 %collective-permute-done.3.x_ref.refs_2_ = bf16[2048,1024]{1,0:T(8,128)(2,1)} collective-permute-done((bf16[2048,1024]{1,0:T(8,128)(2,1)}, bf16[2048,1024]{1,0:T(8,128)(2,1)}, u32[]{:S(2)}, u32[]{:S(2)}) %collective-permute-start.3) | collective-permute-done | bytes 4194336 | tf_op jit(solution)/shard_map/ppermute | solution.py:1330
  119.5 11.3 %project.3 = (bf16[512,2048]{1,0:T(8,128)(2,1)}, bf16[512,2048]{1,0:T(8,128)(2,1)}, bf16[512,2048]{1,0:T(8,128)(2,1)}) custom-call(bf16[2048,1024]{1,0:T(8,128)(2,1)} %collective-permute-done.3.x_ref.refs_2_, bf16[1536,1024]{1,0:T(8,128)(2,1)} %pad_maximum_fusion.w_ref, f32[32,2048]{1,0:T(8,128)} %get-tuple-element.146.cos_ref.refs_14_, ...), custom_call_target="tpu_custom_call" | custom-call | tf_op jit(solution)/shard_map/project/pallas_call | solution.py:92
  130.8 84.1 %far_all.1 = (bf16[512,2048]{1,0:T(8,128)(2,1)}, f32[8,1,2048]{2,1,0:T(1,128)}) custom-call(s32[8]{0:T(128)} %bitcast.61, s32[1]{0:T(128)} %bitcast.4.part_ref.dst_ref, bf16[512,2048]{1,0:T(8,128)(2,1)} %get-tuple-element.92.refs_0_.refs_8_, bf16[512,2048]{1,0:T(8,128)(2,1)} %get-tuple-element.82.refs_1_, bf16[512,2048]{1,0:T(8,128)(2,1)} %get-tuple-element.83.refs_2_, ...), custom_call_target="tpu_custom_call" | custom-call | flops 1073741824 | bytes 131072 | tf_op jit(solution)/shard_map/far_all/pallas_call | solution.py:493
  218.8 4.9 multiply_convert_fusion.g_ref
  224.3 44.5 %near_far.1 = (bf16[512,2048]{1,0:T(8,128)(2,1)}, f32[8,1,2048]{2,1,0:T(1,128)}) custom-call(s32[8]{0:T(128)} %bitcast.62, s32[1]{0:T(128)} %bitcast.4.part_ref.dst_ref, bf16[512,2048]{1,0:T(8,128)(2,1)} %get-tuple-element.81.refs_0_, bf16[512,2048]{1,0:T(8,128)(2,1)} %get-tuple-element.87.refs_1_.refs_3_.refs_9_, ...), custom_call_target="tpu_custom_call" | custom-call | flops 536870912 | bytes 131072 | tf_op jit(solution)/shard_map/near_far/pallas_call | solution.py:493
  268.9 12.7 %collective-permute-done.4.in_ref = bf16[512,2048]{1,0:T(8,128)(2,1)S(1)} collective-permute-done((bf16[512,2048]{1,0:T(8,128)(2,1)}, bf16[512,2048]{1,0:T(8,128)(2,1)S(1)}, u32[]{:S(2)}, u32[]{:S(2)}) %collective-permute-start.4) | collective-permute-done | bytes 2097184 | tf_op jit(solution)/shard_map/ppermute | solution.py:1330
  282.9 12.7 %upper.1 = (f32[2048,1024]{1,0:T(8,128)}, bf16[2048,1024]{1,0:T(8,128)(2,1)}) custom-call(f32[2048,1024]{1,0:T(8,128)} %get-tuple-element.77.h_ref, bf16[512,2048]{1,0:T(8,128)(2,1)} %get-tuple-element.91.near_ref.refs_4_, bf16[512,2048]{1,0:T(8,128)(2,1)} %copy-done.1, bf16[512,1024]{1,0:T(8,128)(2,1)} %own_ref.3, ...), custom_call_target="tpu_custom_call" | custom-call | flops 67108864 | bytes 393216 | tf_op jit(solution)/shard_map/upper/pallas_call | solution.py:182
  295.7 62.9 %ffn_near.1 = (f32[2048,1024]{1,0:T(8,128)}, f32[2048,1024]{1,0:T(8,128)}, bf16[2,2,2304,1024]{3,2,1,0:T(8,128)(2,1)}, f32[1,1,2048]{2,1,0:T(1,128)}) custom-call(s32[1]{0:T(128)} %constant.34.clone.1.src_ref, s32[1]{0:T(128)} %bitcast.4.part_ref.dst_ref, bf16[2048,1024]{1,0:T(8,128)(2,1)} %get-tuple-element.95.n_ref, ...), custom_call_target="tpu_custom_call" | custom-call | flops 805306368 | bytes 262144 | tf_op jit(solution)/shard_map/ffn_near/pallas_call | solution.py:897
  358.7 63.2 %ffn_far.1 = (f32[2048,1024]{1,0:T(8,128)}, f32[2048,1024]{1,0:T(8,128)}, bf16[2,2,2304,1024]{3,2,1,0:T(8,128)(2,1)}, f32[1,1,2048]{2,1,0:T(1,128)}) custom-call(s32[1]{0:T(128)S(6)} %sub.16.src_ref.dst_ref, s32[1]{0:T(128)S(6)} %sub.16.src_ref.dst_ref, bf16[2048,1024]{1,0:T(8,128)(2,1)} %get-tuple-element.95.n_ref, ...), custom_call_target="tpu_custom_call", output_to_operand_aliasing={{2}: (9, {})} | custom-call | flops 805306368 | bytes 262144 | tf_op jit(solution)/shard_map/ffn_far/pallas_call | solution.py:897
  421.9 23.8 %middle.1 = (f32[2048,1024]{1,0:T(8,128)}, f32[2048,1024]{1,0:T(8,128)}, bf16[2048,1024]{1,0:T(8,128)(2,1)}, bf16[512,2048]{1,0:T(8,128)(2,1)}, bf16[512,2048]{1,0:T(8,128)(2,1)}, /*index=5*/f32[3,1024]{1,0:T(4,128)}) custom-call(f32[2048,1024]{1,0:T(8,128)} %get-tuple-element.94.h_ref, f32[2048,1024]{1,0:T(8,128)} %get-tuple-element.102.branch_ref, ...), custom_call_target="tpu_custom_call" | custom-call | flops 67108864 | bytes 786432 | tf_op jit(solution)/shard_map/middle/pallas_call | solution.py:222
  445.7 10.0 out_back.1
  456.1 48.9 %back_near0.1.refs_16_ = f32[3,8,64,2048]{3,2,1,0:T(8,128)} custom-call(s32[8]{0:T(128)} %bitcast.63, s32[1]{0:T(128)} %bitcast.4.part_ref.dst_ref, bf16[512,2048]{1,0:T(8,128)(2,1)} %get-tuple-element.81.refs_0_, bf16[512,2048]{1,0:T(8,128)(2,1)} %get-tuple-element.82.refs_1_, bf16[512,2048]{1,0:T(8,128)(2,1)} %get-tuple-element.83.refs_2_, ...), custom_call_target="tpu_custom_call" | custom-call | flops 671088640 | bytes 327680 | tf_op jit(solution)/shard_map/back_near0/pallas_call | solution.py:783
  504.9 9.7 collective-permute-done.5.refs_11_
  515.9 62.1 %back_first0.1 = (bf16[3,8,64,2048]{3,2,1,0:T(8,128)(2,1)}, bf16[3,8,64,2048]{3,2,1,0:T(8,128)(2,1)}) custom-call(s32[8]{0:T(128)} %bitcast.64, s32[1]{0:T(128)} %bitcast.4.part_ref.dst_ref, bf16[512,2048]{1,0:T(8,128)(2,1)} %get-tuple-element.81.refs_0_, bf16[512,2048]{1,0:T(8,128)(2,1)} %get-tuple-element.82.refs_1_, ...), custom_call_target="tpu_custom_call" | custom-call | flops 1006632960 | bytes 163840 | tf_op jit(solution)/shard_map/back_first0/pallas_call | solution.py:783
  578.1 33.6 %back_first1.1 = (bf16[3,8,64,2048]{3,2,1,0:T(8,128)(2,1)}, bf16[3,8,64,2048]{3,2,1,0:T(8,128)(2,1)}) custom-call(s32[8]{0:T(128)} %bitcast.65, s32[1]{0:T(128)} %bitcast.4.part_ref.dst_ref, bf16[512,2048]{1,0:T(8,128)(2,1)} %get-tuple-element.81.refs_0_, ...), custom_call_target="tpu_custom_call", output_to_operand_aliasing={{0}: (19, {}), {1}: (20, {})} | custom-call | flops 503316480 | bytes 81920 | tf_op jit(solution)/shard_map/back_first1/pallas_call | solution.py:783
  611.6 33.5 %back_first2.1 = (bf16[3,8,64,2048]{3,2,1,0:T(8,128)(2,1)}, bf16[3,8,64,2048]{3,2,1,0:T(8,128)(2,1)}) custom-call(s32[8]{0:T(128)} %bitcast.66, s32[1]{0:T(128)} %bitcast.4.part_ref.dst_ref, bf16[512,2048]{1,0:T(8,128)(2,1)} %get-tuple-element.81.refs_0_, ...), custom_call_target="tpu_custom_call", output_to_operand_aliasing={{0}: (19, {}), {1}: (20, {})} | custom-call | flops 503316480 | bytes 81920 | tf_op jit(solution)/shard_map/back_first2/pallas_call | solution.py:783
  645.7 70.8 %back_second0.1 = (bf16[3,8,64,2048]{3,2,1,0:T(8,128)(2,1)}, f32[3,8,64,2048]{3,2,1,0:T(8,128)}) custom-call(s32[8]{0:T(128)} %bitcast.67, s32[1]{0:T(128)} %bitcast.4.part_ref.dst_ref, bf16[512,2048]{1,0:T(8,128)(2,1)} %get-tuple-element.81.refs_0_, bf16[512,2048]{1,0:T(8,128)(2,1)} %get-tuple-element.82.refs_1_, ...), custom_call_target="tpu_custom_call", output_to_operand_aliasing={{0}: (18, {})} | custom-call | flops 1006632960 | bytes 163840 | tf_op jit(solution)/shard_map/back_second0/pallas_call | solution.py:783
  716.5 74.1 %back_second1.1 = (bf16[3,8,64,2048]{3,2,1,0:T(8,128)(2,1)}, f32[3,8,64,2048]{3,2,1,0:T(8,128)}) custom-call(s32[8]{0:T(128)} %bitcast.68, s32[1]{0:T(128)} %bitcast.4.part_ref.dst_ref, bf16[512,2048]{1,0:T(8,128)(2,1)} %get-tuple-element.81.refs_0_, bf16[512,2048]{1,0:T(8,128)(2,1)} %get-tuple-element.82.refs_1_, ...), custom_call_target="tpu_custom_call", output_to_operand_aliasing={{0}: (18, {}), {1}: (19, {})} | custom-call | flops 1006632960 | bytes 163840 | tf_op jit(solution)/shard_map/back_second1/pallas_call | solution.py:783
  790.7 11.1 %convolution_convert_fusion.refs_10_ = bf16[2048,1024]{1,0:T(8,128)(2,1)} fusion(bf16[1536,2048]{1,0:T(8,128)(2,1)} %bitcast.42, bf16[512,1024]{1,0:T(8,128)(2,1)S(1)} %bitcast.53, bf16[512,1024]{1,0:T(8,128)(2,1)S(1)} %bitcast.55, bf16[512,1024]{1,0:T(8,128)(2,1)S(1)} %bitcast.57), kind=kOutput, calls=%fused_computation.1 | convolution fusion | flops 6453985280 | bytes 13631488 | tf_op jit(solution)/shard_map/dot_general | solution.py:26
  806.7 49.2 %back_near1.1 = bf16[3,8,64,2048]{3,2,1,0:T(8,128)(2,1)} custom-call(s32[8]{0:T(128)} %bitcast.69, s32[1]{0:T(128)} %bitcast.4.part_ref.dst_ref, bf16[512,2048]{1,0:T(8,128)(2,1)} %get-tuple-element.81.refs_0_, bf16[512,2048]{1,0:T(8,128)(2,1)} %get-tuple-element.82.refs_1_, ...), custom_call_target="tpu_custom_call", output_to_operand_aliasing={{}: (11, {})} | custom-call | flops 671088640 | bytes 327680 | tf_op jit(solution)/shard_map/back_near1/pallas_call | solution.py:783
  855.9 19.4 %project_back.1 = (bf16[1536,1024]{1,0:T(8,128)(2,1)}, bf16[2304,1024]{1,0:T(8,128)(2,1)}) custom-call(bf16[2048,1024]{1,0:T(8,128)(2,1)} %get-tuple-element.79.x_ref.refs_0_, bf16[1536,2048]{1,0:T(8,128)(2,1)} %bitcast.44, bf16[2048,1024]{1,0:T(8,128)(2,1)} %collective-permute-done.3.x_ref.refs_2_, ...), custom_call_target="tpu_custom_call", output_to_operand_aliasing={{1}: (4, {})} | custom-call | flops 201326592 | bytes 196608 | tf_op jit(solution)/shard_map/project_back/pallas_call | solution.py:989
  875.3 18.0 %collective-permute-done.6.sent_ref = bf16[2048,1024]{1,0:T(8,128)(2,1)} collective-permute-done((bf16[2048,1024]{1,0:T(8,128)(2,1)}, bf16[2048,1024]{1,0:T(8,128)(2,1)}, u32[]{:S(2)}, u32[]{:S(2)}) %collective-permute-start.6) | collective-permute-done | bytes 4194336 | tf_op jit(solution)/shard_map/ppermute | solution.py:1330
  893.3 17.6 %leave.1 = (bf16[2048,1024]{1,0:T(8,128)(2,1)}, f32[2,1024]{1,0:T(2,128)}) custom-call(bf16[1536,2048]{1,0:T(8,128)(2,1)} %bitcast.45, bf16[1536,1024]{1,0:T(8,128)(2,1)} %pad_maximum_fusion.w_ref, bf16[2048,1024]{1,0:T(8,128)(2,1)} %collective-permute-done.6.sent_ref, f32[2048,1024]{1,0:T(8,128)} %get-tuple-element.77.h_ref, ...), custom_call_target="tpu_custom_call" | custom-call | flops 100663296 | bytes 524288 | tf_op jit(solution)/shard_map/leave/pallas_call | solution.py:255
  913.0 14.0 %concat_back.1.big_ref = bf16[2048,1024]{1,0:T(8,128)(2,1)} custom-call(bf16[2048,1024]{1,0:T(8,128)(2,1)} %x_ref.3, bf16[2048,1024]{1,0:T(8,128)(2,1)} %s_ref.3, bf16[2048,1024]{1,0:T(8,128)(2,1)} %get-tuple-element.123.grad_ref), custom_call_target="tpu_custom_call" | custom-call | flops 134217728 | bytes 262144 | tf_op jit(solution)/shard_map/concat_back/pallas_call | solution.py:1260
  927.0 76.7 %sum_all.1 = (bf16[2048,1024]{1,0:T(8,128)(2,1)}, f32[16,1024]{1,0:T(8,128)}) custom-call(bf16[2048,1024]{1,0:T(8,128)(2,1)} %concat_back.1.big_ref, f32[16,1024]{1,0:T(8,128)} %select_maximum_fusion.small_ref), custom_call_target="tpu_custom_call" | custom-call | flops 32768 | bytes 262144 | tf_op jit(solution)/shard_map/sum_all/pallas_call | solution.py:1189
  1003.7 6.7 convert_element_type.35
  1011.1 13.4 %join_back.1 = (f32[2048,1024]{1,0:T(8,128)}, f32[2048,1024]{1,0:T(8,128)}) custom-call(bf16[2048,1024]{1,0:T(8,128)(2,1)} %get-tuple-element.123.grad_ref, bf16[2048,1024]{1,0:T(8,128)(2,1)} %w_ref.3), custom_call_target="tpu_custom_call" | custom-call | flops 33554432 | bytes 262144 | tf_op jit(solution)/shard_map/join_back/pallas_call | solution.py:1233
  1026.2 6.0 turn.1
  1034.8 11.6 %unpack.1 = (f32[1024,2048]{1,0:T(8,128)}, f32[2048,1024]{1,0:T(8,128)}) custom-call(s32[1]{0:T(128)} %bitcast.28.core_ref, bf16[2304,1024]{1,0:T(8,128)(2,1)} %get-tuple-element.135.own_ref, bf16[2304,1024]{1,0:T(8,128)(2,1)} %collective-permute-done.7.sibling_ref), custom_call_target="tpu_custom_call" | custom-call | flops 32768 | bytes 393216 | tf_op jit(solution)/shard_map/unpack/pallas_call | solution.py:1289
  (93 shorter events, 44.1 us)
Async XLA Ops:
  7.2 351.5 %all-gather.5.cloned.1.call-start = ((), (), s32[]{:S(2)}) async-start(), calls=%async_computation.4 | async-start | bytes 10485760 | tf_op jit(solution)/shard_map/all_gather | solution.py:1344
  8.3 17.9 %collective-permute-start.1 = (bf16[256,1024]{1,0:T(8,128)(2,1)S(1)}, bf16[256,1024]{1,0:T(8,128)(2,1)}, u32[]{:S(2)}, u32[]{:S(2)}) collective-permute-start(bf16[256,1024]{1,0:T(8,128)(2,1)S(1)} %constant_dynamic-slice_fusion.2), channel_id=1, source_target_pairs={{0,1},{1,0},{2,3},{3,2},{4,5},{5,4},{6,7},{7,6},{8,9},{9,8},{10,11... | collective-permute-start | bytes 1572872 | tf_op jit(solution)/shard_map/ppermute | solution.py:1330
  11.3 14.9 %collective-permute-start = (bf16[2048]{0:T(1024)(128)(2,1)}, bf16[2048]{0:T(1024)(128)(2,1)S(1)}, u32[]{:S(2)}, u32[]{:S(2)}) collective-permute-start(bf16[2048]{0:T(1024)(128)(2,1)} %param.31), channel_id=1, source_target_pairs={{0,1},{1,0},{2,3},{3,2},{4,5},{5,4},{6,7},{7,6},{8,9},{9,8},{10,11... | collective-permute-start | bytes 12296 | tf_op jit(solution)/shard_map/ppermute | solution.py:1330
  11.4 16.9 %copy-start.15 = (s32[1,8]{1,0:T(1,128)S(1)}, s32[1,8]{1,0:T(1,128)}, u32[]{:S(2)}) copy-start(s32[1,8]{1,0:T(1,128)} %param.20) | copy-start | bytes 100
  11.4 17.0 %copy-start.6 = (bf16[1024,512]{1,0:T(8,128)(2,1)S(1)}, bf16[1024,512]{1,0:T(8,128)(2,1)}, u32[]{:S(2)}) copy-start(bf16[1024,512]{1,0:T(8,128)(2,1)} %param.26) | copy-start | bytes 3145732
  11.4 17.6 %copy-start.7 = (bf16[1024,512]{1,0:T(8,128)(2,1)S(1)}, bf16[1024,512]{1,0:T(8,128)(2,1)}, u32[]{:S(2)}) copy-start(bf16[1024,512]{1,0:T(8,128)(2,1)} %param.25) | copy-start | bytes 3145732
  26.2 92.4 %collective-permute-start.3 = (bf16[2048,1024]{1,0:T(8,128)(2,1)}, bf16[2048,1024]{1,0:T(8,128)(2,1)}, u32[]{:S(2)}, u32[]{:S(2)}) collective-permute-start(bf16[2048,1024]{1,0:T(8,128)(2,1)} %get-tuple-element.79.x_ref.refs_0_), channel_id=1, source_target_pairs={{0,1},{1,0},{2,3},{3,2},{4,5},{5,4},{6,7},{7,6},{8,9},{9,8},{10,11... | collective-permute-start | bytes 12582920 | tf_op jit(solution)/shard_map/ppermute | solution.py:1330
  28.4 6.5 copy-start.8
  29.5 8.5 copy-start.2
  31.4 6.6 copy-start.4
  39.9 2.9 collective-permute-start.2
  118.7 240.0 %all-gather.7.cloned.1.call-start = ((), (), s32[]{:S(2)}) async-start(), calls=%async_computation.5 | async-start | bytes 10485760 | tf_op jit(solution)/shard_map/all_gather | solution.py:1344
  119.4 492.2 %reduce-scatter.2.cloned.1.call-start = ((), (), s32[]{:S(2)}) async-start(), calls=%async_computation.1 | async-start | bytes 23592960 | tf_op jit(solution)/shard_map/reduce_scatter | solution.py:1438
  130.8 84.2 %copy-start.9 = (s32[8,1]{0,1:T(1,128)S(1)}, s32[8,1]{0,1:T(1,128)}, u32[]{:S(2)}) copy-start(s32[8,1]{0,1:T(1,128)} %copy-done.8) | copy-start | bytes 100
  130.8 84.7 %copy-start.14 = (bf16[2048]{0:T(1024)(128)(2,1)S(1)}, bf16[2048]{0:T(1024)(128)(2,1)}, u32[]{:S(2)}) copy-start(bf16[2048]{0:T(1024)(128)(2,1)} %param.31) | copy-start | bytes 12292
  214.9 66.7 %collective-permute-start.4 = (bf16[512,2048]{1,0:T(8,128)(2,1)}, bf16[512,2048]{1,0:T(8,128)(2,1)S(1)}, u32[]{:S(2)}, u32[]{:S(2)}) collective-permute-start(bf16[512,2048]{1,0:T(8,128)(2,1)} %get-tuple-element.93.refs_12_), channel_id=1, source_target_pairs={{0,1},{1,0},{2,3},{3,2},{4,5},{5,4},{6,7},{7,6},{8,9},{9,8},{10,11... | collective-permute-start | bytes 6291464 | tf_op jit(solution)/shard_map/ppermute | solution.py:1330
  281.6 1.3 copy-start.1
  455.7 58.9 %collective-permute-start.5 = (bf16[512,2048]{1,0:T(8,128)(2,1)}, bf16[512,2048]{1,0:T(8,128)(2,1)S(1)}, u32[]{:S(2)}, u32[]{:S(2)}) collective-permute-start(bf16[512,2048]{1,0:T(8,128)(2,1)} %get-tuple-element.107), channel_id=1, source_target_pairs={{0,1},{1,0},{2,3},{3,2},{4,5},{5,4},{6,7},{7,6},{8,9},{9,8},{10,11... | collective-permute-start | bytes 6291464 | tf_op jit(solution)/shard_map/ppermute | solution.py:1330
  514.6 1.3 copy-start
  645.1 210.8 %all-reduce.4.cloned.1.call-start = ((), (), s32[]{:S(2)}) async-start(), calls=%async_computation.2 | async-start | bytes 9437184 | tf_op jit(solution)/shard_map/psum | solution.py:1441
  716.5 74.2 %copy-start.3 = (bf16[1024,512]{0,1:T(8,128)(2,1)S(1)}, bf16[1024,512]{0,1:T(8,128)(2,1)}, u32[]{:S(2)}) copy-start(bf16[1024,512]{0,1:T(8,128)(2,1)} %copy-done.2) | copy-start | bytes 3145732
  716.5 74.2 %copy-start.5 = (bf16[1024,512]{0,1:T(8,128)(2,1)S(1)}, bf16[1024,512]{0,1:T(8,128)(2,1)}, u32[]{:S(2)}) copy-start(bf16[1024,512]{0,1:T(8,128)(2,1)} %copy-done.4) | copy-start | bytes 3145732
  801.8 91.5 %collective-permute-start.6 = (bf16[2048,1024]{1,0:T(8,128)(2,1)}, bf16[2048,1024]{1,0:T(8,128)(2,1)}, u32[]{:S(2)}, u32[]{:S(2)}) collective-permute-start(bf16[2048,1024]{1,0:T(8,128)(2,1)} %convolution_convert_fusion.refs_10_), channel_id=1, source_target_pairs={{0,1},{1,0},{2,3},{3,2},{4,5},{5,4},{6,7},{7,6},{8,9},{9,8},{10,11... | collective-permute-start | bytes 12582920 | tf_op jit(solution)/shard_map/ppermute | solution.py:1330
  875.3 156.9 %collective-permute-start.7 = (bf16[2304,1024]{1,0:T(8,128)(2,1)}, bf16[2304,1024]{1,0:T(8,128)(2,1)}, u32[]{:S(2)}, u32[]{:S(2)}) collective-permute-start(bf16[2304,1024]{1,0:T(8,128)(2,1)} %get-tuple-element.135.own_ref), channel_id=1, source_target_pairs={{0,2},{2,0},{1,3},{3,1},{4,6},{6,4},{5,7},{7,5},{8,10},{10,8},{9,1... | collective-permute-start | bytes 14155784 | tf_op jit(solution)/shard_map/ppermute | solution.py:1430
  893.3 18.2 %copy-start.12 = (f32[1,1,2048]{2,1,0:T(1,128)S(1)}, f32[1,1,2048]{2,1,0:T(1,128)}, u32[]{:S(2)}) copy-start(f32[1,1,2048]{2,1,0:T(1,128)} %get-tuple-element.128) | copy-start | bytes 24580
  893.3 18.2 %copy-start.13 = (f32[1,1,2048]{2,1,0:T(1,128)S(1)}, f32[1,1,2048]{2,1,0:T(1,128)}, u32[]{:S(2)}) copy-start(f32[1,1,2048]{2,1,0:T(1,128)} %get-tuple-element.129) | copy-start | bytes 24580
  893.3 18.3 %copy-start.11 = (f32[3,1024]{1,0:T(4,128)S(1)}, f32[3,1024]{1,0:T(4,128)}, u32[]{:S(2)}) copy-start(f32[3,1024]{1,0:T(4,128)} %get-tuple-element.126) | copy-start | bytes 36868
  910.9 115.3 %all-reduce.6.cloned.1.call-start = ((), (), s32[]{:S(2)}) async-start(), calls=%async_computation.3 | async-start | bytes 6291456 | tf_op jit(solution)/shard_map/psum | solution.py:1492
  1003.7 6.7 copy-start.10
Sparse Core Ops, SparseCore 0:
  118.8 59.6 all-gather.4
  180.1 77.8 all-gather.6
  455.8 149.6 reduce-scatter.1
  649.7 176.5 all-reduce.3
  915.4 109.8 all-reduce.5

commit v5 on v4

--- a/solution.py
+++ b/solution.py
@@ -194,12 +194,11 @@
 
 
 def middle_kernel(
-    h_ref, branch_ref, dn_ref, g_ref, valid_ref, bias_ref, gain_ref, own_ref, far_ref,
-    out_ref, dh_ref, low_ref, near_ref, sent_ref, sums_ref,
+    h_ref, dn_ref, g_ref, valid_ref, gain_ref, own_ref, far_ref,
+    dh_ref, low_ref, near_ref, sent_ref, sums_ref,
 ):
     valid = valid_ref[...]
     h = h_ref[...]
-    out_ref[...] = valid * (h + branch_ref[...] + bias_ref[...])
     g = g_ref[...].astype(F32) * valid
     back, gain_sum = norm_back_rows(dn_ref[...], h, gain_ref[...])
     dh = g + back
@@ -214,7 +213,7 @@
     )
 
 
-def middle(h1, branch, dn, cotangent, valid, bias, gain, own, far):
+def middle(h1, dn, cotangent, valid, gain, own, far):
     rows, width = h1.shape
     block = min(512, rows)
     tall, whole = row_specs(rows, width, block)
@@ -222,11 +221,9 @@
     return pl.pallas_call(
         middle_kernel,
         grid=(rows // block,),
-        in_specs=[tall(), tall(), tall(), tall(), tall(1), whole(1, width), whole(1, width)]
-        + [whole(*own.shape)] * 2,
-        out_specs=[tall(), tall(), tall(), flat, flat, whole(3, width)],
+        in_specs=[tall(), tall(), tall(), tall(1), whole(1, width)] + [whole(*own.shape)] * 2,
+        out_specs=[tall(), tall(), flat, flat, whole(3, width)],
         out_shape=[
-            jax.ShapeDtypeStruct((rows, width), F32),
             jax.ShapeDtypeStruct((rows, width), F32),
             jax.ShapeDtypeStruct((rows, width), BF),
             jax.ShapeDtypeStruct((own.shape[0], rows), BF),
@@ -236,7 +233,29 @@
         compiler_params=params(),
         name="middle",
         cost_estimate=cost(2 * rows * width * width, 24 * rows * width),
-    )(h1, branch, dn, cotangent, valid, bias[None], gain[None], own, far)
+    )(h1, dn, cotangent, valid, gain[None], own, far)
+
+
+def result_kernel(h_ref, branch_ref, valid_ref, bias_ref, after_ref, out_ref):
+    out_ref[...] = valid_ref[...] * (h_ref[...] + branch_ref[...] + bias_ref[...])
+
+
+def result(h1, branch, valid, bias, after):
+    rows, width = h1.shape
+    block = min(512, rows)
+    tall, whole = row_specs(rows, width, block)
+    return pl.pallas_call(
+        result_kernel,
+        grid=(rows // block,),
+        in_specs=[
+            tall(), tall(), tall(1), whole(1, width), pl.BlockSpec(memory_space=pl.ANY)
+        ],
+        out_specs=tall(),
+        out_shape=jax.ShapeDtypeStruct((rows, width), F32),
+        compiler_params=params(),
+        name="result",
+        cost_estimate=cost(rows * width, 12 * rows * width),
+    )(h1, branch, valid, bias[None], after)
 
 
 def leave_kernel(back_ref, w_ref, sent_ref, h_ref, dh_ref, gain_ref, *refs):
@@ -1359,15 +1378,16 @@
             jnp.concatenate([out_rest, out_piece]),
         )
         tables_near = tables(piece(pos_all, rank, rows))
-        q_near, k_near, v_near = project(n1, w_turned, *tables_near, after=(out_far,))
+        bias_both = jnp.stack([bias_far, bias_far]).reshape(2, 1, hidden)
+        q_near, k_near, v_near = project(
+            n1, w_turned, *tables_near, after=(out_far, grad_low, bias_both, valid_here)
+        )
         start = attend_half(
             "near_near", ends, index, q_near, False, {0: (k_near, v_near)}, last=False
         )
         tables_far = tables(piece(pos_all, 1 - rank, rows))
-        n1_far, start, half_up, half_down = lax.optimization_barrier(
-            (n1_far, start, half_up, half_down)
-        )
-        up_all, down_all = gather(half_up), gather(half_down)
+        n1_far, start, half_up = lax.optimization_barrier((n1_far, start, half_up))
+        up_all = gather(half_up)
         q_far, k_far, v_far = project(n1_far, w_turned, *tables_far)
         mixed_far, log_far = attend_half(
             "far_all", ends, index, q_far, True, {0: (k_near, v_near), 1: (k_far, v_far)}
@@ -1376,20 +1396,23 @@
         mixed_near, log_near = attend_half(
             "near_far", ends, index, q_near, False, {1: (k_far, v_far)}, carry=start
         )
+        mixed_in, mixed_near, half_down = lax.optimization_barrier(
+            (mixed_in, mixed_near, half_down)
+        )
+        down_all = gather(half_down)
         h1, n2 = upper(h0, mixed_near, mixed_in, w_out, out_far, b_out, gain_ffn)
         branch, grad_n2, sums, bias_near = ffn(
             "ffn_near", n2, grad_low, w_up.reshape(2, 1, width // 2, hidden),
             b_up.reshape(1, 1, hidden), w_down.reshape(2, 1, hidden // 2, width),
             extra, parts, zero, index,
         )
-        both = jnp.stack([bias_far, bias_far]).reshape(2, 1, hidden)
         branch, grad_n2, sums, grad_bias = ffn(
-            "ffn_far", n2, grad_low, up_all, both, down_all, extra, parts, other, other,
+            "ffn_far", n2, grad_low, up_all, bias_both, down_all, extra, parts, other, other,
             before=(branch, grad_n2, sums),
         )
         grad_bias = order(bias_near, grad_bias, 0)
-        output, grad_h1, grad_h1_low, grad_near, grad_sent, early = middle(
-            h1, branch, grad_n2, cotangent, valid_here, b_down, gain_ffn, w_out, out_far
+        grad_h1, grad_h1_low, grad_near, grad_sent, early = middle(
+            h1, grad_n2, cotangent, valid_here, gain_ffn, w_out, out_far
         )
         grad_far = across(grad_sent)
         sums = out_back(
@@ -1449,20 +1472,17 @@
         opening = back("back_near0", sides=(near,), first=0, count=middle_head, finish=False)[0]
         written, at = (), 0
         quarter = middle_head // 4
-        for i, count in enumerate((2 * quarter, quarter, middle_head - 3 * quarter)):
+        for i, count in enumerate((middle_head - quarter, quarter)):
             written = back(
                 f"back_first{i}", sides=both, first=at, count=count, finish=True,
-                partial=opening, written=written, after=part if i == 2 else None,
+                partial=opening, written=written, after=part if i else None,
             )
             at += count
         back_far, back_near = written
-        partial = None
-        for i in range(2):
-            back_far, partial = back(
-                f"back_second{i}", sides=both, first=at, count=middle_head // 2, finish=False,
-                written=(back_far, partial),
-            )
-            at += middle_head // 2
+        back_far, partial = back(
+            "back_second", sides=both, first=at, count=heads - at, finish=False,
+            written=(back_far, None),
+        )
         back_far = back_far.reshape(3 * each, rows)
         grad_far_rows = dot_tn(back_far, w_turned).astype(BF)
         sent = across(grad_far_rows)
@@ -1472,8 +1492,9 @@
         )[0].reshape(3 * each, rows)
         pairs = [(n1, back_near, 0), (n1_far, back_far, 0)]
         grad_qkv, summed = project_back(pairs, summed)
+        output = result(h1, branch, valid_here, b_down, grad_qkv)
         grad_h0_low, late = leave(
-            back_near, w_turned, sent, h0, grad_h1, gain_attn, (grad_qkv,)
+            back_near, w_turned, sent, h0, grad_h1, gain_attn, (output,)
         )
     else:
         back = attend_back(ends, query, keys, values, grad_mixed, mixed, logsum, cosine, sine)

time: 1060 us -> 1040 us (0.981)
  waiting for transfers between devices: 59.8 us -> 24.8 us
  starting transfers between devices: 10.5 us -> 23.8 us
    ppermute x6, waiting for transfers between devices: 57.9 us -> 23.6 us  [across(): return lax.ppermute(x, 'mp', [(0, 1), (1, 0)])]
    ppermute x6, starting transfers between devices: 10.4 us -> 23.7 us  [across(): return lax.ppermute(x, 'mp', [(0, 1), (1, 0)])]
    pallas_call x7 -> x5, Pallas kernels: 372 us -> 365 us  [half_back(): pl.pallas_call(functools.partial(half_back_kernel, near_only, partial is...]
  transfers between devices with their start and end apart: 13 -> 13, of which waited for: 4 -> 3; matrix products, arithmetic and copies ran while one was open for 5% -> 5% of each run, Pallas kernels for 73% -> 75%
where the time goes in v5:
time: 1040 us; the launch traced here: 1030 us
  Pallas kernels  917 us (88%)
  other arithmetic  26.1 us (3%)
  waiting for transfers between devices  24.8 us (2%)
  starting transfers between devices  23.8 us (2%)
  local copies, waits for them, and re-layouts  16.2 us (2%)
  between operations  14.3 us (1%)
  matrix products  11.2 us (1%)
    pallas_call x5, Pallas kernels, half_back(): pl.pallas_call(functools.partial(half_back_kernel, near_only, partial is...  365 us
    pallas_call x3, Pallas kernels, attend_half(): pl.pallas_call(functools.partial(half_kernel, query_far, sides, carry is...  173 us
    pallas_call x2, Pallas kernels, ffn(): pl.pallas_call(functools.partial(ffn_kernel, step, before is not None), g...  126 us
    pallas_call x1, Pallas kernels, sum_all(): pl.pallas_call(sum_all_kernel, in_specs=[anywhere, whole], out_specs=[any...  80.5 us
    ppermute x6, starting transfers between devices, across(): return lax.ppermute(x, 'mp', [(0, 1), (1, 0)])  23.7 us
    ppermute x6, waiting for transfers between devices, across(): return lax.ppermute(x, 'mp', [(0, 1), (1, 0)])  23.6 us
    pallas_call x2, Pallas kernels, project(): pl.pallas_call(project_kernel, grid=(count // block,), in_specs=[pl.Block...  22.6 us
  transfers between devices with their start and end apart: 13, of which 3 were waited for; matrix products, arithmetic and copies ran while one was open for 5% of the time, Pallas kernels for 75%

profile of v5, /device:TPU:0, one launch (start us, length us, event | category | flops | bytes accessed | tf_op | source)
XLA Modules:
  0.0 1033.7 jit_solution(8368832915855399745)
XLA Ops:
  11.4 14.8 %enter.1 = (f32[2048,1024]{1,0:T(8,128)}, bf16[2048,1024]{1,0:T(8,128)(2,1)}) custom-call(bf16[2048,1024]{1,0:T(8,128)(2,1)} %x_ref.3, bf16[2048,1024]{1,0:T(8,128)(2,1)} %s_ref.3, bf16[2048,1024]{1,0:T(8,128)(2,1)} %w_ref.3, f32[1,1024]{1,0:T(1,128)} %bitcast.73, f32[1,1024]{1,0:T(1,128)} %bitcast.71), custom_call_target="tpu_custom_call" | custom-call | flops 134217728 | bytes 327680 | tf_op jit(solution)/shard_map/enter/pallas_call | solution.py:156
  35.8 4.9 multiply_convert_fusion.refs_1_.g_ref
  44.0 3.2 constant_dynamic-slice_fusion.1
  50.8 11.3 %project.2 = (bf16[512,2048]{1,0:T(8,128)(2,1)}, bf16[512,2048]{1,0:T(8,128)(2,1)}, bf16[512,2048]{1,0:T(8,128)(2,1)}) custom-call(bf16[2048,1024]{1,0:T(8,128)(2,1)} %get-tuple-element.76.x_ref.refs_0_, bf16[1536,1024]{1,0:T(8,128)(2,1)} %pad_maximum_fusion.w_ref, f32[32,2048]{1,0:T(8,128)} %get-tuple-element.143.cos_ref.refs_6_, ...), custom_call_target="tpu_custom_call" | custom-call | tf_op jit(solution)/shard_map/project/pallas_call | solution.py:92
  62.0 44.5 %near_near.1 = (f32[8,80,2048]{2,1,0:T(8,128)}, f32[8,1,2048]{2,1,0:T(1,128)}) custom-call(s32[8]{0:T(128)} %bitcast.60, s32[1]{0:T(128)} %bitcast.4.part_ref.dst_ref, bf16[512,2048]{1,0:T(8,128)(2,1)} %get-tuple-element.79.refs_0_, bf16[512,2048]{1,0:T(8,128)(2,1)} %get-tuple-element.80.refs_1_, bf16[512,2048]{1,0:T(8,128)(2,1)} %get-tuple-element.81.refs_2_), custom_call_target="tpu_custom_call" | custom-call | flops 536870912 | bytes 131072 | tf_op jit(solution)/shard_map/near_near/pallas_call | solution.py:512
  106.5 12.1 %collective-permute-done.2.x_ref.refs_2_ = bf16[2048,1024]{1,0:T(8,128)(2,1)} collective-permute-done((bf16[2048,1024]{1,0:T(8,128)(2,1)}, bf16[2048,1024]{1,0:T(8,128)(2,1)}, u32[]{:S(2)}, u32[]{:S(2)}) %collective-permute-start.2) | collective-permute-done | bytes 4194336 | tf_op jit(solution)/shard_map/ppermute | solution.py:1349
  118.7 11.4 %project.3 = (bf16[512,2048]{1,0:T(8,128)(2,1)}, bf16[512,2048]{1,0:T(8,128)(2,1)}, bf16[512,2048]{1,0:T(8,128)(2,1)}) custom-call(bf16[2048,1024]{1,0:T(8,128)(2,1)} %collective-permute-done.2.x_ref.refs_2_, bf16[1536,1024]{1,0:T(8,128)(2,1)} %pad_maximum_fusion.w_ref, f32[32,2048]{1,0:T(8,128)} %get-tuple-element.140.cos_ref.refs_14_, ...), custom_call_target="tpu_custom_call" | custom-call | tf_op jit(solution)/shard_map/project/pallas_call | solution.py:92
  130.1 84.0 %far_all.1 = (bf16[512,2048]{1,0:T(8,128)(2,1)}, f32[8,1,2048]{2,1,0:T(1,128)}) custom-call(s32[8]{0:T(128)} %bitcast.61, s32[1]{0:T(128)} %bitcast.4.part_ref.dst_ref, bf16[512,2048]{1,0:T(8,128)(2,1)} %get-tuple-element.85.refs_0_.refs_8_, bf16[512,2048]{1,0:T(8,128)(2,1)} %get-tuple-element.80.refs_1_, bf16[512,2048]{1,0:T(8,128)(2,1)} %get-tuple-element.81.refs_2_, ...), custom_call_target="tpu_custom_call" | custom-call | flops 1073741824 | bytes 131072 | tf_op jit(solution)/shard_map/far_all/pallas_call | solution.py:512
  217.3 44.7 %near_far.1 = (bf16[512,2048]{1,0:T(8,128)(2,1)}, f32[8,1,2048]{2,1,0:T(1,128)}) custom-call(s32[8]{0:T(128)} %bitcast.62, s32[1]{0:T(128)} %bitcast.4.part_ref.dst_ref, bf16[512,2048]{1,0:T(8,128)(2,1)} %get-tuple-element.79.refs_0_, bf16[512,2048]{1,0:T(8,128)(2,1)} %get-tuple-element.86.refs_3_.refs_1_.refs_9_, ...), custom_call_target="tpu_custom_call" | custom-call | flops 536870912 | bytes 131072 | tf_op jit(solution)/shard_map/near_far/pallas_call | solution.py:512
  263.3 13.1 %upper.1 = (f32[2048,1024]{1,0:T(8,128)}, bf16[2048,1024]{1,0:T(8,128)(2,1)}) custom-call(f32[2048,1024]{1,0:T(8,128)} %get-tuple-element.74.h_ref, bf16[512,2048]{1,0:T(8,128)(2,1)} %get-tuple-element.92.near_ref.refs_4_, bf16[512,2048]{1,0:T(8,128)(2,1)} %copy-done.1, bf16[512,1024]{1,0:T(8,128)(2,1)} %own_ref.3, ...), custom_call_target="tpu_custom_call" | custom-call | flops 67108864 | bytes 393216 | tf_op jit(solution)/shard_map/upper/pallas_call | solution.py:182
  276.5 63.0 %ffn_near.1 = (f32[2048,1024]{1,0:T(8,128)}, f32[2048,1024]{1,0:T(8,128)}, bf16[2,2,2304,1024]{3,2,1,0:T(8,128)(2,1)}, f32[1,1,2048]{2,1,0:T(1,128)}) custom-call(s32[1]{0:T(128)} %constant.34.clone.1.src_ref, s32[1]{0:T(128)} %bitcast.4.part_ref.dst_ref, bf16[2048,1024]{1,0:T(8,128)(2,1)} %get-tuple-element.95.n_ref, ...), custom_call_target="tpu_custom_call" | custom-call | flops 805306368 | bytes 262144 | tf_op jit(solution)/shard_map/ffn_near/pallas_call | solution.py:916
  339.5 63.2 %ffn_far.1 = (f32[2048,1024]{1,0:T(8,128)}, f32[2048,1024]{1,0:T(8,128)}, bf16[2,2,2304,1024]{3,2,1,0:T(8,128)(2,1)}, f32[1,1,2048]{2,1,0:T(1,128)}) custom-call(s32[1]{0:T(128)S(6)} %sub.16.src_ref.dst_ref, s32[1]{0:T(128)S(6)} %sub.16.src_ref.dst_ref, bf16[2048,1024]{1,0:T(8,128)(2,1)} %get-tuple-element.95.n_ref, ...), custom_call_target="tpu_custom_call", output_to_operand_aliasing={{2}: (9, {})} | custom-call | flops 805306368 | bytes 262144 | tf_op jit(solution)/shard_map/ffn_far/pallas_call | solution.py:916
  402.7 19.4 %middle.1 = (f32[2048,1024]{1,0:T(8,128)}, bf16[2048,1024]{1,0:T(8,128)(2,1)}, bf16[512,2048]{1,0:T(8,128)(2,1)}, bf16[512,2048]{1,0:T(8,128)(2,1)}, f32[3,1024]{1,0:T(4,128)}) custom-call(f32[2048,1024]{1,0:T(8,128)} %get-tuple-element.94.h_ref, f32[2048,1024]{1,0:T(8,128)} %get-tuple-element.102.dn_ref, bf16[2048,1024]{1,0:T(8,128)(2,1)} %g_ref.1, ...), custom_call_target="tpu_custom_call" | custom-call | flops 67108864 | bytes 786432 | tf_op jit(solution)/shard_map/middle/pallas_call | solution.py:221
  422.1 10.0 out_back.1
  434.3 48.9 %back_near0.1.refs_16_ = f32[3,8,64,2048]{3,2,1,0:T(8,128)} custom-call(s32[8]{0:T(128)} %bitcast.63, s32[1]{0:T(128)} %bitcast.4.part_ref.dst_ref, bf16[512,2048]{1,0:T(8,128)(2,1)} %get-tuple-element.79.refs_0_, bf16[512,2048]{1,0:T(8,128)(2,1)} %get-tuple-element.80.refs_1_, bf16[512,2048]{1,0:T(8,128)(2,1)} %get-tuple-element.81.refs_2_, ...), custom_call_target="tpu_custom_call" | custom-call | flops 671088640 | bytes 327680 | tf_op jit(solution)/shard_map/back_near0/pallas_call | solution.py:802
  483.2 6.7 collective-permute-done.5.refs_11_
  491.2 102.9 %back_first0.1 = (bf16[3,8,64,2048]{3,2,1,0:T(8,128)(2,1)}, bf16[3,8,64,2048]{3,2,1,0:T(8,128)(2,1)}) custom-call(s32[8]{0:T(128)} %bitcast.64, s32[1]{0:T(128)} %bitcast.4.part_ref.dst_ref, bf16[512,2048]{1,0:T(8,128)(2,1)} %get-tuple-element.79.refs_0_, bf16[512,2048]{1,0:T(8,128)(2,1)} %get-tuple-element.80.refs_1_, ...), custom_call_target="tpu_custom_call" | custom-call | flops 1509949440 | bytes 245760 | tf_op jit(solution)/shard_map/back_first0/pallas_call | solution.py:802
  594.1 33.1 %back_first1.1 = (bf16[3,8,64,2048]{3,2,1,0:T(8,128)(2,1)}, bf16[3,8,64,2048]{3,2,1,0:T(8,128)(2,1)}) custom-call(s32[8]{0:T(128)} %bitcast.65, s32[1]{0:T(128)} %bitcast.4.part_ref.dst_ref, bf16[512,2048]{1,0:T(8,128)(2,1)} %get-tuple-element.79.refs_0_, ...), custom_call_target="tpu_custom_call", output_to_operand_aliasing={{0}: (19, {}), {1}: (20, {})} | custom-call | flops 503316480 | bytes 81920 | tf_op jit(solution)/shard_map/back_first1/pallas_call | solution.py:802
  627.8 130.8 %back_second.1 = (bf16[3,8,64,2048]{3,2,1,0:T(8,128)(2,1)}, f32[3,8,64,2048]{3,2,1,0:T(8,128)}) custom-call(s32[8]{0:T(128)} %bitcast.66, s32[1]{0:T(128)} %bitcast.4.part_ref.dst_ref, bf16[512,2048]{1,0:T(8,128)(2,1)} %get-tuple-element.79.refs_0_, bf16[512,2048]{1,0:T(8,128)(2,1)} %get-tuple-element.80.refs_1_, ...), custom_call_target="tpu_custom_call", output_to_operand_aliasing={{0}: (18, {})} | custom-call | flops 2013265920 | bytes 327680 | tf_op jit(solution)/shard_map/back_second/pallas_call | solution.py:802
  758.7 11.2 %convolution_convert_fusion.refs_10_ = bf16[2048,1024]{1,0:T(8,128)(2,1)} fusion(bf16[1536,2048]{1,0:T(8,128)(2,1)} %bitcast.44, bf16[512,1024]{1,0:T(8,128)(2,1)S(1)} %bitcast.53, bf16[512,1024]{1,0:T(8,128)(2,1)S(1)} %bitcast.55, bf16[512,1024]{1,0:T(8,128)(2,1)S(1)} %bitcast.57), kind=kOutput, calls=%fused_computation.1 | convolution fusion | flops 6453985280 | bytes 13631488 | tf_op jit(solution)/shard_map/dot_general | solution.py:26
  769.9 16.4 %collective-permute-start.6 = (bf16[2048,1024]{1,0:T(8,128)(2,1)}, bf16[2048,1024]{1,0:T(8,128)(2,1)}, u32[]{:S(2)}, u32[]{:S(2)}) collective-permute-start(bf16[2048,1024]{1,0:T(8,128)(2,1)} %convolution_convert_fusion.refs_10_), channel_id=1, source_target_pairs={{0,1},{1,0},{2,3},{3,2},{4,5},{5,4},{6,7},{7,6},{8,9},{9,8},{10,11... | collective-permute-start | bytes 12582920 | tf_op jit(solution)/shard_map/ppermute | solution.py:1349
  786.3 49.2 %back_near1.1 = bf16[3,8,64,2048]{3,2,1,0:T(8,128)(2,1)} custom-call(s32[8]{0:T(128)} %bitcast.67, s32[1]{0:T(128)} %bitcast.4.part_ref.dst_ref, bf16[512,2048]{1,0:T(8,128)(2,1)} %get-tuple-element.79.refs_0_, bf16[512,2048]{1,0:T(8,128)(2,1)} %get-tuple-element.80.refs_1_, ...), custom_call_target="tpu_custom_call", output_to_operand_aliasing={{}: (11, {})} | custom-call | flops 671088640 | bytes 327680 | tf_op jit(solution)/shard_map/back_near1/pallas_call | solution.py:802
  835.5 19.2 %project_back.1 = (bf16[1536,1024]{1,0:T(8,128)(2,1)}, bf16[2304,1024]{1,0:T(8,128)(2,1)}) custom-call(bf16[2048,1024]{1,0:T(8,128)(2,1)} %get-tuple-element.76.x_ref.refs_0_, bf16[1536,2048]{1,0:T(8,128)(2,1)} %bitcast.42, bf16[2048,1024]{1,0:T(8,128)(2,1)} %collective-permute-done.2.x_ref.refs_2_, ...), custom_call_target="tpu_custom_call", output_to_operand_aliasing={{1}: (4, {})} | custom-call | flops 201326592 | bytes 196608 | tf_op jit(solution)/shard_map/project_back/pallas_call | solution.py:1008
  854.8 10.4 %result.1.refs_0_ = f32[2048,1024]{1,0:T(8,128)} custom-call(f32[2048,1024]{1,0:T(8,128)} %get-tuple-element.94.h_ref, f32[2048,1024]{1,0:T(8,128)} %get-tuple-element.101.branch_ref, f32[2048,1]{1,0:T(8,128)} %copy.55.refs_3_.valid_ref, f32[1,1024]{1,0:T(1,128)} %bitcast.80, bf16[1536,1024]{1,0:T(8,128)(2,1)} %get-tuple-element.115.after_ref), custom_call_target="tpu_custom_call" | custom-call | flops 32768 | bytes 393216 | tf_op jit(solution)/shard_map/result/pallas_call | solution.py:247
  865.8 4.7 collective-permute-done.6.sent_ref
  870.6 17.8 %leave.1 = (bf16[2048,1024]{1,0:T(8,128)(2,1)}, f32[2,1024]{1,0:T(2,128)}) custom-call(bf16[1536,2048]{1,0:T(8,128)(2,1)} %bitcast.43, bf16[1536,1024]{1,0:T(8,128)(2,1)} %pad_maximum_fusion.w_ref, bf16[2048,1024]{1,0:T(8,128)(2,1)} %collective-permute-done.6.sent_ref, f32[2048,1024]{1,0:T(8,128)} %get-tuple-element.74.h_ref, ...), custom_call_target="tpu_custom_call" | custom-call | flops 100663296 | bytes 524288 | tf_op jit(solution)/shard_map/leave/pallas_call | solution.py:274
  889.7 14.1 %concat_back.1.big_ref = bf16[2048,1024]{1,0:T(8,128)(2,1)} custom-call(bf16[2048,1024]{1,0:T(8,128)(2,1)} %x_ref.3, bf16[2048,1024]{1,0:T(8,128)(2,1)} %s_ref.3, bf16[2048,1024]{1,0:T(8,128)(2,1)} %get-tuple-element.117.grad_ref), custom_call_target="tpu_custom_call" | custom-call | flops 134217728 | bytes 262144 | tf_op jit(solution)/shard_map/concat_back/pallas_call | solution.py:1279
  903.8 80.5 %sum_all.1 = (bf16[2048,1024]{1,0:T(8,128)(2,1)}, f32[16,1024]{1,0:T(8,128)}) custom-call(bf16[2048,1024]{1,0:T(8,128)(2,1)} %concat_back.1.big_ref, f32[16,1024]{1,0:T(8,128)} %select_maximum_fusion.small_ref), custom_call_target="tpu_custom_call" | custom-call | flops 32768 | bytes 262144 | tf_op jit(solution)/shard_map/sum_all/pallas_call | solution.py:1208
  984.3 6.7 convert_element_type.35
  991.6 13.4 %join_back.1 = (f32[2048,1024]{1,0:T(8,128)}, f32[2048,1024]{1,0:T(8,128)}) custom-call(bf16[2048,1024]{1,0:T(8,128)(2,1)} %get-tuple-element.117.grad_ref, bf16[2048,1024]{1,0:T(8,128)(2,1)} %w_ref.3), custom_call_target="tpu_custom_call" | custom-call | flops 33554432 | bytes 262144 | tf_op jit(solution)/shard_map/join_back/pallas_call | solution.py:1252
  1006.8 6.0 turn.1
  1015.4 11.6 %unpack.1 = (f32[1024,2048]{1,0:T(8,128)}, f32[2048,1024]{1,0:T(8,128)}) custom-call(s32[1]{0:T(128)} %bitcast.28.core_ref, bf16[2304,1024]{1,0:T(8,128)(2,1)} %get-tuple-element.129.own_ref, bf16[2304,1024]{1,0:T(8,128)(2,1)} %collective-permute-done.7.sibling_ref), custom_call_target="tpu_custom_call" | custom-call | flops 32768 | bytes 393216 | tf_op jit(solution)/shard_map/unpack/pallas_call | solution.py:1308
  (90 shorter events, 36.3 us)
Async XLA Ops:
  7.2 332.3 %all-gather.5.cloned.1.call-start = ((), (), s32[]{:S(2)}) async-start(), calls=%async_computation.4 | async-start | bytes 10485760 | tf_op jit(solution)/shard_map/all_gather | solution.py:1363
  8.3 17.9 %collective-permute-start.1 = (bf16[256,1024]{1,0:T(8,128)(2,1)S(1)}, bf16[256,1024]{1,0:T(8,128)(2,1)}, u32[]{:S(2)}, u32[]{:S(2)}) collective-permute-start(bf16[256,1024]{1,0:T(8,128)(2,1)S(1)} %constant_dynamic-slice_fusion.2), channel_id=1, source_target_pairs={{0,1},{1,0},{2,3},{3,2},{4,5},{5,4},{6,7},{7,6},{8,9},{9,8},{10,11... | collective-permute-start | bytes 1572872 | tf_op jit(solution)/shard_map/ppermute | solution.py:1349
  11.3 14.9 %collective-permute-start = (bf16[2048]{0:T(1024)(128)(2,1)}, bf16[2048]{0:T(1024)(128)(2,1)S(1)}, u32[]{:S(2)}, u32[]{:S(2)}) collective-permute-start(bf16[2048]{0:T(1024)(128)(2,1)} %param.31), channel_id=1, source_target_pairs={{0,1},{1,0},{2,3},{3,2},{4,5},{5,4},{6,7},{7,6},{8,9},{9,8},{10,11... | collective-permute-start | bytes 12296 | tf_op jit(solution)/shard_map/ppermute | solution.py:1349
  11.4 16.9 %copy-start.14 = (s32[1,8]{1,0:T(1,128)S(1)}, s32[1,8]{1,0:T(1,128)}, u32[]{:S(2)}) copy-start(s32[1,8]{1,0:T(1,128)} %param.20) | copy-start | bytes 100
  11.4 17.0 %copy-start.6 = (bf16[1024,512]{1,0:T(8,128)(2,1)S(1)}, bf16[1024,512]{1,0:T(8,128)(2,1)}, u32[]{:S(2)}) copy-start(bf16[1024,512]{1,0:T(8,128)(2,1)} %param.26) | copy-start | bytes 3145732
  11.4 17.6 %copy-start.7 = (bf16[1024,512]{1,0:T(8,128)(2,1)S(1)}, bf16[1024,512]{1,0:T(8,128)(2,1)}, u32[]{:S(2)}) copy-start(bf16[1024,512]{1,0:T(8,128)(2,1)} %param.25) | copy-start | bytes 3145732
  26.2 92.4 %collective-permute-start.2 = (bf16[2048,1024]{1,0:T(8,128)(2,1)}, bf16[2048,1024]{1,0:T(8,128)(2,1)}, u32[]{:S(2)}, u32[]{:S(2)}) collective-permute-start(bf16[2048,1024]{1,0:T(8,128)(2,1)} %get-tuple-element.76.x_ref.refs_0_), channel_id=1, source_target_pairs={{0,1},{1,0},{2,3},{3,2},{4,5},{5,4},{6,7},{7,6},{8,9},{9,8},{10,11... | collective-permute-start | bytes 12582920 | tf_op jit(solution)/shard_map/ppermute | solution.py:1349
  28.4 12.3 %copy-start.8 = (s32[8,1]{0,1:T(1,128)}, s32[8,1]{0,1:T(1,128)S(1)}, u32[]{:S(2)}) copy-start(s32[8,1]{0,1:T(1,128)S(1)} %reduce-window.4) | copy-start | bytes 100
  29.5 11.2 %copy-start.2 = (bf16[1024,512]{0,1:T(8,128)(2,1)}, bf16[1024,512]{0,1:T(8,128)(2,1)S(1)}, u32[]{:S(2)}) copy-start(bf16[1024,512]{0,1:T(8,128)(2,1)S(1)} %copy.52) | copy-start | bytes 3145732
  31.4 9.3 copy-start.4
  40.7 7.1 collective-permute-start.3
  118.7 220.9 %all-gather.7.cloned.1.call-start = ((), (), s32[]{:S(2)}) async-start(), calls=%async_computation.5 | async-start | bytes 10485760 | tf_op jit(solution)/shard_map/all_gather | solution.py:1363
  214.1 47.8 %collective-permute-start.4 = (bf16[512,2048]{1,0:T(8,128)(2,1)}, bf16[512,2048]{1,0:T(8,128)(2,1)S(1)}, u32[]{:S(2)}, u32[]{:S(2)}) collective-permute-start(bf16[512,2048]{1,0:T(8,128)(2,1)} %get-tuple-element.88.refs_12_), channel_id=1, source_target_pairs={{0,1},{1,0},{2,3},{3,2},{4,5},{5,4},{6,7},{7,6},{8,9},{9,8},{10,11... | collective-permute-start | bytes 6291464 | tf_op jit(solution)/shard_map/ppermute | solution.py:1349
  217.3 44.7 %copy-start.13 = (bf16[2048]{0:T(1024)(128)(2,1)S(1)}, bf16[2048]{0:T(1024)(128)(2,1)}, u32[]{:S(2)}) copy-start(bf16[2048]{0:T(1024)(128)(2,1)} %param.31) | copy-start | bytes 12292
  261.9 1.4 copy-start.1
  261.9 332.2 %reduce-scatter.2.cloned.1.call-start = ((), (), s32[]{:S(2)}) async-start(), calls=%async_computation.1 | async-start | bytes 23592960 | tf_op jit(solution)/shard_map/reduce_scatter | solution.py:1461
  432.1 57.7 %collective-permute-start.5 = (bf16[512,2048]{1,0:T(8,128)(2,1)}, bf16[512,2048]{1,0:T(8,128)(2,1)S(1)}, u32[]{:S(2)}, u32[]{:S(2)}) collective-permute-start(bf16[512,2048]{1,0:T(8,128)(2,1)} %get-tuple-element.105), channel_id=1, source_target_pairs={{0,1},{1,0},{2,3},{3,2},{4,5},{5,4},{6,7},{7,6},{8,9},{9,8},{10,11... | collective-permute-start | bytes 6291464 | tf_op jit(solution)/shard_map/ppermute | solution.py:1349
  489.9 1.3 copy-start
  627.3 208.3 %all-reduce.4.cloned.1.call-start = ((), (), s32[]{:S(2)}) async-start(), calls=%async_computation.2 | async-start | bytes 9437184 | tf_op jit(solution)/shard_map/psum | solution.py:1464
  627.8 130.9 %copy-start.3 = (bf16[1024,512]{0,1:T(8,128)(2,1)S(1)}, bf16[1024,512]{0,1:T(8,128)(2,1)}, u32[]{:S(2)}) copy-start(bf16[1024,512]{0,1:T(8,128)(2,1)} %copy-done.2) | copy-start | bytes 3145732
  627.8 130.9 %copy-start.5 = (bf16[1024,512]{0,1:T(8,128)(2,1)S(1)}, bf16[1024,512]{0,1:T(8,128)(2,1)}, u32[]{:S(2)}) copy-start(bf16[1024,512]{0,1:T(8,128)(2,1)} %copy-done.4) | copy-start | bytes 3145732
  769.9 100.6 %collective-permute-start.6 = (bf16[2048,1024]{1,0:T(8,128)(2,1)}, bf16[2048,1024]{1,0:T(8,128)(2,1)}, u32[]{:S(2)}, u32[]{:S(2)}) collective-permute-start(bf16[2048,1024]{1,0:T(8,128)(2,1)} %convolution_convert_fusion.refs_10_), channel_id=1, source_target_pairs={{0,1},{1,0},{2,3},{3,2},{4,5},{5,4},{6,7},{7,6},{8,9},{9,8},{10,11... | collective-permute-start | bytes 12582920 | tf_op jit(solution)/shard_map/ppermute | solution.py:1349
  854.7 158.0 %collective-permute-start.7 = (bf16[2304,1024]{1,0:T(8,128)(2,1)}, bf16[2304,1024]{1,0:T(8,128)(2,1)}, u32[]{:S(2)}, u32[]{:S(2)}) collective-permute-start(bf16[2304,1024]{1,0:T(8,128)(2,1)} %get-tuple-element.129.own_ref), channel_id=1, source_target_pairs={{0,2},{2,0},{1,3},{3,1},{4,6},{6,4},{5,7},{7,5},{8,10},{10,8},{9,1... | collective-permute-start | bytes 14155784 | tf_op jit(solution)/shard_map/ppermute | solution.py:1453
  854.7 11.0 %copy-start.11 = (f32[1,1,2048]{2,1,0:T(1,128)S(1)}, f32[1,1,2048]{2,1,0:T(1,128)}, u32[]{:S(2)}) copy-start(f32[1,1,2048]{2,1,0:T(1,128)} %get-tuple-element.122) | copy-start | bytes 24580
  854.7 11.0 %copy-start.12 = (f32[1,1,2048]{2,1,0:T(1,128)S(1)}, f32[1,1,2048]{2,1,0:T(1,128)}, u32[]{:S(2)}) copy-start(f32[1,1,2048]{2,1,0:T(1,128)} %get-tuple-element.123) | copy-start | bytes 24580
  865.2 141.6 %all-reduce.6.cloned.1.call-start = ((), (), s32[]{:S(2)}) async-start(), calls=%async_computation.3 | async-start | bytes 6291456 | tf_op jit(solution)/shard_map/psum | solution.py:1513
  870.6 17.8 %copy-start.10 = (f32[3,1024]{1,0:T(4,128)S(1)}, f32[3,1024]{1,0:T(4,128)}, u32[]{:S(2)}) copy-start(f32[3,1024]{1,0:T(4,128)} %get-tuple-element.120) | copy-start | bytes 36868
  984.3 6.7 copy-start.9
Sparse Core Ops, SparseCore 0:
  118.8 59.7 all-gather.4
  262.1 60.4 all-gather.6
  432.3 149.3 reduce-scatter.1
  631.8 178.7 all-reduce.3
  869.7 114.5 all-reduce.5

commit v6 on v5

--- a/solution.py
+++ b/solution.py
@@ -1237,31 +1237,35 @@
     )(big, small)
 
 
-def join_back_kernel(grad_ref, w_ref, first_ref, second_ref):
+def join_back_kernel(grad_ref, w_ref, sum_ref, first_ref, second_ref, wide_ref):
+    wide_ref[...] = sum_ref[...].astype(F32)
     grad = grad_ref[...]
     width = first_ref.shape[1]
     first_ref[...] = dot_nt(grad, w_ref[:width, :])
     second_ref[...] = dot_nt(grad, w_ref[width:, :])
 
 
-def join_back(grad, w):
+def join_back(grad, w, total):
     rows, depth = grad.shape
     width = w.shape[0] // 2
     block = min(512, rows)
     out = pl.BlockSpec((block, width), lambda i: (i, 0))
+    piece = pl.BlockSpec((w.shape[0] * block // rows, depth), lambda i: (i, 0))
     return pl.pallas_call(
         join_back_kernel,
         grid=(rows // block,),
         in_specs=[
             pl.BlockSpec((block, depth), lambda i: (i, 0)),
             pl.BlockSpec(w.shape, lambda i: (0, 0)),
+            piece,
         ],
-        out_specs=[out, out],
-        out_shape=[jax.ShapeDtypeStruct((rows, width), F32)] * 2,
+        out_specs=[out, out, piece],
+        out_shape=[jax.ShapeDtypeStruct((rows, width), F32)] * 2
+        + [jax.ShapeDtypeStruct(w.shape, F32)],
         compiler_params=params(),
         name="join_back",
         cost_estimate=cost(rows * depth * width, 8 * rows * width),
-    )(grad, w)
+    )(grad, w, total)
 
 
 def concat_back_kernel(x_ref, s_ref, grad_ref, out_ref):
@@ -1380,7 +1384,7 @@
         tables_near = tables(piece(pos_all, rank, rows))
         bias_both = jnp.stack([bias_far, bias_far]).reshape(2, 1, hidden)
         q_near, k_near, v_near = project(
-            n1, w_turned, *tables_near, after=(out_far, grad_low, bias_both, valid_here)
+            n1, w_turned, *tables_near, after=(out_far, grad_low, bias_both, valid_here, half_down)
         )
         start = attend_half(
             "near_near", ends, index, q_near, False, {0: (k_near, v_near)}, last=False
@@ -1514,13 +1518,13 @@
     else:
         tail, small = lax.psum((grad_w_concat, small), dp + ("mp",))
         grad_qkv = lax.psum(grad_qkv, dp)
-    grad_inputs, grad_skip = join_back(grad_h0_low, w_concat)
+    grad_inputs, grad_skip, tail = join_back(grad_h0_low, w_concat, tail)
     grad_query, grad_key, grad_value = turn(grad_qkv, 3)
     return (
         output,
         grad_inputs,
         grad_skip,
-        tail.astype(F32),
+        tail,
         small[3],
         small[4],
         grad_query,

time: 1040 us -> 1030 us (level)
  transfers between devices with their start and end apart: 13 -> 13, of which waited for: 3 -> 4; matrix products, arithmetic and copies ran while one was open for 5% -> 4% of each run, Pallas kernels for 75% -> 76%
where the time goes in v6:
time: 1030 us
  Pallas kernels  918 us (89%)
  waiting for transfers between devices  27.9 us (3%)
  starting transfers between devices  21.2 us (2%)
  local copies, waits for them, and re-layouts  17.2 us (2%)
  other arithmetic  17.1 us (2%)
  between operations  14.3 us (1%)
  matrix products  11.1 us (1%)
    pallas_call x5, Pallas kernels, half_back(): pl.pallas_call(functools.partial(half_back_kernel, near_only, partial is...  365 us
    pallas_call x3, Pallas kernels, attend_half(): pl.pallas_call(functools.partial(half_kernel, query_far, sides, carry is...  173 us
    pallas_call x2, Pallas kernels, ffn(): pl.pallas_call(functools.partial(ffn_kernel, step, before is not None), g...  126 us
    pallas_call x1, Pallas kernels, sum_all(): pl.pallas_call(sum_all_kernel, in_specs=[anywhere, whole], out_specs=[any...  80.3 us
    ppermute x6, waiting for transfers between devices, across(): return lax.ppermute(x, 'mp', [(0, 1), (1, 0)])  26.6 us
    pallas_call x2, Pallas kernels, project(): pl.pallas_call(project_kernel, grid=(count // block,), in_specs=[pl.Block...  22.6 us
    ppermute x6, starting transfers between devices, across(): return lax.ppermute(x, 'mp', [(0, 1), (1, 0)])  21.1 us
  transfers between devices with their start and end apart: 13, of which 4 were waited for; matrix products, arithmetic and copies ran while one was open for 4% of the time, Pallas kernels for 76%

profile of v6, /device:TPU:0, one launch (start us, length us, event | category | flops | bytes accessed | tf_op | source)
XLA Modules:
  0.0 1027.3 jit_solution(7883868243309574382)
XLA Ops:
  8.3 3.0 collective-permute-start.1
  11.4 14.8 %enter.1 = (f32[2048,1024]{1,0:T(8,128)}, bf16[2048,1024]{1,0:T(8,128)(2,1)}) custom-call(bf16[2048,1024]{1,0:T(8,128)(2,1)} %x_ref.3, bf16[2048,1024]{1,0:T(8,128)(2,1)} %s_ref.3, bf16[2048,1024]{1,0:T(8,128)(2,1)} %w_ref.3, f32[1,1024]{1,0:T(1,128)} %bitcast.73, f32[1,1024]{1,0:T(1,128)} %bitcast.71), custom_call_target="tpu_custom_call" | custom-call | flops 134217728 | bytes 327680 | tf_op jit(solution)/shard_map/enter/pallas_call | solution.py:156
  35.1 2.8 multiply_sine_fusion
  44.2 3.2 constant_dynamic-slice_fusion
  50.6 11.2 %project.2 = (bf16[512,2048]{1,0:T(8,128)(2,1)}, bf16[512,2048]{1,0:T(8,128)(2,1)}, bf16[512,2048]{1,0:T(8,128)(2,1)}) custom-call(bf16[2048,1024]{1,0:T(8,128)(2,1)} %get-tuple-element.77.x_ref.refs_0_, bf16[1536,1024]{1,0:T(8,128)(2,1)} %pad_maximum_fusion.w_ref, f32[32,2048]{1,0:T(8,128)} %get-tuple-element.145.cos_ref.refs_6_, ...), custom_call_target="tpu_custom_call" | custom-call | tf_op jit(solution)/shard_map/project/pallas_call | solution.py:92
  61.9 44.5 %near_near.1 = (f32[8,80,2048]{2,1,0:T(8,128)}, f32[8,1,2048]{2,1,0:T(1,128)}) custom-call(s32[8]{0:T(128)} %bitcast.60, s32[1]{0:T(128)} %bitcast.4.part_ref.dst_ref, bf16[512,2048]{1,0:T(8,128)(2,1)} %get-tuple-element.80.refs_0_, bf16[512,2048]{1,0:T(8,128)(2,1)} %get-tuple-element.81.refs_1_, bf16[512,2048]{1,0:T(8,128)(2,1)} %get-tuple-element.82.refs_2_), custom_call_target="tpu_custom_call" | custom-call | flops 536870912 | bytes 131072 | tf_op jit(solution)/shard_map/near_near/pallas_call | solution.py:512
  106.4 12.3 %collective-permute-done.2.x_ref.refs_2_ = bf16[2048,1024]{1,0:T(8,128)(2,1)} collective-permute-done((bf16[2048,1024]{1,0:T(8,128)(2,1)}, bf16[2048,1024]{1,0:T(8,128)(2,1)}, u32[]{:S(2)}, u32[]{:S(2)}) %collective-permute-start.2) | collective-permute-done | bytes 4194336 | tf_op jit(solution)/shard_map/ppermute | solution.py:1353
  118.7 11.4 %project.3 = (bf16[512,2048]{1,0:T(8,128)(2,1)}, bf16[512,2048]{1,0:T(8,128)(2,1)}, bf16[512,2048]{1,0:T(8,128)(2,1)}) custom-call(bf16[2048,1024]{1,0:T(8,128)(2,1)} %collective-permute-done.2.x_ref.refs_2_, bf16[1536,1024]{1,0:T(8,128)(2,1)} %pad_maximum_fusion.w_ref, f32[32,2048]{1,0:T(8,128)} %get-tuple-element.142.cos_ref.refs_14_, ...), custom_call_target="tpu_custom_call" | custom-call | tf_op jit(solution)/shard_map/project/pallas_call | solution.py:92
  130.1 83.9 %far_all.1 = (bf16[512,2048]{1,0:T(8,128)(2,1)}, f32[8,1,2048]{2,1,0:T(1,128)}) custom-call(s32[8]{0:T(128)} %bitcast.61, s32[1]{0:T(128)} %bitcast.4.part_ref.dst_ref, bf16[512,2048]{1,0:T(8,128)(2,1)} %get-tuple-element.86.refs_0_.refs_8_, bf16[512,2048]{1,0:T(8,128)(2,1)} %get-tuple-element.81.refs_1_, bf16[512,2048]{1,0:T(8,128)(2,1)} %get-tuple-element.82.refs_2_, ...), custom_call_target="tpu_custom_call" | custom-call | flops 1073741824 | bytes 131072 | tf_op jit(solution)/shard_map/far_all/pallas_call | solution.py:512
  214.2 44.5 %near_far.1 = (bf16[512,2048]{1,0:T(8,128)(2,1)}, f32[8,1,2048]{2,1,0:T(1,128)}) custom-call(s32[8]{0:T(128)} %bitcast.62, s32[1]{0:T(128)} %bitcast.4.part_ref.dst_ref, bf16[512,2048]{1,0:T(8,128)(2,1)} %get-tuple-element.80.refs_0_, bf16[512,2048]{1,0:T(8,128)(2,1)} %get-tuple-element.87.refs_3_.refs_1_.refs_9_, ...), custom_call_target="tpu_custom_call" | custom-call | flops 536870912 | bytes 131072 | tf_op jit(solution)/shard_map/near_far/pallas_call | solution.py:512
  261.9 13.0 %upper.1 = (f32[2048,1024]{1,0:T(8,128)}, bf16[2048,1024]{1,0:T(8,128)(2,1)}) custom-call(f32[2048,1024]{1,0:T(8,128)} %get-tuple-element.75.h_ref, bf16[512,2048]{1,0:T(8,128)(2,1)} %get-tuple-element.93.near_ref.refs_4_, bf16[512,2048]{1,0:T(8,128)(2,1)} %copy-done.3, bf16[512,1024]{1,0:T(8,128)(2,1)} %own_ref.3, ...), custom_call_target="tpu_custom_call" | custom-call | flops 67108864 | bytes 393216 | tf_op jit(solution)/shard_map/upper/pallas_call | solution.py:182
  275.0 63.0 %ffn_near.1 = (f32[2048,1024]{1,0:T(8,128)}, f32[2048,1024]{1,0:T(8,128)}, bf16[2,2,2304,1024]{3,2,1,0:T(8,128)(2,1)}, f32[1,1,2048]{2,1,0:T(1,128)}) custom-call(s32[1]{0:T(128)} %constant.34.clone.1.src_ref, s32[1]{0:T(128)} %bitcast.4.part_ref.dst_ref, bf16[2048,1024]{1,0:T(8,128)(2,1)} %get-tuple-element.96.n_ref, ...), custom_call_target="tpu_custom_call" | custom-call | flops 805306368 | bytes 262144 | tf_op jit(solution)/shard_map/ffn_near/pallas_call | solution.py:916
  338.0 63.2 %ffn_far.1 = (f32[2048,1024]{1,0:T(8,128)}, f32[2048,1024]{1,0:T(8,128)}, bf16[2,2,2304,1024]{3,2,1,0:T(8,128)(2,1)}, f32[1,1,2048]{2,1,0:T(1,128)}) custom-call(s32[1]{0:T(128)S(6)} %sub.16.src_ref.dst_ref, s32[1]{0:T(128)S(6)} %sub.16.src_ref.dst_ref, bf16[2048,1024]{1,0:T(8,128)(2,1)} %get-tuple-element.96.n_ref, ...), custom_call_target="tpu_custom_call", output_to_operand_aliasing={{2}: (9, {})} | custom-call | flops 805306368 | bytes 262144 | tf_op jit(solution)/shard_map/ffn_far/pallas_call | solution.py:916
  401.2 19.4 %middle.1 = (f32[2048,1024]{1,0:T(8,128)}, bf16[2048,1024]{1,0:T(8,128)(2,1)}, bf16[512,2048]{1,0:T(8,128)(2,1)}, bf16[512,2048]{1,0:T(8,128)(2,1)}, f32[3,1024]{1,0:T(4,128)}) custom-call(f32[2048,1024]{1,0:T(8,128)} %get-tuple-element.95.h_ref, f32[2048,1024]{1,0:T(8,128)} %get-tuple-element.103.dn_ref, bf16[2048,1024]{1,0:T(8,128)(2,1)} %g_ref.1, ...), custom_call_target="tpu_custom_call" | custom-call | flops 67108864 | bytes 786432 | tf_op jit(solution)/shard_map/middle/pallas_call | solution.py:221
  420.6 10.0 out_back.1
  431.1 48.9 %back_near0.1.refs_16_ = f32[3,8,64,2048]{3,2,1,0:T(8,128)} custom-call(s32[8]{0:T(128)} %bitcast.63, s32[1]{0:T(128)} %bitcast.4.part_ref.dst_ref, bf16[512,2048]{1,0:T(8,128)(2,1)} %get-tuple-element.80.refs_0_, bf16[512,2048]{1,0:T(8,128)(2,1)} %get-tuple-element.81.refs_1_, bf16[512,2048]{1,0:T(8,128)(2,1)} %get-tuple-element.82.refs_2_, ...), custom_call_target="tpu_custom_call" | custom-call | flops 671088640 | bytes 327680 | tf_op jit(solution)/shard_map/back_near0/pallas_call | solution.py:802
  480.0 7.8 collective-permute-done.5.refs_11_
  489.1 102.8 %back_first0.1 = (bf16[3,8,64,2048]{3,2,1,0:T(8,128)(2,1)}, bf16[3,8,64,2048]{3,2,1,0:T(8,128)(2,1)}) custom-call(s32[8]{0:T(128)} %bitcast.64, s32[1]{0:T(128)} %bitcast.4.part_ref.dst_ref, bf16[512,2048]{1,0:T(8,128)(2,1)} %get-tuple-element.80.refs_0_, bf16[512,2048]{1,0:T(8,128)(2,1)} %get-tuple-element.81.refs_1_, ...), custom_call_target="tpu_custom_call" | custom-call | flops 1509949440 | bytes 245760 | tf_op jit(solution)/shard_map/back_first0/pallas_call | solution.py:802
  591.9 33.1 %back_first1.1 = (bf16[3,8,64,2048]{3,2,1,0:T(8,128)(2,1)}, bf16[3,8,64,2048]{3,2,1,0:T(8,128)(2,1)}) custom-call(s32[8]{0:T(128)} %bitcast.65, s32[1]{0:T(128)} %bitcast.4.part_ref.dst_ref, bf16[512,2048]{1,0:T(8,128)(2,1)} %get-tuple-element.80.refs_0_, ...), custom_call_target="tpu_custom_call", output_to_operand_aliasing={{0}: (19, {}), {1}: (20, {})} | custom-call | flops 503316480 | bytes 81920 | tf_op jit(solution)/shard_map/back_first1/pallas_call | solution.py:802
  625.6 130.8 %back_second.1 = (bf16[3,8,64,2048]{3,2,1,0:T(8,128)(2,1)}, f32[3,8,64,2048]{3,2,1,0:T(8,128)}) custom-call(s32[8]{0:T(128)} %bitcast.66, s32[1]{0:T(128)} %bitcast.4.part_ref.dst_ref, bf16[512,2048]{1,0:T(8,128)(2,1)} %get-tuple-element.80.refs_0_, bf16[512,2048]{1,0:T(8,128)(2,1)} %get-tuple-element.81.refs_1_, ...), custom_call_target="tpu_custom_call", output_to_operand_aliasing={{0}: (18, {})} | custom-call | flops 2013265920 | bytes 327680 | tf_op jit(solution)/shard_map/back_second/pallas_call | solution.py:802
  756.4 11.1 %convolution_convert_fusion.refs_10_ = bf16[2048,1024]{1,0:T(8,128)(2,1)} fusion(bf16[1536,2048]{1,0:T(8,128)(2,1)} %bitcast.44, bf16[512,1024]{1,0:T(8,128)(2,1)S(1)} %bitcast.53, bf16[512,1024]{1,0:T(8,128)(2,1)S(1)} %bitcast.55, bf16[512,1024]{1,0:T(8,128)(2,1)S(1)} %bitcast.57), kind=kOutput, calls=%fused_computation.1 | convolution fusion | flops 6453985280 | bytes 13631488 | tf_op jit(solution)/shard_map/dot_general | solution.py:26
  767.6 15.5 %collective-permute-start.6 = (bf16[2048,1024]{1,0:T(8,128)(2,1)}, bf16[2048,1024]{1,0:T(8,128)(2,1)}, u32[]{:S(2)}, u32[]{:S(2)}) collective-permute-start(bf16[2048,1024]{1,0:T(8,128)(2,1)} %convolution_convert_fusion.refs_10_), channel_id=1, source_target_pairs={{0,1},{1,0},{2,3},{3,2},{4,5},{5,4},{6,7},{7,6},{8,9},{9,8},{10,11... | collective-permute-start | bytes 12582920 | tf_op jit(solution)/shard_map/ppermute | solution.py:1353
  783.0 49.2 %back_near1.1 = bf16[3,8,64,2048]{3,2,1,0:T(8,128)(2,1)} custom-call(s32[8]{0:T(128)} %bitcast.67, s32[1]{0:T(128)} %bitcast.4.part_ref.dst_ref, bf16[512,2048]{1,0:T(8,128)(2,1)} %get-tuple-element.80.refs_0_, bf16[512,2048]{1,0:T(8,128)(2,1)} %get-tuple-element.81.refs_1_, ...), custom_call_target="tpu_custom_call", output_to_operand_aliasing={{}: (11, {})} | custom-call | flops 671088640 | bytes 327680 | tf_op jit(solution)/shard_map/back_near1/pallas_call | solution.py:802
  832.3 19.2 %project_back.1 = (bf16[1536,1024]{1,0:T(8,128)(2,1)}, bf16[2304,1024]{1,0:T(8,128)(2,1)}) custom-call(bf16[2048,1024]{1,0:T(8,128)(2,1)} %get-tuple-element.77.x_ref.refs_0_, bf16[1536,2048]{1,0:T(8,128)(2,1)} %bitcast.42, bf16[2048,1024]{1,0:T(8,128)(2,1)} %collective-permute-done.2.x_ref.refs_2_, ...), custom_call_target="tpu_custom_call", output_to_operand_aliasing={{1}: (4, {})} | custom-call | flops 201326592 | bytes 196608 | tf_op jit(solution)/shard_map/project_back/pallas_call | solution.py:1008
  851.5 10.4 %result.1.refs_0_ = f32[2048,1024]{1,0:T(8,128)} custom-call(f32[2048,1024]{1,0:T(8,128)} %get-tuple-element.95.h_ref, f32[2048,1024]{1,0:T(8,128)} %get-tuple-element.102.branch_ref, f32[2048,1]{1,0:T(8,128)} %copy.55.refs_3_.valid_ref, f32[1,1024]{1,0:T(1,128)} %bitcast.80, bf16[1536,1024]{1,0:T(8,128)(2,1)} %get-tuple-element.116.after_ref), custom_call_target="tpu_custom_call" | custom-call | flops 32768 | bytes 393216 | tf_op jit(solution)/shard_map/result/pallas_call | solution.py:247
  862.5 4.7 collective-permute-done.6.sent_ref
  867.3 17.8 %leave.1 = (bf16[2048,1024]{1,0:T(8,128)(2,1)}, f32[2,1024]{1,0:T(2,128)}) custom-call(bf16[1536,2048]{1,0:T(8,128)(2,1)} %bitcast.43, bf16[1536,1024]{1,0:T(8,128)(2,1)} %pad_maximum_fusion.w_ref, bf16[2048,1024]{1,0:T(8,128)(2,1)} %collective-permute-done.6.sent_ref, f32[2048,1024]{1,0:T(8,128)} %get-tuple-element.75.h_ref, ...), custom_call_target="tpu_custom_call" | custom-call | flops 100663296 | bytes 524288 | tf_op jit(solution)/shard_map/leave/pallas_call | solution.py:274
  886.4 14.1 %concat_back.1.big_ref = bf16[2048,1024]{1,0:T(8,128)(2,1)} custom-call(bf16[2048,1024]{1,0:T(8,128)(2,1)} %x_ref.3, bf16[2048,1024]{1,0:T(8,128)(2,1)} %s_ref.3, bf16[2048,1024]{1,0:T(8,128)(2,1)} %get-tuple-element.118.grad_ref), custom_call_target="tpu_custom_call" | custom-call | flops 134217728 | bytes 262144 | tf_op jit(solution)/shard_map/concat_back/pallas_call | solution.py:1283
  900.5 80.3 %sum_all.1 = (bf16[2048,1024]{1,0:T(8,128)(2,1)}, f32[16,1024]{1,0:T(8,128)}) custom-call(bf16[2048,1024]{1,0:T(8,128)(2,1)} %concat_back.1.big_ref, f32[16,1024]{1,0:T(8,128)} %select_maximum_fusion.small_ref), custom_call_target="tpu_custom_call" | custom-call | flops 32768 | bytes 262144 | tf_op jit(solution)/shard_map/sum_all/pallas_call | solution.py:1208
  982.3 15.3 %join_back.1 = (f32[2048,1024]{1,0:T(8,128)}, f32[2048,1024]{1,0:T(8,128)}, f32[2048,1024]{1,0:T(8,128)}) custom-call(bf16[2048,1024]{1,0:T(8,128)(2,1)} %get-tuple-element.118.grad_ref, bf16[2048,1024]{1,0:T(8,128)(2,1)} %w_ref.3, bf16[2048,1024]{1,0:T(8,128)(2,1)} %get-tuple-element.123.sum_ref), custom_call_target="tpu_custom_call" | custom-call | flops 33554432 | bytes 262144 | tf_op jit(solution)/shard_map/join_back/pallas_call | solution.py:1254
  1000.4 6.0 turn.1
  1009.0 11.6 %unpack.1 = (f32[1024,2048]{1,0:T(8,128)}, f32[2048,1024]{1,0:T(8,128)}) custom-call(s32[1]{0:T(128)} %bitcast.28.core_ref, bf16[2304,1024]{1,0:T(8,128)(2,1)} %get-tuple-element.131.own_ref, bf16[2304,1024]{1,0:T(8,128)(2,1)} %collective-permute-done.7.sibling_ref), custom_call_target="tpu_custom_call" | custom-call | flops 32768 | bytes 393216 | tf_op jit(solution)/shard_map/unpack/pallas_call | solution.py:1312
  (91 shorter events, 34.3 us)
Async XLA Ops:
  7.2 330.8 %all-gather.5.cloned.1.call-start = ((), (), s32[]{:S(2)}) async-start(), calls=%async_computation.4 | async-start | bytes 10485760 | tf_op jit(solution)/shard_map/all_gather | solution.py:1367
  8.3 17.9 %collective-permute-start.1 = (bf16[256,1024]{1,0:T(8,128)(2,1)S(1)}, bf16[256,1024]{1,0:T(8,128)(2,1)}, u32[]{:S(2)}, u32[]{:S(2)}) collective-permute-start(bf16[256,1024]{1,0:T(8,128)(2,1)S(1)} %constant_dynamic-slice_fusion.2), channel_id=1, source_target_pairs={{0,1},{1,0},{2,3},{3,2},{4,5},{5,4},{6,7},{7,6},{8,9},{9,8},{10,11... | collective-permute-start | bytes 1572872 | tf_op jit(solution)/shard_map/ppermute | solution.py:1353
  11.3 14.9 %collective-permute-start = (bf16[2048]{0:T(1024)(128)(2,1)}, bf16[2048]{0:T(1024)(128)(2,1)S(1)}, u32[]{:S(2)}, u32[]{:S(2)}) collective-permute-start(bf16[2048]{0:T(1024)(128)(2,1)} %param.31), channel_id=1, source_target_pairs={{0,1},{1,0},{2,3},{3,2},{4,5},{5,4},{6,7},{7,6},{8,9},{9,8},{10,11... | collective-permute-start | bytes 12296 | tf_op jit(solution)/shard_map/ppermute | solution.py:1353
  11.4 16.8 %copy-start.15 = (s32[1,8]{1,0:T(1,128)S(1)}, s32[1,8]{1,0:T(1,128)}, u32[]{:S(2)}) copy-start(s32[1,8]{1,0:T(1,128)} %param.20) | copy-start | bytes 100
  11.4 17.0 %copy-start.8 = (bf16[1024,512]{1,0:T(8,128)(2,1)S(1)}, bf16[1024,512]{1,0:T(8,128)(2,1)}, u32[]{:S(2)}) copy-start(bf16[1024,512]{1,0:T(8,128)(2,1)} %param.26) | copy-start | bytes 3145732
  11.4 17.6 %copy-start.9 = (bf16[1024,512]{1,0:T(8,128)(2,1)S(1)}, bf16[1024,512]{1,0:T(8,128)(2,1)}, u32[]{:S(2)}) copy-start(bf16[1024,512]{1,0:T(8,128)(2,1)} %param.25) | copy-start | bytes 3145732
  26.2 92.4 %collective-permute-start.2 = (bf16[2048,1024]{1,0:T(8,128)(2,1)}, bf16[2048,1024]{1,0:T(8,128)(2,1)}, u32[]{:S(2)}, u32[]{:S(2)}) collective-permute-start(bf16[2048,1024]{1,0:T(8,128)(2,1)} %get-tuple-element.77.x_ref.refs_0_), channel_id=1, source_target_pairs={{0,1},{1,0},{2,3},{3,2},{4,5},{5,4},{6,7},{7,6},{8,9},{9,8},{10,11... | collective-permute-start | bytes 12582920 | tf_op jit(solution)/shard_map/ppermute | solution.py:1353
  28.4 6.7 copy-start.10
  29.5 5.6 copy-start.4
  31.4 9.2 copy-start.6
  32.1 5.8 copy-start.1
  37.9 3.4 copy-start.2
  40.6 7.4 collective-permute-start.3
  118.7 219.3 %all-gather.7.cloned.1.call-start = ((), (), s32[]{:S(2)}) async-start(), calls=%async_computation.5 | async-start | bytes 10485760 | tf_op jit(solution)/shard_map/all_gather | solution.py:1367
  214.1 46.6 %copy-start.14 = (bf16[2048]{0:T(1024)(128)(2,1)S(1)}, bf16[2048]{0:T(1024)(128)(2,1)}, u32[]{:S(2)}) copy-start(bf16[2048]{0:T(1024)(128)(2,1)} %param.31) | copy-start | bytes 12292
  214.1 46.5 %collective-permute-start.4 = (bf16[512,2048]{1,0:T(8,128)(2,1)}, bf16[512,2048]{1,0:T(8,128)(2,1)S(1)}, u32[]{:S(2)}, u32[]{:S(2)}) collective-permute-start(bf16[512,2048]{1,0:T(8,128)(2,1)} %get-tuple-element.89.refs_12_), channel_id=1, source_target_pairs={{0,1},{1,0},{2,3},{3,2},{4,5},{5,4},{6,7},{7,6},{8,9},{9,8},{10,11... | collective-permute-start | bytes 6291464 | tf_op jit(solution)/shard_map/ppermute | solution.py:1353
  260.6 1.4 copy-start.3
  260.6 331.3 %reduce-scatter.2.cloned.1.call-start = ((), (), s32[]{:S(2)}) async-start(), calls=%async_computation.1 | async-start | bytes 23592960 | tf_op jit(solution)/shard_map/reduce_scatter | solution.py:1465
  430.6 57.1 %collective-permute-start.5 = (bf16[512,2048]{1,0:T(8,128)(2,1)}, bf16[512,2048]{1,0:T(8,128)(2,1)S(1)}, u32[]{:S(2)}, u32[]{:S(2)}) collective-permute-start(bf16[512,2048]{1,0:T(8,128)(2,1)} %get-tuple-element.106), channel_id=1, source_target_pairs={{0,1},{1,0},{2,3},{3,2},{4,5},{5,4},{6,7},{7,6},{8,9},{9,8},{10,11... | collective-permute-start | bytes 6291464 | tf_op jit(solution)/shard_map/ppermute | solution.py:1353
  487.7 1.3 copy-start
  625.0 207.3 %all-reduce.4.cloned.1.call-start = ((), (), s32[]{:S(2)}) async-start(), calls=%async_computation.2 | async-start | bytes 9437184 | tf_op jit(solution)/shard_map/psum | solution.py:1468
  625.5 130.8 %copy-start.5 = (bf16[1024,512]{0,1:T(8,128)(2,1)S(1)}, bf16[1024,512]{0,1:T(8,128)(2,1)}, u32[]{:S(2)}) copy-start(bf16[1024,512]{0,1:T(8,128)(2,1)} %copy-done.4) | copy-start | bytes 3145732
  625.5 130.8 %copy-start.7 = (bf16[1024,512]{0,1:T(8,128)(2,1)S(1)}, bf16[1024,512]{0,1:T(8,128)(2,1)}, u32[]{:S(2)}) copy-start(bf16[1024,512]{0,1:T(8,128)(2,1)} %copy-done.6) | copy-start | bytes 3145732
  767.6 99.7 %collective-permute-start.6 = (bf16[2048,1024]{1,0:T(8,128)(2,1)}, bf16[2048,1024]{1,0:T(8,128)(2,1)}, u32[]{:S(2)}, u32[]{:S(2)}) collective-permute-start(bf16[2048,1024]{1,0:T(8,128)(2,1)} %convolution_convert_fusion.refs_10_), channel_id=1, source_target_pairs={{0,1},{1,0},{2,3},{3,2},{4,5},{5,4},{6,7},{7,6},{8,9},{9,8},{10,11... | collective-permute-start | bytes 12582920 | tf_op jit(solution)/shard_map/ppermute | solution.py:1353
  851.4 154.9 %collective-permute-start.7 = (bf16[2304,1024]{1,0:T(8,128)(2,1)}, bf16[2304,1024]{1,0:T(8,128)(2,1)}, u32[]{:S(2)}, u32[]{:S(2)}) collective-permute-start(bf16[2304,1024]{1,0:T(8,128)(2,1)} %get-tuple-element.131.own_ref), channel_id=1, source_target_pairs={{0,2},{2,0},{1,3},{3,1},{4,6},{6,4},{5,7},{7,5},{8,10},{10,8},{9,1... | collective-permute-start | bytes 14155784 | tf_op jit(solution)/shard_map/ppermute | solution.py:1457
  851.4 11.0 %copy-start.12 = (f32[1,1,2048]{2,1,0:T(1,128)S(1)}, f32[1,1,2048]{2,1,0:T(1,128)}, u32[]{:S(2)}) copy-start(f32[1,1,2048]{2,1,0:T(1,128)} %get-tuple-element.121) | copy-start | bytes 24580
  851.5 11.0 %copy-start.13 = (f32[1,1,2048]{2,1,0:T(1,128)S(1)}, f32[1,1,2048]{2,1,0:T(1,128)}, u32[]{:S(2)}) copy-start(f32[1,1,2048]{2,1,0:T(1,128)} %get-tuple-element.122) | copy-start | bytes 24580
  861.9 138.5 %all-reduce.6.cloned.1.call-start = ((), (), s32[]{:S(2)}) async-start(), calls=%async_computation.3 | async-start | bytes 6291456 | tf_op jit(solution)/shard_map/psum | solution.py:1517
  867.3 17.8 %copy-start.11 = (f32[3,1024]{1,0:T(4,128)S(1)}, f32[3,1024]{1,0:T(4,128)}, u32[]{:S(2)}) copy-start(f32[3,1024]{1,0:T(4,128)} %get-tuple-element.119) | copy-start | bytes 36868
Sparse Core Ops, SparseCore 0:
  118.8 59.7 all-gather.4
  260.7 58.5 all-gather.6
  430.8 148.1 reduce-scatter.1
  629.5 177.6 all-reduce.3
  866.4 114.5 all-reduce.5
